TPU v7x, 32 devices: a whole 2x2x4 slice. The times are simulated.
32 devices in a mesh: groups: 2 (over x), views: 16 (over z, y, core).
Axes of the slice: x: 2, y: 2, z: 4, core: 2. Of those that a mesh axis runs over, the one named last changes fastest.
Arguments:
- tokens: bfloat16 [32, 128, 1024], P(('groups', 'views')), parts along dimension 0, may hold values from -6 to 6
- in_gain: float32 [1024], replicated, may hold values from 0.7 to 6, as said below
- w_query: bfloat16 [1024, 1024], replicated, may hold values from -0.1875 to 0.1875
- w_key: bfloat16 [1024, 1024], replicated, may hold values from -0.1875 to 0.1875
- w_value: bfloat16 [1024, 1024], replicated, may hold values from -0.1875 to 0.1875
- w_out: bfloat16 [1024, 1024], replicated, may hold values from -0.1875 to 0.1875
- out_gain: float32 [1024], replicated, may hold values from 0.1 to 1.9
- covis_list: int32 [32, 12], P(('groups', 'views')), parts along dimension 0, may hold values from 0 to 15, as said below
- covis_count: int32 [32], P(('groups', 'views')), parts along dimension 0, may hold values from 2 to 12
Outputs:
- mixed: bfloat16 [32, 128, 1024], P(('groups', 'views')), parts along dimension 0
There are 2 independent parts, one for each index of `groups`. A program takes and returns all parts, laid end to end along the dimension named above; an argument that names none is the same for every part. Nothing has to cross between parts.
Inputs may be any that keep to these rules, and one draw needn't show every extreme that they name: `covis_list`: row v lists 12 distinct view ids w, each with w - v modulo 16 among -6 to -1 and 1 to 6; only the first covis_count[v] entries are covisible views, the others are not used. `in_gain`: positive gains.
All inputs are finite; a program needn't handle non-finite values.
Results may differ from a plain program's by a relative error of at most 0.0085.
The roundings to bfloat16 on the way count: a program that leaves them out, or rounds other values in their place, can miss the bound.
Values may be sent and summed in bfloat16 or wider, within the bound.
No kernel may reach another device: no remote copies, remote signals or barrier semaphores. Data moves between devices by JAX's collectives and lax.ppermute only.
A program may use at most 128 MiB of HBM per device.

v0:
```python
import jax
import jax.numpy as jnp
from jax import lax
from jax.sharding import PartitionSpec as P

HEADS = 16
HEAD_DIM = 64
REACH = 6


def from_behind(block, axis, distance):
    devices = range(lax.axis_size(axis))
    route = [((i - distance) % len(devices), i) for i in devices]
    return lax.ppermute(block, axis, route)


def rms_scale(values, gain):
    mean_sq = jnp.mean(values * values, axis=-1, keepdims=True)
    return values * lax.rsqrt(mean_sq + 1e-06) * gain


def attend_block(query3, key_flat, value_flat):
    tok_rows = query3.shape[0]
    key3 = key_flat.reshape(-1, HEADS, HEAD_DIM)
    value3 = value_flat.reshape(-1, HEADS, HEAD_DIM)
    scores = jnp.einsum(
        "qhd,khd->qhk", query3, key3, preferred_element_type=jnp.float32
    ) * HEAD_DIM ** (-0.5)
    peak = jnp.max(scores, axis=-1)
    weights = jnp.exp(scores - peak[..., None])
    total = jnp.sum(weights, axis=-1)
    numer = jnp.einsum(
        "qhk,khd->qhd", weights.astype(jnp.bfloat16), value3, preferred_element_type=jnp.float32
    )
    return (numer.reshape(tok_rows, HEADS * HEAD_DIM), peak, total)


def combine(state, piece, flag):
    numer, peak, total = state
    other_numer, other_peak, other_total = piece
    other_peak = jnp.where(flag, other_peak, -jnp.inf)
    newest = jnp.maximum(peak, other_peak)
    keep_old = jnp.exp(peak - newest)
    keep_new = jnp.where(flag, jnp.exp(other_peak - newest), 0.0)
    tok_rows = numer.shape[0]
    numer = (
        numer.reshape(tok_rows, HEADS, HEAD_DIM) * keep_old[..., None]
        + other_numer.reshape(tok_rows, HEADS, HEAD_DIM) * keep_new[..., None]
    ).reshape(tok_rows, HEADS * HEAD_DIM)
    total = total * keep_old + other_total * keep_new
    return (numer, newest, total)


def on_device(tokens, in_gain, w_query, w_key, w_value, w_out, out_gain, covis_list, covis_count):
    view_count = lax.axis_size("views")
    own_view = lax.axis_index("views")
    source = tokens[0]
    tok_rows = source.shape[0]
    width = source.shape[1]
    normed = rms_scale(source.astype(jnp.float32), in_gain).astype(jnp.bfloat16)
    query = jnp.dot(normed, w_query, preferred_element_type=jnp.float32).astype(jnp.bfloat16)
    key_own = jnp.dot(normed, w_key, preferred_element_type=jnp.float32).astype(jnp.bfloat16)
    value_own = jnp.dot(normed, w_value, preferred_element_type=jnp.float32).astype(jnp.bfloat16)
    query3 = query.reshape(tok_rows, HEADS, HEAD_DIM)
    listed_row = covis_list[0]
    valid = jnp.arange(listed_row.shape[0], dtype=jnp.int32) < covis_count[0]

    def flag_for(offset):
        target = (own_view + offset) % view_count
        return jnp.any((listed_row == target) & valid)

    state = attend_block(query3, key_own, value_own)
    upward = (key_own, value_own)
    downward = (key_own, value_own)
    for step in range(1, REACH + 1):
        upward = from_behind((upward[0], upward[1]), "views", 1)
        state = combine(state, attend_block(query3, upward[0], upward[1]), flag_for(-step))
        downward = from_behind((downward[0], downward[1]), "views", -1)
        state = combine(state, attend_block(query3, downward[0], downward[1]), flag_for(step))
    numer, peak, total = state
    attended = numer.reshape(tok_rows, HEADS, HEAD_DIM) / total[..., None]
    head_normed = (
        rms_scale(attended, out_gain.reshape(HEADS, HEAD_DIM))
        .astype(jnp.bfloat16)
        .reshape(tok_rows, width)
    )
    update = jnp.dot(head_normed, w_out, preferred_element_type=jnp.float32)
    return (source.astype(jnp.float32) + update).astype(jnp.bfloat16)[None]


def solution(mesh):
    in_specs = (
        P(("groups", "views"), None, None),
        P(),
        P(),
        P(),
        P(),
        P(),
        P(),
        P(("groups", "views"), None),
        P(("groups", "views")),
    )
    out_specs = P(("groups", "views"), None, None)
    return jax.shard_map(
        on_device, mesh=mesh, in_specs=in_specs, out_specs=out_specs, check_vma=False
    )
```

profile of v0, /device:TPU:1, one launch (start us, length us, event | category | flops | bytes accessed | tf_op | source)
XLA Modules:
  0.0 155.2 jit_solution(14820396399054723734)
XLA Ops:
  1.7 2.1 %convolution_convert_fusion.1 = bf16[128,1024]{1,0:T(8,128)(2,1)} fusion(bf16[1024,1024]{1,0:T(8,128)(2,1)S(1)} %copy-done, bf16[1,128,1024]{2,1,0:T(8,128)(2,1)} %param.9, f32[1024]{0:T(1024)} %param.10, f32[128]{0:T(128)S(1)} %add_rsqrt_fusion.1), kind=kOutput, calls=%fused_computation.78 | convolution fusion | flops 269090816 | bytes 2626048 | tf_op jit(solution)/shard_map/dot_general | solution.py:62
  3.9 2.6 %collective-permute-start = (bf16[128,1024]{1,0:T(8,128)(2,1)}, bf16[128,1024]{1,0:T(8,128)(2,1)}, u32[]{:S(2)}, u32[]{:S(2)}) collective-permute-start(bf16[128,1024]{1,0:T(8,128)(2,1)} %convolution_convert_fusion.1), channel_id=1, source_target_pairs={{15,0},{0,1},{1,2},{2,3},{3,4},{4,5},{5,6},{6,7},{7,8},{8,9},{9,10... | collective-permute-start | bytes 786440 | tf_op jit(solution)/shard_map/ppermute | solution.py:14
  7.7 2.9 %collective-permute-start.3 = (bf16[128,1024]{1,0:T(8,128)(2,1)}, bf16[128,1024]{1,0:T(8,128)(2,1)}, u32[]{:S(2)}, u32[]{:S(2)}) collective-permute-start(bf16[128,1024]{1,0:T(8,128)(2,1)} %convolution_convert_fusion.2), channel_id=1, source_target_pairs={{1,0},{2,1},{3,2},{4,3},{5,4},{6,5},{7,6},{8,7},{9,8},{10,9},{11,1... | collective-permute-start | bytes 786440 | tf_op jit(solution)/shard_map/ppermute | solution.py:14
  10.6 1.8 %copy.63 = bf16[128,1024]{0,1:T(8,128)(2,1)} copy(bf16[128,1024]{1,0:T(8,128)(2,1)} %convolution_convert_fusion.1) | data formatting | bytes 524288 | tf_op jit(solution)/shard_map/convert_element_type | solution.py:62
  12.4 1.8 %copy.62 = bf16[128,1024]{0,1:T(8,128)(2,1)} copy(bf16[128,1024]{1,0:T(8,128)(2,1)} %convolution_convert_fusion.2) | data formatting | bytes 524288 | tf_op jit(solution)/shard_map/convert_element_type | solution.py:63
  14.8 2.1 %convolution_convert_fusion = bf16[128,1024]{1,0:T(8,128)(2,1)S(1)} fusion(bf16[1024,1024]{1,0:T(8,128)(2,1)} %param.11, bf16[1,128,1024]{2,1,0:T(8,128)(2,1)S(1)} %copy-done.15, f32[1024]{0:T(1024)S(1)} %copy-done.31, f32[128]{0:T(128)S(1)} %add_rsqrt_fusion.1), kind=kOutput, calls=%fused_computation.77 | convolution fusion | flops 269090816 | bytes 2626048 | tf_op jit(solution)/shard_map/dot_general | solution.py:61
  20.0 1.8 %copy.66 = bf16[128,1024]{0,1:T(8,128)(2,1)} copy(bf16[128,1024]{1,0:T(8,128)(2,1)} %collective-permute-done) | data formatting | bytes 524288 | tf_op jit(solution)/shard_map/ppermute | solution.py:14
  21.8 2.3 %fusion.138 = (f32[128,16]{0,1:T(8,128)S(1)}, f32[128,16,128]{0,2,1:T(8,128)}) fusion(bf16[128,16,64]{0,2,1:T(8,128)(2,1)} %bitcast.290, bf16[128,16,64]{0,2,1:T(8,128)(2,1)S(1)} %bitcast.259), kind=kOutput, calls=%fused_computation.218 | convolution fusion | flops 34076672 | bytes 1581056 | tf_op jit(solution)/shard_map/qhd,khd->qhk/dot_general | solution.py:26
  24.1 4.4 %collective-permute-start.6 = (bf16[128,1024]{1,0:T(8,128)(2,1)}, bf16[128,1024]{1,0:T(8,128)(2,1)}, u32[]{:S(2)}, u32[]{:S(2)}) collective-permute-start(bf16[128,1024]{1,0:T(8,128)(2,1)} %collective-permute-done.2), channel_id=1, source_target_pairs={{1,0},{2,1},{3,2},{4,3},{5,4},{6,5},{7,6},{8,7},{9,8},{10,9},{11,1... | collective-permute-start | bytes 786440 | tf_op jit(solution)/shard_map/ppermute | solution.py:14
  28.5 1.8 %copy.69 = bf16[128,1024]{0,1:T(8,128)(2,1)} copy(bf16[128,1024]{1,0:T(8,128)(2,1)} %collective-permute-done.2) | data formatting | bytes 524288 | tf_op jit(solution)/shard_map/ppermute | solution.py:14
  30.3 1.8 %copy.70 = bf16[128,1024]{0,1:T(8,128)(2,1)} copy(bf16[128,1024]{1,0:T(8,128)(2,1)} %collective-permute-done.3) | data formatting | bytes 524288 | tf_op jit(solution)/shard_map/ppermute | solution.py:14
  32.1 4.5 %collective-permute-start.7 = (bf16[128,1024]{1,0:T(8,128)(2,1)}, bf16[128,1024]{1,0:T(8,128)(2,1)}, u32[]{:S(2)}, u32[]{:S(2)}) collective-permute-start(bf16[128,1024]{1,0:T(8,128)(2,1)} %collective-permute-done.3), channel_id=1, source_target_pairs={{1,0},{2,1},{3,2},{4,3},{5,4},{6,5},{7,6},{8,7},{9,8},{10,9},{11,1... | collective-permute-start | bytes 786440 | tf_op jit(solution)/shard_map/ppermute | solution.py:14
  38.2 1.8 %copy.67 = bf16[128,1024]{0,1:T(8,128)(2,1)} copy(bf16[128,1024]{1,0:T(8,128)(2,1)} %collective-permute-done.1) | data formatting | bytes 524288 | tf_op jit(solution)/shard_map/ppermute | solution.py:14
  40.0 2.3 %fusion.137 = (f32[128,16]{0,1:T(8,128)S(1)}, f32[128,16,128]{0,2,1:T(8,128)}) fusion(bf16[128,16,64]{0,2,1:T(8,128)(2,1)} %bitcast.287, bf16[128,16,64]{0,2,1:T(8,128)(2,1)S(1)} %bitcast.260), kind=kOutput, calls=%fused_computation.217 | convolution fusion | flops 34076672 | bytes 1581056 | tf_op jit(solution)/shard_map/qhd,khd->qhk/dot_general | solution.py:26
  42.3 1.8 %copy.72 = bf16[128,1024]{0,1:T(8,128)(2,1)} copy(bf16[128,1024]{1,0:T(8,128)(2,1)} %collective-permute-done.4) | data formatting | bytes 524288 | tf_op jit(solution)/shard_map/ppermute | solution.py:14
  44.1 2.3 %fusion.136 = (f32[128,16]{0,1:T(8,128)S(1)}, f32[128,16,128]{0,2,1:T(8,128)}) fusion(bf16[128,16,64]{0,2,1:T(8,128)(2,1)} %bitcast.291, bf16[128,16,64]{0,2,1:T(8,128)(2,1)S(1)} %bitcast.261), kind=kOutput, calls=%fused_computation.216 | convolution fusion | flops 34076672 | bytes 1581056 | tf_op jit(solution)/shard_map/qhd,khd->qhk/dot_general | solution.py:26
  46.9 1.8 %copy.75 = bf16[128,1024]{0,1:T(8,128)(2,1)} copy(bf16[128,1024]{1,0:T(8,128)(2,1)} %collective-permute-done.6) | data formatting | bytes 524288 | tf_op jit(solution)/shard_map/ppermute | solution.py:14
  50.5 4.5 %collective-permute-start.11 = (bf16[128,1024]{1,0:T(8,128)(2,1)}, bf16[128,1024]{1,0:T(8,128)(2,1)}, u32[]{:S(2)}, u32[]{:S(2)}) collective-permute-start(bf16[128,1024]{1,0:T(8,128)(2,1)} %collective-permute-done.7), channel_id=1, source_target_pairs={{1,0},{2,1},{3,2},{4,3},{5,4},{6,5},{7,6},{8,7},{9,8},{10,9},{11,1... | collective-permute-start | bytes 786440 | tf_op jit(solution)/shard_map/ppermute | solution.py:14
  55.0 1.9 %fusion.56 = (f32[128,16]{0,1:T(8,128)S(1)}, f32[128,16]{0,1:T(8,128)S(1)}) fusion(f32[128,16,128]{0,2,1:T(8,128)} %get-tuple-element.68, f32[128,16]{0,1:T(8,128)S(1)} %get-tuple-element.67, f32[128,16,128]{0,2,1:T(8,128)} %get-tuple-element.66, f32[128,16]{0,1:T(8,128)S(1)} %get-tuple-element.65), kind=kLoop, calls=%fused_computation.99 | loop fusion | flops 1044480 | bytes 2129920 | tf_op jit(solution)/shard_map/reduce_sum | solution.py:31
  56.9 1.8 %copy.73 = bf16[128,1024]{0,1:T(8,128)(2,1)} copy(bf16[128,1024]{1,0:T(8,128)(2,1)} %collective-permute-done.5) | data formatting | bytes 524288 | tf_op jit(solution)/shard_map/ppermute | solution.py:14
  58.7 2.3 %fusion.135 = (f32[128,16]{0,1:T(8,128)S(1)}, f32[128,16,128]{0,2,1:T(8,128)}) fusion(bf16[128,16,64]{0,2,1:T(8,128)(2,1)} %bitcast.284, bf16[128,16,64]{0,2,1:T(8,128)(2,1)S(1)} %bitcast.262), kind=kOutput, calls=%fused_computation.215 | convolution fusion | flops 34076672 | bytes 1581056 | tf_op jit(solution)/shard_map/qhd,khd->qhk/dot_general | solution.py:26
  61.0 1.8 %copy.78 = bf16[128,1024]{0,1:T(8,128)(2,1)} copy(bf16[128,1024]{1,0:T(8,128)(2,1)} %collective-permute-done.8) | data formatting | bytes 524288 | tf_op jit(solution)/shard_map/ppermute | solution.py:14
  62.8 2.3 %fusion.134 = (f32[128,16]{0,1:T(8,128)S(1)}, f32[128,16,128]{0,2,1:T(8,128)}) fusion(bf16[128,16,64]{0,2,1:T(8,128)(2,1)} %bitcast.292, bf16[128,16,64]{0,2,1:T(8,128)(2,1)S(1)} %bitcast.263), kind=kOutput, calls=%fused_computation.214 | convolution fusion | flops 34076672 | bytes 1581056 | tf_op jit(solution)/shard_map/qhd,khd->qhk/dot_general | solution.py:26
  65.6 1.8 %copy.81 = bf16[128,1024]{0,1:T(8,128)(2,1)} copy(bf16[128,1024]{1,0:T(8,128)(2,1)} %collective-permute-done.10) | data formatting | bytes 524288 | tf_op jit(solution)/shard_map/ppermute | solution.py:14
  67.4 1.8 %copy.82 = bf16[128,1024]{0,1:T(8,128)(2,1)} copy(bf16[128,1024]{1,0:T(8,128)(2,1)} %collective-permute-done.11) | data formatting | bytes 524288 | tf_op jit(solution)/shard_map/ppermute | solution.py:14
  69.2 4.5 %collective-permute-start.15 = (bf16[128,1024]{1,0:T(8,128)(2,1)}, bf16[128,1024]{1,0:T(8,128)(2,1)}, u32[]{:S(2)}, u32[]{:S(2)}) collective-permute-start(bf16[128,1024]{1,0:T(8,128)(2,1)} %collective-permute-done.11), channel_id=1, source_target_pairs={{1,0},{2,1},{3,2},{4,3},{5,4},{6,5},{7,6},{8,7},{9,8},{10,9},{11,1... | collective-permute-start | bytes 786440 | tf_op jit(solution)/shard_map/ppermute | solution.py:14
  73.6 2.5 %fusion.60 = (f32[128,16]{0,1:T(8,128)S(1)}, f32[128,16]{0,1:T(8,128)}) fusion(f32[128,16,128]{0,2,1:T(8,128)} %get-tuple-element.64, f32[128,16]{0,1:T(8,128)S(1)} %get-tuple-element.63, f32[128,16,128]{0,2,1:T(8,128)} %get-tuple-element.62, f32[128,16]{0,1:T(8,128)S(1)} %get-tuple-element.61), kind=kLoop, calls=%fused_computation.103 | loop fusion | flops 1044480 | bytes 2129920 | tf_op jit(solution)/shard_map/reduce_sum | solution.py:31
  77.9 2.3 %fusion.133 = (f32[128,16]{0,1:T(8,128)S(1)}, f32[128,16,128]{0,2,1:T(8,128)}) fusion(bf16[128,16,64]{0,2,1:T(8,128)(2,1)} %bitcast.285, bf16[128,16,64]{0,2,1:T(8,128)(2,1)S(1)} %bitcast.264), kind=kOutput, calls=%fused_computation.213 | convolution fusion | flops 34076672 | bytes 1581056 | tf_op jit(solution)/shard_map/qhd,khd->qhk/dot_general | solution.py:26
  80.2 1.8 %copy.84 = bf16[128,1024]{0,1:T(8,128)(2,1)} copy(bf16[128,1024]{1,0:T(8,128)(2,1)} %collective-permute-done.12) | data formatting | bytes 524288 | tf_op jit(solution)/shard_map/ppermute | solution.py:14
  82.0 2.3 %fusion.132 = (f32[128,16]{0,1:T(8,128)S(1)}, f32[128,16,128]{0,2,1:T(8,128)}) fusion(bf16[128,16,64]{0,2,1:T(8,128)(2,1)} %bitcast.293, bf16[128,16,64]{0,2,1:T(8,128)(2,1)S(1)} %bitcast.265), kind=kOutput, calls=%fused_computation.212 | convolution fusion | flops 34076672 | bytes 1581056 | tf_op jit(solution)/shard_map/qhd,khd->qhk/dot_general | solution.py:26
  84.9 1.8 %copy.87 = bf16[128,1024]{0,1:T(8,128)(2,1)} copy(bf16[128,1024]{1,0:T(8,128)(2,1)} %collective-permute-done.14) | data formatting | bytes 524288 | tf_op jit(solution)/shard_map/ppermute | solution.py:14
  86.6 1.8 %copy.88 = bf16[128,1024]{0,1:T(8,128)(2,1)} copy(bf16[128,1024]{1,0:T(8,128)(2,1)} %collective-permute-done.15) | data formatting | bytes 524288 | tf_op jit(solution)/shard_map/ppermute | solution.py:14
  88.5 4.5 %collective-permute-start.19 = (bf16[128,1024]{1,0:T(8,128)(2,1)}, bf16[128,1024]{1,0:T(8,128)(2,1)}, u32[]{:S(2)}, u32[]{:S(2)}) collective-permute-start(bf16[128,1024]{1,0:T(8,128)(2,1)} %collective-permute-done.15), channel_id=1, source_target_pairs={{1,0},{2,1},{3,2},{4,3},{5,4},{6,5},{7,6},{8,7},{9,8},{10,9},{11,1... | collective-permute-start | bytes 786440 | tf_op jit(solution)/shard_map/ppermute | solution.py:14
  92.9 2.5 %fusion.64 = (f32[128,16]{0,1:T(8,128)}, f32[128,16]{0,1:T(8,128)}) fusion(f32[128,16,128]{0,2,1:T(8,128)} %get-tuple-element.60, f32[128,16]{0,1:T(8,128)S(1)} %get-tuple-element.59, f32[128,16,128]{0,2,1:T(8,128)} %get-tuple-element.58, f32[128,16]{0,1:T(8,128)S(1)} %get-tuple-element.57), kind=kLoop, calls=%fused_computation.107 | loop fusion | flops 1044480 | bytes 2129920 | tf_op jit(solution)/shard_map/reduce_sum | solution.py:31
  95.4 1.8 %copy.85 = bf16[128,1024]{0,1:T(8,128)(2,1)} copy(bf16[128,1024]{1,0:T(8,128)(2,1)} %collective-permute-done.13) | data formatting | bytes 524288 | tf_op jit(solution)/shard_map/ppermute | solution.py:14
  97.2 2.3 %fusion.131 = (f32[128,16]{0,1:T(8,128)S(1)}, f32[128,16,128]{0,2,1:T(8,128)}) fusion(bf16[128,16,64]{0,2,1:T(8,128)(2,1)} %bitcast.286, bf16[128,16,64]{0,2,1:T(8,128)(2,1)S(1)} %bitcast.266), kind=kOutput, calls=%fused_computation.211 | convolution fusion | flops 34076672 | bytes 1581056 | tf_op jit(solution)/shard_map/qhd,khd->qhk/dot_general | solution.py:26
  99.5 1.8 %copy.93 = bf16[128,1024]{0,1:T(8,128)(2,1)} copy(bf16[128,1024]{1,0:T(8,128)(2,1)} %collective-permute-done.18) | data formatting | bytes 524288 | tf_op jit(solution)/shard_map/ppermute | solution.py:14
  101.3 2.3 %fusion.129 = (f32[128,16]{0,1:T(8,128)S(1)}, f32[128,16,128]{0,2,1:T(8,128)}) fusion(bf16[128,16,64]{0,2,1:T(8,128)(2,1)} %bitcast.294, bf16[128,16,64]{0,2,1:T(8,128)(2,1)S(1)} %bitcast.267), kind=kOutput, calls=%fused_computation.209 | convolution fusion | flops 34076672 | bytes 1581056 | tf_op jit(solution)/shard_map/qhd,khd->qhk/dot_general | solution.py:26
  103.6 1.8 %copy.90 = bf16[128,1024]{0,1:T(8,128)(2,1)} copy(bf16[128,1024]{1,0:T(8,128)(2,1)} %collective-permute-done.16) | data formatting | bytes 524288 | tf_op jit(solution)/shard_map/ppermute | solution.py:14
  108.3 1.8 %copy.94 = bf16[128,1024]{0,1:T(8,128)(2,1)} copy(bf16[128,1024]{1,0:T(8,128)(2,1)} %collective-permute-done.19) | data formatting | bytes 524288 | tf_op jit(solution)/shard_map/ppermute | solution.py:14
  110.1 4.4 %collective-permute-start.23 = (bf16[128,1024]{1,0:T(8,128)(2,1)}, bf16[128,1024]{1,0:T(8,128)(2,1)}, u32[]{:S(2)}, u32[]{:S(2)}) collective-permute-start(bf16[128,1024]{1,0:T(8,128)(2,1)} %collective-permute-done.19), channel_id=1, source_target_pairs={{1,0},{2,1},{3,2},{4,3},{5,4},{6,5},{7,6},{8,7},{9,8},{10,9},{11,1... | collective-permute-start | bytes 786440 | tf_op jit(solution)/shard_map/ppermute | solution.py:14
  114.5 1.8 %copy.91 = bf16[128,1024]{0,1:T(8,128)(2,1)} copy(bf16[128,1024]{1,0:T(8,128)(2,1)} %collective-permute-done.17) | data formatting | bytes 524288 | tf_op jit(solution)/shard_map/ppermute | solution.py:14
  116.3 6.9 %select_maximum_fusion.1 = (f32[128,16]{0,1:T(8,128)}, f32[128,16]{0,1:T(8,128)}, f32[128,16]{0,1:T(8,128)}, f32[128,16]{0,1:T(8,128)}, f32[128,16]{0,1:T(8,128)}) fusion(f32[128,16]{0,1:T(8,128)S(1)} %get-tuple-element.51, pred[]{:T(512)} %get-tuple-element.6, f32[128,16]{0,1:T(8,128)S(1)} %get-tuple-element.53, pred[]{:T(512)} %get-tuple-element.7, ...), kind=kLoop, calls=%fused_computation.171 | loop fusion | flops 40960 | bytes 131082 | tf_op jit(solution)/shard_map/max | solution.py:42
  123.2 1.8 %copy.96 = bf16[128,1024]{0,1:T(8,128)(2,1)} copy(bf16[128,1024]{1,0:T(8,128)(2,1)} %collective-permute-done.20) | data formatting | bytes 524288 | tf_op jit(solution)/shard_map/ppermute | solution.py:14
  125.0 2.4 %fusion.128 = (f32[128,16]{0,1:T(8,128)S(1)}, f32[128,16,128]{0,2,1:T(8,128)}) fusion(bf16[128,16,64]{0,2,1:T(8,128)(2,1)} %bitcast.289, bf16[128,16,64]{0,2,1:T(8,128)(2,1)S(1)} %bitcast.269), kind=kOutput, calls=%fused_computation.208 | convolution fusion | flops 34076672 | bytes 1581056 | tf_op jit(solution)/shard_map/qhd,khd->qhk/dot_general | solution.py:26
  127.4 1.8 %copy.99 = bf16[128,1024]{0,1:T(8,128)(2,1)} copy(bf16[128,1024]{1,0:T(8,128)(2,1)} %collective-permute-done.22) | data formatting | bytes 524288 | tf_op jit(solution)/shard_map/ppermute | solution.py:14
  132.4 8.4 %multiply_add_fusion = (f32[128,16]{0,1:T(8,128)}, f32[128,16]{0,1:T(8,128)}, f32[128,16]{0,1:T(8,128)}, f32[128,16]{0,1:T(8,128)S(1)}, f32[128,16]{0,1:T(8,128)...) fusion(f32[128,16]{0,1:T(8,128)S(1)} %fusion.76, ...), kind=kLoop, calls=%fused_computation.147 | loop fusion | flops 186368 | bytes 458764 | tf_op jit(solution)/shard_map/add | solution.py:50
  151.7 2.0 %multiply_reduce_fusion = (f32[128,16]{0,1:T(8,128)S(1)}, f32[128,16,64]{0,2,1:T(8,128)S(1)}) fusion(f32[128,16]{0,1:T(8,128)S(1)} %copy-done.44, f32[128,16,64]{0,2,1:T(8,128)} %fusion.49, f32[128,16]{0,1:T(8,128)S(1)} %copy-done.46, f32[128,16,64]{0,2,1:T(8,128)} %fusion.42, f32[128,16]{0,1:T(8,128)S(1)} %copy-done.45, ...), kind=kOutput, calls=%fused_computation.127 | convolution fusion | flops 34994176 | bytes 2924544 | tf_op jit(solution)/shard_map/qhk,khd->qhd/dot_general | solution.py:32
  (170 shorter events, 30.7 us)
Async XLA Ops:
  0.0 6.5 %copy-start.15 = (bf16[1,128,1024]{2,1,0:T(8,128)(2,1)S(1)}, bf16[1,128,1024]{2,1,0:T(8,128)(2,1)}, u32[]{:S(2)}) copy-start(bf16[1,128,1024]{2,1,0:T(8,128)(2,1)} %param.9) | copy-start | bytes 786436
  0.0 6.5 %copy-start.31 = (f32[1024]{0:T(1024)S(1)}, f32[1024]{0:T(1024)}, u32[]{:S(2)}) copy-start(f32[1024]{0:T(1024)} %param.10) | copy-start | bytes 12292
  0.0 6.4 %copy-start.18 = (bf16[1024,1024]{1,0:T(8,128)(2,1)S(1)}, bf16[1024,1024]{1,0:T(8,128)(2,1)}, u32[]{:S(2)}) copy-start(bf16[1024,1024]{1,0:T(8,128)(2,1)} %param.13) | copy-start | bytes 6291460
  3.8 20.3 %collective-permute-start.2 = (bf16[128,1024]{1,0:T(8,128)(2,1)}, bf16[128,1024]{1,0:T(8,128)(2,1)}, u32[]{:S(2)}, u32[]{:S(2)}) collective-permute-start(bf16[128,1024]{1,0:T(8,128)(2,1)} %convolution_convert_fusion.1), channel_id=1, source_target_pairs={{1,0},{2,1},{3,2},{4,3},{5,4},{6,5},{7,6},{8,7},{9,8},{10,9},{11,1... | collective-permute-start | bytes 786440 | tf_op jit(solution)/shard_map/ppermute | solution.py:14
  3.9 16.1 %collective-permute-start = (bf16[128,1024]{1,0:T(8,128)(2,1)}, bf16[128,1024]{1,0:T(8,128)(2,1)}, u32[]{:S(2)}, u32[]{:S(2)}) collective-permute-start(bf16[128,1024]{1,0:T(8,128)(2,1)} %convolution_convert_fusion.1), channel_id=1, source_target_pairs={{15,0},{0,1},{1,2},{2,3},{3,4},{4,5},{5,6},{6,7},{7,8},{8,9},{9,10... | collective-permute-start | bytes 786440 | tf_op jit(solution)/shard_map/ppermute | solution.py:14
  7.7 22.7 %collective-permute-start.3 = (bf16[128,1024]{1,0:T(8,128)(2,1)}, bf16[128,1024]{1,0:T(8,128)(2,1)}, u32[]{:S(2)}, u32[]{:S(2)}) collective-permute-start(bf16[128,1024]{1,0:T(8,128)(2,1)} %convolution_convert_fusion.2), channel_id=1, source_target_pairs={{1,0},{2,1},{3,2},{4,3},{5,4},{6,5},{7,6},{8,7},{9,8},{10,9},{11,1... | collective-permute-start | bytes 786440 | tf_op jit(solution)/shard_map/ppermute | solution.py:14
  10.6 27.7 %collective-permute-start.1 = (bf16[128,1024]{1,0:T(8,128)(2,1)}, bf16[128,1024]{1,0:T(8,128)(2,1)}, u32[]{:S(2)}, u32[]{:S(2)}) collective-permute-start(bf16[128,1024]{1,0:T(8,128)(2,1)} %convolution_convert_fusion.2), channel_id=1, source_target_pairs={{15,0},{0,1},{1,2},{2,3},{3,4},{4,5},{5,6},{6,7},{7,8},{8,9},{9,10... | collective-permute-start | bytes 786440 | tf_op jit(solution)/shard_map/ppermute | solution.py:14
  10.6 6.6 %copy-start.47 = (f32[1024]{0:T(1024)S(1)}, f32[1024]{0:T(1024)}, u32[]{:S(2)}) copy-start(f32[1024]{0:T(1024)} %param.15) | copy-start | bytes 12292
  10.6 7.2 %copy-start.48 = (s32[1,12]{1,0:T(1,128)S(1)}, s32[1,12]{1,0:T(1,128)}, u32[]{:S(2)}) copy-start(s32[1,12]{1,0:T(1,128)} %param.16) | copy-start | bytes 148
  24.1 18.2 %collective-permute-start.4 = (bf16[128,1024]{1,0:T(8,128)(2,1)}, bf16[128,1024]{1,0:T(8,128)(2,1)}, u32[]{:S(2)}, u32[]{:S(2)}) collective-permute-start(bf16[128,1024]{1,0:T(8,128)(2,1)} %collective-permute-done), channel_id=1, source_target_pairs={{15,0},{0,1},{1,2},{2,3},{3,4},{4,5},{5,6},{6,7},{7,8},{8,9},{9,10... | collective-permute-start | bytes 786440 | tf_op jit(solution)/shard_map/ppermute | solution.py:14
  24.1 22.3 %collective-permute-start.6 = (bf16[128,1024]{1,0:T(8,128)(2,1)}, bf16[128,1024]{1,0:T(8,128)(2,1)}, u32[]{:S(2)}, u32[]{:S(2)}) collective-permute-start(bf16[128,1024]{1,0:T(8,128)(2,1)} %collective-permute-done.2), channel_id=1, source_target_pairs={{1,0},{2,1},{3,2},{4,3},{5,4},{6,5},{7,6},{8,7},{9,8},{10,9},{11,1... | collective-permute-start | bytes 786440 | tf_op jit(solution)/shard_map/ppermute | solution.py:14
  32.1 16.6 %collective-permute-start.7 = (bf16[128,1024]{1,0:T(8,128)(2,1)}, bf16[128,1024]{1,0:T(8,128)(2,1)}, u32[]{:S(2)}, u32[]{:S(2)}) collective-permute-start(bf16[128,1024]{1,0:T(8,128)(2,1)} %collective-permute-done.3), channel_id=1, source_target_pairs={{1,0},{2,1},{3,2},{4,3},{5,4},{6,5},{7,6},{8,7},{9,8},{10,9},{11,1... | collective-permute-start | bytes 786440 | tf_op jit(solution)/shard_map/ppermute | solution.py:14
  40.0 16.9 %collective-permute-start.5 = (bf16[128,1024]{1,0:T(8,128)(2,1)}, bf16[128,1024]{1,0:T(8,128)(2,1)}, u32[]{:S(2)}, u32[]{:S(2)}) collective-permute-start(bf16[128,1024]{1,0:T(8,128)(2,1)} %collective-permute-done.1), channel_id=1, source_target_pairs={{15,0},{0,1},{1,2},{2,3},{3,4},{4,5},{5,6},{6,7},{7,8},{8,9},{9,10... | collective-permute-start | bytes 786440 | tf_op jit(solution)/shard_map/ppermute | solution.py:14
  46.4 14.6 %collective-permute-start.8 = (bf16[128,1024]{1,0:T(8,128)(2,1)}, bf16[128,1024]{1,0:T(8,128)(2,1)}, u32[]{:S(2)}, u32[]{:S(2)}) collective-permute-start(bf16[128,1024]{1,0:T(8,128)(2,1)} %collective-permute-done.4), channel_id=1, source_target_pairs={{15,0},{0,1},{1,2},{2,3},{3,4},{4,5},{5,6},{6,7},{7,8},{8,9},{9,10... | collective-permute-start | bytes 786440 | tf_op jit(solution)/shard_map/ppermute | solution.py:14
  46.4 18.6 %collective-permute-start.10 = (bf16[128,1024]{1,0:T(8,128)(2,1)}, bf16[128,1024]{1,0:T(8,128)(2,1)}, u32[]{:S(2)}, u32[]{:S(2)}) collective-permute-start(bf16[128,1024]{1,0:T(8,128)(2,1)} %collective-permute-done.6), channel_id=1, source_target_pairs={{1,0},{2,1},{3,2},{4,3},{5,4},{6,5},{7,6},{8,7},{9,8},{10,9},{11,1... | collective-permute-start | bytes 786440 | tf_op jit(solution)/shard_map/ppermute | solution.py:14
  50.5 16.9 %collective-permute-start.11 = (bf16[128,1024]{1,0:T(8,128)(2,1)}, bf16[128,1024]{1,0:T(8,128)(2,1)}, u32[]{:S(2)}, u32[]{:S(2)}) collective-permute-start(bf16[128,1024]{1,0:T(8,128)(2,1)} %collective-permute-done.7), channel_id=1, source_target_pairs={{1,0},{2,1},{3,2},{4,3},{5,4},{6,5},{7,6},{8,7},{9,8},{10,9},{11,1... | collective-permute-start | bytes 786440 | tf_op jit(solution)/shard_map/ppermute | solution.py:14
  58.7 17.4 %collective-permute-start.9 = (bf16[128,1024]{1,0:T(8,128)(2,1)}, bf16[128,1024]{1,0:T(8,128)(2,1)}, u32[]{:S(2)}, u32[]{:S(2)}) collective-permute-start(bf16[128,1024]{1,0:T(8,128)(2,1)} %collective-permute-done.5), channel_id=1, source_target_pairs={{15,0},{0,1},{1,2},{2,3},{3,4},{4,5},{5,6},{6,7},{7,8},{8,9},{9,10... | collective-permute-start | bytes 786440 | tf_op jit(solution)/shard_map/ppermute | solution.py:14
  65.1 15.2 %collective-permute-start.12 = (bf16[128,1024]{1,0:T(8,128)(2,1)}, bf16[128,1024]{1,0:T(8,128)(2,1)}, u32[]{:S(2)}, u32[]{:S(2)}) collective-permute-start(bf16[128,1024]{1,0:T(8,128)(2,1)} %collective-permute-done.8), channel_id=1, source_target_pairs={{15,0},{0,1},{1,2},{2,3},{3,4},{4,5},{5,6},{6,7},{7,8},{8,9},{9,10... | collective-permute-start | bytes 786440 | tf_op jit(solution)/shard_map/ppermute | solution.py:14
  65.1 19.3 %collective-permute-start.14 = (bf16[128,1024]{1,0:T(8,128)(2,1)}, bf16[128,1024]{1,0:T(8,128)(2,1)}, u32[]{:S(2)}, u32[]{:S(2)}) collective-permute-start(bf16[128,1024]{1,0:T(8,128)(2,1)} %collective-permute-done.10), channel_id=1, source_target_pairs={{1,0},{2,1},{3,2},{4,3},{5,4},{6,5},{7,6},{8,7},{9,8},{10,9},{11,1... | collective-permute-start | bytes 786440 | tf_op jit(solution)/shard_map/ppermute | solution.py:14
  69.2 17.5 %collective-permute-start.15 = (bf16[128,1024]{1,0:T(8,128)(2,1)}, bf16[128,1024]{1,0:T(8,128)(2,1)}, u32[]{:S(2)}, u32[]{:S(2)}) collective-permute-start(bf16[128,1024]{1,0:T(8,128)(2,1)} %collective-permute-done.11), channel_id=1, source_target_pairs={{1,0},{2,1},{3,2},{4,3},{5,4},{6,5},{7,6},{8,7},{9,8},{10,9},{11,1... | collective-permute-start | bytes 786440 | tf_op jit(solution)/shard_map/ppermute | solution.py:14
  77.9 17.5 %collective-permute-start.13 = (bf16[128,1024]{1,0:T(8,128)(2,1)}, bf16[128,1024]{1,0:T(8,128)(2,1)}, u32[]{:S(2)}, u32[]{:S(2)}) collective-permute-start(bf16[128,1024]{1,0:T(8,128)(2,1)} %collective-permute-done.9), channel_id=1, source_target_pairs={{15,0},{0,1},{1,2},{2,3},{3,4},{4,5},{5,6},{6,7},{7,8},{8,9},{9,10... | collective-permute-start | bytes 786440 | tf_op jit(solution)/shard_map/ppermute | solution.py:14
  84.3 19.2 %collective-permute-start.16 = (bf16[128,1024]{1,0:T(8,128)(2,1)}, bf16[128,1024]{1,0:T(8,128)(2,1)}, u32[]{:S(2)}, u32[]{:S(2)}) collective-permute-start(bf16[128,1024]{1,0:T(8,128)(2,1)} %collective-permute-done.12), channel_id=1, source_target_pairs={{15,0},{0,1},{1,2},{2,3},{3,4},{4,5},{5,6},{6,7},{7,8},{8,9},{9,10... | collective-permute-start | bytes 786440 | tf_op jit(solution)/shard_map/ppermute | solution.py:14
  84.3 15.2 %collective-permute-start.18 = (bf16[128,1024]{1,0:T(8,128)(2,1)}, bf16[128,1024]{1,0:T(8,128)(2,1)}, u32[]{:S(2)}, u32[]{:S(2)}) collective-permute-start(bf16[128,1024]{1,0:T(8,128)(2,1)} %collective-permute-done.14), channel_id=1, source_target_pairs={{1,0},{2,1},{3,2},{4,3},{5,4},{6,5},{7,6},{8,7},{9,8},{10,9},{11,1... | collective-permute-start | bytes 786440 | tf_op jit(solution)/shard_map/ppermute | solution.py:14
  88.5 19.9 %collective-permute-start.19 = (bf16[128,1024]{1,0:T(8,128)(2,1)}, bf16[128,1024]{1,0:T(8,128)(2,1)}, u32[]{:S(2)}, u32[]{:S(2)}) collective-permute-start(bf16[128,1024]{1,0:T(8,128)(2,1)} %collective-permute-done.15), channel_id=1, source_target_pairs={{1,0},{2,1},{3,2},{4,3},{5,4},{6,5},{7,6},{8,7},{9,8},{10,9},{11,1... | collective-permute-start | bytes 786440 | tf_op jit(solution)/shard_map/ppermute | solution.py:14
  97.2 17.3 %collective-permute-start.17 = (bf16[128,1024]{1,0:T(8,128)(2,1)}, bf16[128,1024]{1,0:T(8,128)(2,1)}, u32[]{:S(2)}, u32[]{:S(2)}) collective-permute-start(bf16[128,1024]{1,0:T(8,128)(2,1)} %collective-permute-done.13), channel_id=1, source_target_pairs={{15,0},{0,1},{1,2},{2,3},{3,4},{4,5},{5,6},{6,7},{7,8},{8,9},{9,10... | collective-permute-start | bytes 786440 | tf_op jit(solution)/shard_map/ppermute | solution.py:14
  106.8 16.4 %collective-permute-start.20 = (bf16[128,1024]{1,0:T(8,128)(2,1)}, bf16[128,1024]{1,0:T(8,128)(2,1)}, u32[]{:S(2)}, u32[]{:S(2)}) collective-permute-start(bf16[128,1024]{1,0:T(8,128)(2,1)} %collective-permute-done.16), channel_id=1, source_target_pairs={{15,0},{0,1},{1,2},{2,3},{3,4},{4,5},{5,6},{6,7},{7,8},{8,9},{9,10... | collective-permute-start | bytes 786440 | tf_op jit(solution)/shard_map/ppermute | solution.py:14
  107.8 19.6 %collective-permute-start.22 = (bf16[128,1024]{1,0:T(8,128)(2,1)}, bf16[128,1024]{1,0:T(8,128)(2,1)}, u32[]{:S(2)}, u32[]{:S(2)}) collective-permute-start(bf16[128,1024]{1,0:T(8,128)(2,1)} %collective-permute-done.18), channel_id=1, source_target_pairs={{1,0},{2,1},{3,2},{4,3},{5,4},{6,5},{7,6},{8,7},{9,8},{10,9},{11,1... | collective-permute-start | bytes 786440 | tf_op jit(solution)/shard_map/ppermute | solution.py:14
  110.1 38.1 %collective-permute-start.23 = (bf16[128,1024]{1,0:T(8,128)(2,1)}, bf16[128,1024]{1,0:T(8,128)(2,1)}, u32[]{:S(2)}, u32[]{:S(2)}) collective-permute-start(bf16[128,1024]{1,0:T(8,128)(2,1)} %collective-permute-done.19), channel_id=1, source_target_pairs={{1,0},{2,1},{3,2},{4,3},{5,4},{6,5},{7,6},{8,7},{9,8},{10,9},{11,1... | collective-permute-start | bytes 786440 | tf_op jit(solution)/shard_map/ppermute | solution.py:14
  116.3 34.2 %collective-permute-start.21 = (bf16[128,1024]{1,0:T(8,128)(2,1)}, bf16[128,1024]{1,0:T(8,128)(2,1)}, u32[]{:S(2)}, u32[]{:S(2)}) collective-permute-start(bf16[128,1024]{1,0:T(8,128)(2,1)} %collective-permute-done.17), channel_id=1, source_target_pairs={{15,0},{0,1},{1,2},{2,3},{3,4},{4,5},{5,6},{6,7},{7,8},{8,9},{9,10... | collective-permute-start | bytes 786440 | tf_op jit(solution)/shard_map/ppermute | solution.py:14
  129.2 3.1 %copy-start.32 = (f32[128,16]{0,1:T(8,128)S(1)}, f32[128,16]{0,1:T(8,128)}, u32[]{:S(2)}) copy-start(f32[128,16]{0,1:T(8,128)} %get-tuple-element.80) | copy-start | bytes 24580
  129.2 3.1 %copy-start.33 = (f32[128,16]{0,1:T(8,128)S(1)}, f32[128,16]{0,1:T(8,128)}, u32[]{:S(2)}) copy-start(f32[128,16]{0,1:T(8,128)} %get-tuple-element.81) | copy-start | bytes 24580
  129.2 3.1 %copy-start.34 = (f32[128,16]{0,1:T(8,128)S(1)}, f32[128,16]{0,1:T(8,128)}, u32[]{:S(2)}) copy-start(f32[128,16]{0,1:T(8,128)} %get-tuple-element.82) | copy-start | bytes 24580
  129.2 3.1 %copy-start.36 = (f32[128,16]{0,1:T(8,128)S(1)}, f32[128,16]{0,1:T(8,128)}, u32[]{:S(2)}) copy-start(f32[128,16]{0,1:T(8,128)} %get-tuple-element.83) | copy-start | bytes 24580
  129.2 3.1 %copy-start.37 = (f32[128,16]{0,1:T(8,128)S(1)}, f32[128,16]{0,1:T(8,128)}, u32[]{:S(2)}) copy-start(f32[128,16]{0,1:T(8,128)} %get-tuple-element.84) | copy-start | bytes 24580
  129.2 3.1 %copy-start.38 = (f32[128,16]{0,1:T(8,128)S(1)}, f32[128,16]{0,1:T(8,128)}, u32[]{:S(2)}) copy-start(f32[128,16]{0,1:T(8,128)} %get-tuple-element.42) | copy-start | bytes 24580
  129.2 3.1 %copy-start.39 = (f32[128,16]{0,1:T(8,128)S(1)}, f32[128,16]{0,1:T(8,128)}, u32[]{:S(2)}) copy-start(f32[128,16]{0,1:T(8,128)} %get-tuple-element.43) | copy-start | bytes 24580
  129.2 3.1 %copy-start.40 = (f32[128,16]{0,1:T(8,128)S(1)}, f32[128,16]{0,1:T(8,128)}, u32[]{:S(2)}) copy-start(f32[128,16]{0,1:T(8,128)} %get-tuple-element.44) | copy-start | bytes 24580
  129.2 3.1 %copy-start.41 = (f32[128,16]{0,1:T(8,128)S(1)}, f32[128,16]{0,1:T(8,128)}, u32[]{:S(2)}) copy-start(f32[128,16]{0,1:T(8,128)} %get-tuple-element.45) | copy-start | bytes 24580
  129.3 3.1 %copy-start.42 = (f32[128,16]{0,1:T(8,128)S(1)}, f32[128,16]{0,1:T(8,128)}, u32[]{:S(2)}) copy-start(f32[128,16]{0,1:T(8,128)} %get-tuple-element.46) | copy-start | bytes 24580
  130.7 10.0 %copy-start.1 = (f32[128,16,128]{0,2,1:T(8,128)S(1)}, f32[128,16,128]{0,2,1:T(8,128)}, u32[]{:S(2)}) copy-start(f32[128,16,128]{0,2,1:T(8,128)} %get-tuple-element.68) | copy-start | bytes 3145732
  130.7 10.0 %copy-start.22 = (bf16[128,1024]{0,1:T(8,128)(2,1)S(1)}, bf16[128,1024]{0,1:T(8,128)(2,1)}, u32[]{:S(2)}) copy-start(bf16[128,1024]{0,1:T(8,128)(2,1)} %copy.70) | copy-start | bytes 786436
  131.9 9.1 %copy-start.20 = (bf16[128,1024]{0,1:T(8,128)(2,1)S(1)}, bf16[128,1024]{0,1:T(8,128)(2,1)}, u32[]{:S(2)}) copy-start(bf16[128,1024]{0,1:T(8,128)(2,1)} %copy.62) | copy-start | bytes 786436
  132.2 9.1 %copy-start.2 = (f32[128,16,128]{0,2,1:T(8,128)S(1)}, f32[128,16,128]{0,2,1:T(8,128)}, u32[]{:S(2)}) copy-start(f32[128,16,128]{0,2,1:T(8,128)} %get-tuple-element.64) | copy-start | bytes 3145732
  132.3 9.1 %copy-start.24 = (bf16[128,1024]{0,1:T(8,128)(2,1)S(1)}, bf16[128,1024]{0,1:T(8,128)(2,1)}, u32[]{:S(2)}) copy-start(bf16[128,1024]{0,1:T(8,128)(2,1)} %copy.76) | copy-start | bytes 786436
  148.2 3.4 %copy-start.44 = (f32[128,16]{0,1:T(8,128)S(1)}, f32[128,16]{0,1:T(8,128)}, u32[]{:S(2)}) copy-start(f32[128,16]{0,1:T(8,128)} %get-tuple-element.17) | copy-start | bytes 24580
  148.3 3.4 %copy-start.45 = (f32[128,16]{0,1:T(8,128)S(1)}, f32[128,16]{0,1:T(8,128)}, u32[]{:S(2)}) copy-start(f32[128,16]{0,1:T(8,128)} %get-tuple-element.18) | copy-start | bytes 24580
  148.3 3.4 %copy-start.46 = (f32[128,16]{0,1:T(8,128)S(1)}, f32[128,16]{0,1:T(8,128)}, u32[]{:S(2)}) copy-start(f32[128,16]{0,1:T(8,128)} %get-tuple-element.19) | copy-start | bytes 24580
  150.5 3.2 %copy-start.43 = (f32[16,64]{1,0:T(8,128)S(1)}, f32[16,64]{1,0:T(8,128)}, u32[]{:S(2)}) copy-start(f32[16,64]{1,0:T(8,128)} %mul.584) | copy-start | bytes 12292
  (25 other events, 41.1 us)
where the time goes:
time: 157 us; the launch traced here: 155 us
  local copies, waits for them, and re-layouts  51 us (32%)
  matrix products  40.8 us (26%)
  starting transfers between devices  34.4 us (22%)
  other arithmetic  27.5 us (18%)
    ppermute x24, local copies, waits for them, and re-layouts, from_behind(): return lax.ppermute(block, axis, route)  41.7 us
    ppermute x24, starting transfers between devices, from_behind(): return lax.ppermute(block, axis, route)  34.4 us
    dot_general x13, matrix products, attend_block(): jnp.einsum('qhd,khd->qhk', query3, key3, preferred_element_type=jnp.float32)  27.2 us
    reduce_sum x7, other arithmetic, attend_block(): total = jnp.sum(weights, axis=-1)  9.91 us
    add x1, other arithmetic, combine(): total = total * keep_old + other_total * keep_new  8.35 us
    dot_general x13, matrix products, attend_block(): jnp.einsum('qhk,khd->qhd', weights.astype(jnp.bfloat16), value3, preferre...  7.03 us
    max x1, other arithmetic, combine(): newest = jnp.maximum(peak, other_peak)  6.86 us
    unnamed x98, local copies, waits for them, and re-layouts  4.86 us
  transfers between devices with their start and end apart: 24, of which 0 were waited for; matrix products, arithmetic and copies ran while one was open for 69% of the time, Pallas kernels for 0%

commit v1 on v0

v1 whole, which is shorter than its diff:
```python
import functools

import jax
import jax.numpy as jnp
from jax import lax
from jax.experimental import pallas as pl
from jax.experimental.pallas import tpu as pltpu
from jax.sharding import PartitionSpec as P

HEADS = 16
HEAD_DIM = 64
REACH = 6
PAIRS = HEADS // 2
F32 = jnp.float32
BF16 = jnp.bfloat16
BY_ROWS = (((1,), (1,)), ((), ()))
BY_COLUMNS = (((0,), (0,)), ((), ()))
MIB = 1024 * 1024


def normalize(block, gain):
    values = block.astype(F32)
    mean_sq = jnp.mean(values * values, axis=-1, keepdims=True)
    return (values * lax.rsqrt(mean_sq + 1e-06) * gain).astype(BF16)


def project_query(normed, w_query, query_ref):
    query = jnp.dot(normed, w_query[...], preferred_element_type=F32).astype(BF16)
    query = query * jnp.asarray(HEAD_DIM**-0.5, BF16)
    rows = query.shape[0]
    lane = lax.broadcasted_iota(jnp.int32, (rows, 2 * HEAD_DIM), 1)
    for pair in range(PAIRS):
        both = query[:, 2 * HEAD_DIM * pair : 2 * HEAD_DIM * (pair + 1)]
        zero = jnp.zeros_like(both)
        query_ref[pair, :rows, :] = jnp.where(lane < HEAD_DIM, both, zero)
        query_ref[pair, rows:, :] = jnp.where(lane >= HEAD_DIM, both, zero)


def attend(normed, flags, w_key, w_value_t, query_ref, key_ref, value_ref, old, new):
    blocks = len(flags)
    rows = normed.shape[0] // blocks
    key_ref[...] = jnp.dot(normed, w_key[...], preferred_element_type=F32).astype(BF16)
    value_ref[...] = lax.dot_general(
        w_value_t[...], normed, BY_ROWS, preferred_element_type=F32
    ).astype(BF16)
    peak_ref, total_ref, numer_ref = new
    for pair in range(PAIRS):
        span = slice(2 * HEAD_DIM * pair, 2 * HEAD_DIM * (pair + 1))
        line = slice(pair, pair + 1)
        scores = lax.dot_general(
            key_ref[:, span], query_ref[pair], BY_ROWS, preferred_element_type=F32
        )
        parts = [scores[rows * b : rows * (b + 1)] for b in range(blocks)]
        peak = None if old is None else old[0][line, :]
        for flag, part in zip(flags, parts):
            top = jnp.max(part, axis=0, keepdims=True)
            if flag is not None:
                top = jnp.where(flag, top, -jnp.inf)
            peak = top if peak is None else jnp.maximum(peak, top)
        total = None
        weights = []
        for flag, part in zip(flags, parts):
            shift = peak if flag is None else jnp.where(flag, peak, jnp.inf)
            e = jnp.exp(part - shift)
            weights.append(e.astype(BF16))
            summed = jnp.sum(e, axis=0, keepdims=True)
            total = summed if total is None else total + summed
        weights = jnp.concatenate(weights, axis=0) if blocks > 1 else weights[0]
        numer = jnp.dot(value_ref[span, :], weights, preferred_element_type=F32)
        head_spans = [
            (slice(span.start + HEAD_DIM * j, span.start + HEAD_DIM * (j + 1)), slice(rows * j, rows * (j + 1)))
            for j in range(2)
        ]
        numers = [numer[HEAD_DIM * j : HEAD_DIM * (j + 1), head_spans[j][1]] for j in range(2)]
        if old is not None:
            keep = jnp.exp(old[0][line, :] - peak)
            total = old[1][line, :] * keep + total
            numers = [
                old[2][head, :] * keep[:, lanes] + part for (head, lanes), part in zip(head_spans, numers)
            ]
        peak_ref[line, :] = peak
        total_ref[line, :] = total
        for (head, _), part in zip(head_spans, numers):
            numer_ref[head, :] = part


def finish(total_ref, numer_ref, gain_col, w_out, source, headed_ref):
    rows = source.shape[0]
    for pair in range(PAIRS):
        for j in range(2):
            head = slice((2 * pair + j) * HEAD_DIM, (2 * pair + j + 1) * HEAD_DIM)
            attended = numer_ref[head, :] / total_ref[pair : pair + 1, rows * j : rows * (j + 1)]
            mean_sq = jnp.mean(attended * attended, axis=0, keepdims=True)
            headed_ref[head, :] = (attended * lax.rsqrt(mean_sq + 1e-06) * gain_col[head, :]).astype(BF16)
    update = lax.dot_general(headed_ref[...], w_out[...], BY_COLUMNS, preferred_element_type=F32)
    return (source.astype(F32) + update).astype(BF16)


def join_normed(block_refs, gain_ref):
    parts = [normalize(block[...], gain_ref[...]) for block in block_refs]
    return jnp.concatenate(parts, axis=0) if len(parts) > 1 else parts[0]


def first_kernel(slots, *refs):
    blocks = refs[: len(slots)]
    flags, in_gain, w_query, w_key, w_value_t, query, peak, total, numer, key, value = refs[len(slots) :]
    normed = join_normed(blocks, in_gain)
    project_query(normed[: blocks[0].shape[0]], w_query, query)
    on = [None] + [flags[s] > 0 for s in slots[1:]]
    attend(normed, on, w_key, w_value_t, query, key, value, None, (peak, total, numer))


def later_kernel(slots, *refs):
    blocks = refs[: len(slots)]
    flags, in_gain, w_key, w_value_t, query, peak, total, numer = refs[len(slots) : len(slots) + 8]
    new_peak, new_total, new_numer, key, value = refs[len(slots) + 8 :]
    on = [flags[s] > 0 for s in slots]
    attend(
        join_normed(blocks, in_gain), on, w_key, w_value_t, query, key, value,
        (peak, total, numer), (new_peak, new_total, new_numer),
    )


def last_kernel(slots, *refs):
    blocks = refs[: len(slots)]
    flags, in_gain, w_key, w_value_t, query, peak, total, numer = refs[len(slots) : len(slots) + 8]
    out_gain, w_out, source, out, new_peak, new_total, new_numer, headed, key, value = refs[len(slots) + 8 :]
    on = [flags[s] > 0 for s in slots]
    attend(
        join_normed(blocks, in_gain), on, w_key, w_value_t, query, key, value,
        (peak, total, numer), (new_peak, new_total, new_numer),
    )
    out[...] = finish(new_total, new_numer, out_gain, w_out, source[...], headed)


VMEM = pl.BlockSpec(memory_space=pltpu.VMEM)
SMEM = pl.BlockSpec(memory_space=pltpu.SMEM)


def scratch_for(blocks, rows, width):
    return [pltpu.VMEM((blocks * rows, width), BF16), pltpu.VMEM((width, blocks * rows), BF16)]


def cost_of(blocks, rows, width):
    keys = blocks * rows
    return pl.CostEstimate(
        flops=4 * keys * width * width + 8 * keys * rows * width,
        bytes_accessed=2 * keys * width + 4 * width * width,
        transcendentals=keys * rows * HEADS,
    )


def routes(axis, view_count):
    def swap(mask):
        return lambda block: lax.ppermute(block, axis, [(i, i ^ mask) for i in range(view_count)])

    def shift(step):
        return lambda block: lax.ppermute(
            block, axis, [(i, (i + step) % view_count) for i in range(view_count)]
        )

    masks = (0, 1, 2, 3, 4, 5, 6, 7, 10, 11, 12, 13, 14, 15)
    reached = all(
        any(v ^ mask == (v + d) % view_count for mask in masks)
        for v in range(view_count)
        for d in range(-REACH, REACH + 1)
    )
    if reached and max(masks) < view_count:

        def gather(own):
            got = {0: own}
            got[10] = swap(10)(own)
            got[2] = swap(2)(own)
            got[4] = swap(4)(own)
            got[1] = swap(1)(own)
            got[14] = swap(4)(got[10])
            got[12] = swap(6)(got[10])
            got[6] = swap(2)(got[4])
            for mask in (2, 4, 6, 10, 12, 14):
                got[mask ^ 1] = swap(1)(got[mask])
            return [got[mask] for mask in masks]

        return gather, lambda me: [me ^ mask for mask in masks]

    def gather(own):
        got = [own, swap(1)(own)]
        for step in (2, -2):
            moving = own
            for _ in range((REACH + 1) // 2):
                moving = shift(step)(moving)
                got += [moving, swap(1)(moving)]
        return got

    def owners(me):
        ids = [me, me ^ 1]
        for step in (2, -2):
            for hop in range(1, (REACH + 1) // 2 + 1):
                far = (me - step * hop) % view_count
                ids += [far, far ^ 1]
        return ids

    return gather, owners


CHUNKS = ((0, 1), (2, 3, 4, 5), (6, 7, 8, 9), (10, 11, 12, 13))


def on_device(view_count, tokens, in_gain, w_query, w_key, w_value, w_out, out_gain, covis_list, covis_count):
    source = tokens[0]
    rows, width = source.shape
    own_view = lax.axis_index("views")
    gather, owners = routes("views", view_count)
    blocks = gather(source)
    ids = jnp.stack(owners(own_view)).astype(jnp.int32)
    valid = jnp.arange(covis_list.shape[1], dtype=jnp.int32) < covis_count[0]
    flags = jnp.any((covis_list[0][None, :] == ids[:, None]) & valid[None, :], axis=1).astype(jnp.int32)
    gain_row = in_gain.reshape(1, width)
    gain_col = out_gain.reshape(width, 1)
    w_value_t = w_value.T
    pair_rows = 2 * rows
    state_shapes = [
        jax.ShapeDtypeStruct((PAIRS, pair_rows), F32),
        jax.ShapeDtypeStruct((PAIRS, pair_rows), F32),
        jax.ShapeDtypeStruct((width, rows), F32),
    ]
    state = None
    for index, slots in enumerate(CHUNKS):
        count = len(slots)
        parts = [blocks[s] for s in slots]
        params = pltpu.CompilerParams(vmem_limit_bytes=32 * MIB)
        cost = cost_of(count, rows, width)
        scratch = scratch_for(count, rows, width)
        if index == 0:
            query, *state = pl.pallas_call(
                functools.partial(first_kernel, slots),
                out_shape=[jax.ShapeDtypeStruct((PAIRS, pair_rows, 2 * HEAD_DIM), BF16)] + state_shapes,
                in_specs=[VMEM] * count + [SMEM] + [VMEM] * 4,
                out_specs=[VMEM] * 4,
                scratch_shapes=scratch,
                compiler_params=params,
                cost_estimate=cost,
            )(*parts, flags, gain_row, w_query, w_key, w_value_t)
        elif index < len(CHUNKS) - 1:
            state = pl.pallas_call(
                functools.partial(later_kernel, slots),
                out_shape=state_shapes,
                in_specs=[VMEM] * count + [SMEM] + [VMEM] * 7,
                out_specs=[VMEM] * 3,
                scratch_shapes=scratch,
                compiler_params=params,
                cost_estimate=cost,
            )(*parts, flags, gain_row, w_key, w_value_t, query, *state)
        else:
            mixed = pl.pallas_call(
                functools.partial(last_kernel, slots),
                out_shape=jax.ShapeDtypeStruct((rows, width), BF16),
                in_specs=[VMEM] * count + [SMEM] + [VMEM] * 10,
                out_specs=VMEM,
                scratch_shapes=[pltpu.VMEM(s.shape, s.dtype) for s in state_shapes]
                + [pltpu.VMEM((width, rows), BF16)]
                + scratch,
                compiler_params=params,
                cost_estimate=cost,
            )(*parts, flags, gain_row, w_key, w_value_t, query, *state, gain_col, w_out, source)
    return mixed[None]


def solution(mesh):
    in_specs = (
        P(("groups", "views"), None, None),
        P(),
        P(),
        P(),
        P(),
        P(),
        P(),
        P(("groups", "views"), None),
        P(("groups", "views")),
    )
    out_specs = P(("groups", "views"), None, None)
    return jax.shard_map(
        functools.partial(on_device, mesh.shape["views"]),
        mesh=mesh, in_specs=in_specs, out_specs=out_specs, check_vma=False,
    )
```

time: 157 us -> 61.1 us (0.39)
  local copies, waits for them, and re-layouts: 51 us -> 6.42 us
  matrix products: 40.8 us -> 0 us
  other arithmetic: 27.5 us -> 0.85 us
  Pallas kernels: 0 us -> 26.4 us
  starting transfers between devices: 34.4 us -> 15.9 us
  waiting for transfers between devices: 0.06 us -> 9.84 us
    ppermute x24 -> x0, local copies, waits for them, and re-layouts: 41.7 us -> none  [from_behind(): return lax.ppermute(block, axis, route)]
    dot_general x30 -> x0, matrix products: 40.8 us -> none  [the longest x13 27.2 us: attend_block(): jnp.einsum('qhd,khd->qhk', query3, key3, preferred_element_type=jnp.float32)]
    pallas_call x0 -> x4, Pallas kernels: none -> 26.4 us  [the longest x2 13.6 us: on_device(): pl.pallas_call(functools.partial(later_kernel, slots), out_shape=state_sh...]
    ppermute x24 -> x13, starting transfers between devices: 34.4 us -> 15.9 us  [swap(): lax.ppermute(block, axis, [(i, i ^ mask) for i in range(view_count)])]
    reduce_sum x8 -> x0, other arithmetic: 11.1 us -> none  [the longest x7 9.91 us: attend_block(): total = jnp.sum(weights, axis=-1)]
    ppermute x24 -> x13, waiting for transfers between devices: 0.06 us -> 9.84 us  [swap(): lax.ppermute(block, axis, [(i, i ^ mask) for i in range(view_count)])]
    add x1 -> x0, other arithmetic: 8.35 us -> none  [combine(): total = total * keep_old + other_total * keep_new]
    max x1 -> x0, other arithmetic: 6.86 us -> none  [combine(): newest = jnp.maximum(peak, other_peak)]
  transfers between devices with their start and end apart: 24 -> 13, of which waited for: 0 -> 2; matrix products, arithmetic and copies ran while one was open for 69% -> 7% of each run, Pallas kernels for 0% -> 30%
where the time goes in v1:
time: 61.1 us; the launch traced here: 60.2 us
  Pallas kernels  26.4 us (43%)
  starting transfers between devices  15.9 us (26%)
  waiting for transfers between devices  9.84 us (16%)
  local copies, waits for them, and re-layouts  6.42 us (11%)
  other arithmetic  0.85 us (1%)
  between operations  0.83 us (1%)
    ppermute x13, starting transfers between devices, swap(): lax.ppermute(block, axis, [(i, i ^ mask) for i in range(view_count)])  15.9 us
    pallas_call x2, Pallas kernels, on_device(): pl.pallas_call(functools.partial(later_kernel, slots), out_shape=state_sh...  13.6 us
    ppermute x13, waiting for transfers between devices, swap(): lax.ppermute(block, axis, [(i, i ^ mask) for i in range(view_count)])  9.84 us
    pallas_call x1, Pallas kernels, on_device(): pl.pallas_call(functools.partial(last_kernel, slots), out_shape=jax.Shape...  8.26 us
    unnamed x15, local copies, waits for them, and re-layouts  6.11 us
    pallas_call x1, Pallas kernels, on_device(): pl.pallas_call(functools.partial(first_kernel, slots), out_shape=[jax.Sha...  4.49 us
  transfers between devices with their start and end apart: 13, of which 2 were waited for; matrix products, arithmetic and copies ran while one was open for 7% of the time, Pallas kernels for 30%

profile of v1, /device:TPU:1, one launch (start us, length us, event | category | flops | bytes accessed | tf_op | source)
XLA Modules:
  0.0 60.2 jit_solution(11136186564540471439)
XLA Ops:
  0.0 2.1 %collective-permute-start.6 = (bf16[128,1024]{1,0:T(8,128)(2,1)}, bf16[128,1024]{1,0:T(8,128)(2,1)}, u32[]{:S(2)}, u32[]{:S(2)}) collective-permute-start(bf16[128,1024]{1,0:T(8,128)(2,1)} %bitcast.26), channel_id=1, source_target_pairs={{0,4},{1,5},{2,6},{3,7},{4,0},{5,1},{6,2},{7,3},{8,12},{9,13},{10,... | collective-permute-start | bytes 786440 | tf_op jit(solution)/shard_map/ppermute | solution.py:155
  2.1 3.3 %collective-permute-start = (bf16[128,1024]{1,0:T(8,128)(2,1)}, bf16[128,1024]{1,0:T(8,128)(2,1)S(1)}, u32[]{:S(2)}, u32[]{:S(2)}) collective-permute-start(bf16[128,1024]{1,0:T(8,128)(2,1)} %bitcast.27), channel_id=1, source_target_pairs={{0,10},{1,11},{2,8},{3,9},{4,14},{5,15},{6,12},{7,13},{8,2},{9,3},... | collective-permute-start | bytes 786440 | tf_op jit(solution)/shard_map/ppermute | solution.py:155
  5.4 1.2 %collective-permute-start.5 = (bf16[128,1024]{1,0:T(8,128)(2,1)}, bf16[128,1024]{1,0:T(8,128)(2,1)S(1)}, u32[]{:S(2)}, u32[]{:S(2)}) collective-permute-start(bf16[128,1024]{1,0:T(8,128)(2,1)} %bitcast.28), channel_id=1, source_target_pairs={{0,1},{1,0},{2,3},{3,2},{4,5},{5,4},{6,7},{7,6},{8,9},{9,8},{10,11... | collective-permute-start | bytes 786440 | tf_op jit(solution)/shard_map/ppermute | solution.py:155
  6.6 0.2 collective-permute-start.10
  6.9 6.2 %collective-permute-done.6.refs_2_ = bf16[128,1024]{1,0:T(8,128)(2,1)} collective-permute-done((bf16[128,1024]{1,0:T(8,128)(2,1)}, bf16[128,1024]{1,0:T(8,128)(2,1)}, u32[]{:S(2)}, u32[]{:S(2)}) %collective-permute-start.6) | collective-permute-done | bytes 262176 | tf_op jit(solution)/shard_map/ppermute | solution.py:155
  13.0 1.2 %collective-permute-start.12 = (bf16[128,1024]{1,0:T(8,128)(2,1)}, bf16[128,1024]{1,0:T(8,128)(2,1)}, u32[]{:S(2)}, u32[]{:S(2)}) collective-permute-start(bf16[128,1024]{1,0:T(8,128)(2,1)} %collective-permute-done.6.refs_2_), channel_id=1, source_target_pairs={{0,1},{1,0},{2,3},{3,2},{4,5},{5,4},{6,7},{7,6},{8,9},{9,8},{10,11... | collective-permute-start | bytes 786440 | tf_op jit(solution)/shard_map/ppermute | solution.py:155
  14.2 2.4 %collective-permute-start.7 = (bf16[128,1024]{1,0:T(8,128)(2,1)}, bf16[128,1024]{1,0:T(8,128)(2,1)}, u32[]{:S(2)}, u32[]{:S(2)}) collective-permute-start(bf16[128,1024]{1,0:T(8,128)(2,1)} %collective-permute-done.6.refs_2_), channel_id=1, source_target_pairs={{0,2},{1,3},{2,0},{3,1},{4,6},{5,7},{6,4},{7,5},{8,10},{9,11},{10,... | collective-permute-start | bytes 786440 | tf_op jit(solution)/shard_map/ppermute | solution.py:155
  17.3 0.0 collective-permute-done.refs_2_
  17.3 0.1 collective-permute-start.1
  17.4 0.0 collective-permute-done.5.refs_1_
  17.4 1.2 %collective-permute-start.3 = (bf16[128,1024]{1,0:T(8,128)(2,1)S(1)}, bf16[128,1024]{1,0:T(8,128)(2,1)}, u32[]{:S(2)}, u32[]{:S(2)}) collective-permute-start(bf16[128,1024]{1,0:T(8,128)(2,1)S(1)} %collective-permute-done.refs_2_), channel_id=1, source_target_pairs={{0,4},{1,5},{2,6},{3,7},{4,0},{5,1},{6,2},{7,3},{8,12},{9,13},{10,... | collective-permute-start | bytes 786440 | tf_op jit(solution)/shard_map/ppermute | solution.py:155
  18.5 0.0 collective-permute-done.10.refs_0_
  18.6 3.0 %collective-permute-start.11 = (bf16[128,1024]{1,0:T(8,128)(2,1)}, bf16[128,1024]{1,0:T(8,128)(2,1)}, u32[]{:S(2)}, u32[]{:S(2)}) collective-permute-start(bf16[128,1024]{1,0:T(8,128)(2,1)} %collective-permute-done.10.refs_0_), channel_id=1, source_target_pairs={{0,1},{1,0},{2,3},{3,2},{4,5},{5,4},{6,7},{7,6},{8,9},{9,8},{10,11... | collective-permute-start | bytes 786440 | tf_op jit(solution)/shard_map/ppermute | solution.py:155
  21.6 0.1 stack.59
  21.7 0.8 %and_reduce_fusion = pred[14]{0:T(512)(128)(4,1)S(1)} fusion(s32[12]{0:T(128)} %bitcast.37, s32[14]{0:T(128)S(1)} %stack.59, pred[12]{0:T(512)(128)(4,1)S(1)} %iota_compare_fusion), kind=kLoop, calls=%fused_computation | loop fusion | flops 490 | bytes 130 | tf_op jit(solution)/shard_map/reduce_or | solution.py:216
  22.5 0.0 copy-start.6
  22.5 0.0 copy-start.3
  22.5 0.0 copy-start.4
  22.5 2.9 %copy.13 = bf16[1024,1024]{0,1:T(8,128)(2,1)S(1)} copy(bf16[1024,1024]{1,0:T(8,128)(2,1)} %param.13) | data formatting | bytes 4194304 | tf_op args[4]
  25.5 0.0 copy-done.6
  25.5 0.2 copy.14.refs_12_
  25.7 0.0 collective-permute-done.12.refs_3_
  25.7 0.1 collective-permute-start.9
  25.8 3.6 %collective-permute-done.7.refs_0_ = bf16[128,1024]{1,0:T(8,128)(2,1)} collective-permute-done((bf16[128,1024]{1,0:T(8,128)(2,1)}, bf16[128,1024]{1,0:T(8,128)(2,1)}, u32[]{:S(2)}, u32[]{:S(2)}) %collective-permute-start.7) | collective-permute-done | bytes 262176 | tf_op jit(solution)/shard_map/ppermute | solution.py:155
  29.4 0.5 collective-permute-start.8
  30.0 0.0 copy-done.3
  30.0 0.0 copy-done.4
  30.0 0.0 copy-start
  30.0 1.6 %copy-done = bf16[1024,1024]{1,0:T(8,128)(2,1)S(1)} copy-done((bf16[1024,1024]{1,0:T(8,128)(2,1)S(1)}, bf16[1024,1024]{1,0:T(8,128)(2,1)}, u32[]{:S(2)}) %copy-start) | copy-done | bytes 2097176
  31.6 0.0 copy-start.1
  31.6 1.6 %copy-done.1 = bf16[1024,1024]{1,0:T(8,128)(2,1)S(1)} copy-done((bf16[1024,1024]{1,0:T(8,128)(2,1)S(1)}, bf16[1024,1024]{1,0:T(8,128)(2,1)}, u32[]{:S(2)}) %copy-start.1) | copy-done | bytes 2097176
  33.1 0.0 copy-start.2
  33.1 4.5 %shard_map.91 = (bf16[8,256,128]{2,1,0:T(8,128)(2,1)S(1)}, f32[8,256]{1,0:T(8,128)S(1)}, f32[8,256]{1,0:T(8,128)S(1)}, f32[1024,128]{1,0:T(8,128)S(1)}) custom-call(bf16[128,1024]{1,0:T(8,128)(2,1)S(1)} %bitcast.30, bf16[128,1024]{1,0:T(8,128)(2,1)S(1)} %collective-permute-done.5.refs_1_, s32[14]{0:T(128)S(1)} %convert_element_type.3.refs_2_.refs_4_, ...), custom_call_target="tpu_custom_call" | custom-call | flops 1342177280 | bytes 4718592 | tf_op jit(solution)/shard_map/pallas_call | solution.py:234
  37.6 0.0 collective-permute-done.1.refs_0_
  37.6 0.1 collective-permute-start.2
  37.7 0.0 collective-permute-done.3.refs_2_
  37.7 0.5 collective-permute-start.4
  38.2 0.0 collective-permute-done.11.refs_1_
  38.2 0.0 copy-done.2
  38.2 6.9 %shard_map.92 = (f32[8,256]{1,0:T(8,128)S(1)}, f32[8,256]{1,0:T(8,128)S(1)}, f32[1024,128]{1,0:T(8,128)S(1)}) custom-call(bf16[128,1024]{1,0:T(8,128)(2,1)} %collective-permute-done.10.refs_0_, bf16[128,1024]{1,0:T(8,128)(2,1)} %collective-permute-done.11.refs_1_, bf16[128,1024]{1,0:T(8,128)(2,1)} %collective-permute-done.6.refs_2_, ...), custom_call_target="tpu_custom_call" | custom-call | flops 2684354560 | bytes 5242880 | tf_op jit(solution)/shard_map/pallas_call | solution.py:244
  45.1 0.0 collective-permute-done.9.refs_3_
  45.1 0.0 collective-permute-done.8.refs_1_
  45.1 0.0 copy-start.5
  45.1 6.8 %shard_map.93 = (f32[8,256]{1,0:T(8,128)S(1)}, f32[8,256]{1,0:T(8,128)S(1)}, f32[1024,128]{1,0:T(8,128)S(1)}) custom-call(bf16[128,1024]{1,0:T(8,128)(2,1)} %collective-permute-done.7.refs_0_, bf16[128,1024]{1,0:T(8,128)(2,1)S(1)} %collective-permute-done.8.refs_1_, bf16[128,1024]{1,0:T(8,128)(2,1)S(1)} %collective-permute-done.refs_2_, ...), custom_call_target="tpu_custom_call" | custom-call | flops 2684354560 | bytes 5242880 | tf_op jit(solution)/shard_map/pallas_call | solution.py:244
  51.9 0.0 collective-permute-done.2.refs_1_
  51.9 0.0 collective-permute-done.4.refs_3_
  51.9 0.0 copy-done.5
  51.9 8.3 %shard_map.94 = bf16[128,1024]{1,0:T(8,128)(2,1)} custom-call(bf16[128,1024]{1,0:T(8,128)(2,1)} %collective-permute-done.1.refs_0_, bf16[128,1024]{1,0:T(8,128)(2,1)S(1)} %collective-permute-done.2.refs_1_, bf16[128,1024]{1,0:T(8,128)(2,1)} %collective-permute-done.3.refs_2_, bf16[128,1024]{1,0:T(8,128)(2,1)S(1)} %collective-permute-done.4.refs_3_, ...), custom_call_target="tpu_custom_call" | custom-call | flops 2684354560 | bytes 5242880 | tf_op jit(solution)/shard_map/pallas_call | solution.py:254
  (2 shorter events, 0.0 us)
Async XLA Ops:
  0.0 13.0 %collective-permute-start.6 = (bf16[128,1024]{1,0:T(8,128)(2,1)}, bf16[128,1024]{1,0:T(8,128)(2,1)}, u32[]{:S(2)}, u32[]{:S(2)}) collective-permute-start(bf16[128,1024]{1,0:T(8,128)(2,1)} %bitcast.26), channel_id=1, source_target_pairs={{0,4},{1,5},{2,6},{3,7},{4,0},{5,1},{6,2},{7,3},{8,12},{9,13},{10,... | collective-permute-start | bytes 786440 | tf_op jit(solution)/shard_map/ppermute | solution.py:155
  2.1 15.2 %collective-permute-start = (bf16[128,1024]{1,0:T(8,128)(2,1)}, bf16[128,1024]{1,0:T(8,128)(2,1)S(1)}, u32[]{:S(2)}, u32[]{:S(2)}) collective-permute-start(bf16[128,1024]{1,0:T(8,128)(2,1)} %bitcast.27), channel_id=1, source_target_pairs={{0,10},{1,11},{2,8},{3,9},{4,14},{5,15},{6,12},{7,13},{8,2},{9,3},... | collective-permute-start | bytes 786440 | tf_op jit(solution)/shard_map/ppermute | solution.py:155
  5.4 12.0 %collective-permute-start.5 = (bf16[128,1024]{1,0:T(8,128)(2,1)}, bf16[128,1024]{1,0:T(8,128)(2,1)S(1)}, u32[]{:S(2)}, u32[]{:S(2)}) collective-permute-start(bf16[128,1024]{1,0:T(8,128)(2,1)} %bitcast.28), channel_id=1, source_target_pairs={{0,1},{1,0},{2,3},{3,2},{4,5},{5,4},{6,7},{7,6},{8,9},{9,8},{10,11... | collective-permute-start | bytes 786440 | tf_op jit(solution)/shard_map/ppermute | solution.py:155
  6.6 11.9 %collective-permute-start.10 = (bf16[128,1024]{1,0:T(8,128)(2,1)}, bf16[128,1024]{1,0:T(8,128)(2,1)}, u32[]{:S(2)}, u32[]{:S(2)}) collective-permute-start(bf16[128,1024]{1,0:T(8,128)(2,1)} %bitcast.29), channel_id=1, source_target_pairs={{0,2},{1,3},{2,0},{3,1},{4,6},{5,7},{6,4},{7,5},{8,10},{9,11},{10,... | collective-permute-start | bytes 786440 | tf_op jit(solution)/shard_map/ppermute | solution.py:155
  13.0 12.7 %collective-permute-start.12 = (bf16[128,1024]{1,0:T(8,128)(2,1)}, bf16[128,1024]{1,0:T(8,128)(2,1)}, u32[]{:S(2)}, u32[]{:S(2)}) collective-permute-start(bf16[128,1024]{1,0:T(8,128)(2,1)} %collective-permute-done.6.refs_2_), channel_id=1, source_target_pairs={{0,1},{1,0},{2,3},{3,2},{4,5},{5,4},{6,7},{7,6},{8,9},{9,8},{10,11... | collective-permute-start | bytes 786440 | tf_op jit(solution)/shard_map/ppermute | solution.py:155
  14.2 15.2 %collective-permute-start.7 = (bf16[128,1024]{1,0:T(8,128)(2,1)}, bf16[128,1024]{1,0:T(8,128)(2,1)}, u32[]{:S(2)}, u32[]{:S(2)}) collective-permute-start(bf16[128,1024]{1,0:T(8,128)(2,1)} %collective-permute-done.6.refs_2_), channel_id=1, source_target_pairs={{0,2},{1,3},{2,0},{3,1},{4,6},{5,7},{6,4},{7,5},{8,10},{9,11},{10,... | collective-permute-start | bytes 786440 | tf_op jit(solution)/shard_map/ppermute | solution.py:155
  17.3 20.3 %collective-permute-start.1 = (bf16[128,1024]{1,0:T(8,128)(2,1)S(1)}, bf16[128,1024]{1,0:T(8,128)(2,1)}, u32[]{:S(2)}, u32[]{:S(2)}) collective-permute-start(bf16[128,1024]{1,0:T(8,128)(2,1)S(1)} %collective-permute-done.refs_2_), channel_id=1, source_target_pairs={{0,6},{1,7},{2,4},{3,5},{4,2},{5,3},{6,0},{7,1},{8,14},{9,15},{10,... | collective-permute-start | bytes 786440 | tf_op jit(solution)/shard_map/ppermute | solution.py:155
  17.4 20.3 %collective-permute-start.3 = (bf16[128,1024]{1,0:T(8,128)(2,1)S(1)}, bf16[128,1024]{1,0:T(8,128)(2,1)}, u32[]{:S(2)}, u32[]{:S(2)}) collective-permute-start(bf16[128,1024]{1,0:T(8,128)(2,1)S(1)} %collective-permute-done.refs_2_), channel_id=1, source_target_pairs={{0,4},{1,5},{2,6},{3,7},{4,0},{5,1},{6,2},{7,3},{8,12},{9,13},{10,... | collective-permute-start | bytes 786440 | tf_op jit(solution)/shard_map/ppermute | solution.py:155
  18.6 19.7 %collective-permute-start.11 = (bf16[128,1024]{1,0:T(8,128)(2,1)}, bf16[128,1024]{1,0:T(8,128)(2,1)}, u32[]{:S(2)}, u32[]{:S(2)}) collective-permute-start(bf16[128,1024]{1,0:T(8,128)(2,1)} %collective-permute-done.10.refs_0_), channel_id=1, source_target_pairs={{0,1},{1,0},{2,3},{3,2},{4,5},{5,4},{6,7},{7,6},{8,9},{9,8},{10,11... | collective-permute-start | bytes 786440 | tf_op jit(solution)/shard_map/ppermute | solution.py:155
  22.5 2.9 %copy-start.6 = (f32[1024]{0:T(1024)S(1)}, f32[1024]{0:T(1024)}, u32[]{:S(2)}) copy-start(f32[1024]{0:T(1024)} %param.15) | copy-start | bytes 12292
  22.5 7.4 %copy-start.3 = (bf16[1,128,1024]{2,1,0:T(8,128)(2,1)S(1)}, bf16[1,128,1024]{2,1,0:T(8,128)(2,1)}, u32[]{:S(2)}) copy-start(bf16[1,128,1024]{2,1,0:T(8,128)(2,1)} %param.9) | copy-start | bytes 786436
  22.5 7.4 %copy-start.4 = (f32[1024]{0:T(1024)S(1)}, f32[1024]{0:T(1024)}, u32[]{:S(2)}) copy-start(f32[1024]{0:T(1024)} %param.10) | copy-start | bytes 12292
  25.7 19.4 %collective-permute-start.9 = (bf16[128,1024]{1,0:T(8,128)(2,1)S(1)}, bf16[128,1024]{1,0:T(8,128)(2,1)S(1)}, u32[]{:S(2)}, u32[]{:S(2)}) collective-permute-start(bf16[128,1024]{1,0:T(8,128)(2,1)S(1)} %collective-permute-done.refs_2_), channel_id=1, source_target_pairs={{0,1},{1,0},{2,3},{3,2},{4,5},{5,4},{6,7},{7,6},{8,9},{9,8},{10,11... | collective-permute-start | bytes 786440 | tf_op jit(solution)/shard_map/ppermute | solution.py:155
  29.4 15.7 %collective-permute-start.8 = (bf16[128,1024]{1,0:T(8,128)(2,1)}, bf16[128,1024]{1,0:T(8,128)(2,1)S(1)}, u32[]{:S(2)}, u32[]{:S(2)}) collective-permute-start(bf16[128,1024]{1,0:T(8,128)(2,1)} %collective-permute-done.7.refs_0_), channel_id=1, source_target_pairs={{0,1},{1,0},{2,3},{3,2},{4,5},{5,4},{6,7},{7,6},{8,9},{9,8},{10,11... | collective-permute-start | bytes 786440 | tf_op jit(solution)/shard_map/ppermute | solution.py:155
  30.0 1.6 %copy-start = (bf16[1024,1024]{1,0:T(8,128)(2,1)S(1)}, bf16[1024,1024]{1,0:T(8,128)(2,1)}, u32[]{:S(2)}) copy-start(bf16[1024,1024]{1,0:T(8,128)(2,1)} %refs_4_.1) | copy-start | bytes 6291460
  31.6 1.6 %copy-start.1 = (bf16[1024,1024]{1,0:T(8,128)(2,1)S(1)}, bf16[1024,1024]{1,0:T(8,128)(2,1)}, u32[]{:S(2)}) copy-start(bf16[1024,1024]{1,0:T(8,128)(2,1)} %refs_6_.5) | copy-start | bytes 6291460
  33.1 5.1 %copy-start.2 = (bf16[1024,1024]{1,0:T(8,128)(2,1)S(1)}, bf16[1024,1024]{1,0:T(8,128)(2,1)}, u32[]{:S(2)}) copy-start(bf16[1024,1024]{1,0:T(8,128)(2,1)} %refs_6_.5) | copy-start | bytes 6291460
  37.6 14.3 %collective-permute-start.2 = (bf16[128,1024]{1,0:T(8,128)(2,1)}, bf16[128,1024]{1,0:T(8,128)(2,1)S(1)}, u32[]{:S(2)}, u32[]{:S(2)}) collective-permute-start(bf16[128,1024]{1,0:T(8,128)(2,1)} %collective-permute-done.1.refs_0_), channel_id=1, source_target_pairs={{0,1},{1,0},{2,3},{3,2},{4,5},{5,4},{6,7},{7,6},{8,9},{9,8},{10,11... | collective-permute-start | bytes 786440 | tf_op jit(solution)/shard_map/ppermute | solution.py:155
  37.7 14.2 %collective-permute-start.4 = (bf16[128,1024]{1,0:T(8,128)(2,1)}, bf16[128,1024]{1,0:T(8,128)(2,1)S(1)}, u32[]{:S(2)}, u32[]{:S(2)}) collective-permute-start(bf16[128,1024]{1,0:T(8,128)(2,1)} %collective-permute-done.3.refs_2_), channel_id=1, source_target_pairs={{0,1},{1,0},{2,3},{3,2},{4,5},{5,4},{6,7},{7,6},{8,9},{9,8},{10,11... | collective-permute-start | bytes 786440 | tf_op jit(solution)/shard_map/ppermute | solution.py:155
  45.1 6.8 %copy-start.5 = (bf16[1024,1024]{1,0:T(8,128)(2,1)S(1)}, bf16[1024,1024]{1,0:T(8,128)(2,1)}, u32[]{:S(2)}) copy-start(bf16[1024,1024]{1,0:T(8,128)(2,1)} %refs_13_.1) | copy-start | bytes 6291460

commit v2 on v1

v2 whole, which is shorter than its diff:
```python
import functools

import jax
import jax.numpy as jnp
from jax import lax
from jax.experimental import pallas as pl
from jax.experimental.pallas import tpu as pltpu
from jax.sharding import PartitionSpec as P

HEADS = 16
HEAD_DIM = 64
REACH = 6
PAIRS = HEADS // 2
F32 = jnp.float32
BF16 = jnp.bfloat16
BY_ROWS = (((1,), (1,)), ((), ()))
BY_COLUMNS = (((0,), (0,)), ((), ()))
MIB = 1024 * 1024


def normalize(block, gain):
    values = block.astype(F32)
    mean_sq = jnp.mean(values * values, axis=-1, keepdims=True)
    return (values * lax.rsqrt(mean_sq + 1e-06) * gain).astype(BF16)


def project_query(normed, w_query, query_ref):
    query = jnp.dot(normed, w_query[...], preferred_element_type=F32).astype(BF16)
    query = query * jnp.asarray(HEAD_DIM**-0.5, BF16)
    rows = query.shape[0]
    lane = lax.broadcasted_iota(jnp.int32, (rows, 2 * HEAD_DIM), 1)
    for pair in range(PAIRS):
        both = query[:, 2 * HEAD_DIM * pair : 2 * HEAD_DIM * (pair + 1)]
        zero = jnp.zeros_like(both)
        query_ref[pair, :rows, :] = jnp.where(lane < HEAD_DIM, both, zero)
        query_ref[pair, rows:, :] = jnp.where(lane >= HEAD_DIM, both, zero)


def attend(normed, flags, w_key, w_value_t, query_ref, key_ref, value_ref, old, new):
    blocks = len(flags)
    rows = normed.shape[0] // blocks
    peak_ref, total_ref, numer_ref = new

    def span_of(pair):
        return slice(2 * HEAD_DIM * pair, 2 * HEAD_DIM * (pair + 1))

    def scores_of(pair):
        return lax.dot_general(
            key_ref[:, span_of(pair)], query_ref[pair], BY_ROWS, preferred_element_type=F32
        )

    def soften(pair, scores):
        line = slice(pair, pair + 1)
        parts = [scores[rows * b : rows * (b + 1)] for b in range(blocks)]
        peak = None if old is None else old[0][line, :]
        for flag, part in zip(flags, parts):
            top = jnp.max(part, axis=0, keepdims=True)
            if flag is not None:
                top = jnp.where(flag, top, -jnp.inf)
            peak = top if peak is None else jnp.maximum(peak, top)
        total = None
        weights = []
        for flag, part in zip(flags, parts):
            shift = peak if flag is None else jnp.where(flag, peak, jnp.inf)
            e = jnp.exp(part - shift)
            weights.append(e.astype(BF16))
            summed = jnp.sum(e, axis=0, keepdims=True)
            total = summed if total is None else total + summed
        keep = None
        if old is not None:
            keep = jnp.exp(old[0][line, :] - peak)
            total = old[1][line, :] * keep + total
        peak_ref[line, :] = peak
        total_ref[line, :] = total
        return (jnp.concatenate(weights, axis=0) if blocks > 1 else weights[0]), keep

    def gather_values(pair, weights, keep):
        span = span_of(pair)
        numer = jnp.dot(value_ref[span, :], weights, preferred_element_type=F32)
        for j in range(2):
            head = slice(span.start + HEAD_DIM * j, span.start + HEAD_DIM * (j + 1))
            lanes = slice(rows * j, rows * (j + 1))
            part = numer[HEAD_DIM * j : HEAD_DIM * (j + 1), lanes]
            if keep is not None:
                part = old[2][head, :] * keep[:, lanes] + part
            numer_ref[head, :] = part

    key_ref[...] = jnp.dot(normed, w_key[...], preferred_element_type=F32).astype(BF16)
    scores = scores_of(0)
    value_ref[...] = lax.dot_general(
        w_value_t[...], normed, BY_ROWS, preferred_element_type=F32
    ).astype(BF16)
    held = None
    for pair in range(PAIRS):
        ahead = scores_of(pair + 1) if pair + 1 < PAIRS else None
        if held is not None:
            gather_values(pair - 1, *held)
        held = soften(pair, scores)
        scores = ahead
    gather_values(PAIRS - 1, *held)


def finish(total_ref, numer_ref, gain_col, w_out, source, headed_ref):
    rows = source.shape[0]
    for pair in range(PAIRS):
        for j in range(2):
            head = slice((2 * pair + j) * HEAD_DIM, (2 * pair + j + 1) * HEAD_DIM)
            attended = numer_ref[head, :] / total_ref[pair : pair + 1, rows * j : rows * (j + 1)]
            mean_sq = jnp.mean(attended * attended, axis=0, keepdims=True)
            headed_ref[head, :] = (attended * lax.rsqrt(mean_sq + 1e-06) * gain_col[head, :]).astype(BF16)
    update = lax.dot_general(headed_ref[...], w_out[...], BY_COLUMNS, preferred_element_type=F32)
    return (source.astype(F32) + update).astype(BF16)


def join_normed(block_refs, gain_ref):
    parts = [normalize(block[...], gain_ref[...]) for block in block_refs]
    return jnp.concatenate(parts, axis=0) if len(parts) > 1 else parts[0]


def listed(owners, slots, covis_list, covis_count):
    ids = owners(lax.axis_index("views"))
    count = covis_count[0]
    entries = [jnp.where(i < count, covis_list[0, i], -1) for i in range(covis_list.shape[1])]
    return [functools.reduce(jnp.logical_or, [entry == ids[s] for entry in entries]) for s in slots]


def first_kernel(
    owners, slots, own, other, covis_list, covis_count, in_gain, w_query, w_key, w_value,
    query, peak, total, numer, w_key_here, w_value_t,
    own_here, in_gain_here, w_query_here, w_value_here, key, value, arrived,
):
    copies = [
        pltpu.make_async_copy(source, target, arrived.at[i])
        for i, (source, target) in enumerate(
            (
                (own, own_here),
                (in_gain, in_gain_here),
                (w_query, w_query_here),
                (w_value, w_value_here),
                (w_key, w_key_here),
            )
        )
    ]
    for copy in copies:
        copy.start()
    flags = [None] + listed(owners, slots, covis_list, covis_count)
    copies[0].wait()
    copies[1].wait()
    normed = join_normed((own_here, other), in_gain_here)
    copies[2].wait()
    project_query(normed[: own.shape[0]], w_query_here, query)
    copies[3].wait()
    w_value_t[...] = w_value_here[...].T
    copies[4].wait()
    attend(normed, flags, w_key_here, w_value_t, query, key, value, None, (peak, total, numer))


def later_kernel(slots, owners, *refs):
    blocks = refs[: len(slots)]
    covis_list, covis_count, in_gain, w_key, w_value_t, query, peak, total, numer = refs[len(slots) : len(slots) + 9]
    new_peak, new_total, new_numer, key, value = refs[len(slots) + 9 :]
    attend(
        join_normed(blocks, in_gain), listed(owners, slots, covis_list, covis_count),
        w_key, w_value_t, query, key, value,
        (peak, total, numer), (new_peak, new_total, new_numer),
    )


def last_kernel(slots, owners, *refs):
    blocks = refs[: len(slots)]
    covis_list, covis_count, in_gain, w_key, w_value_t, query, peak, total, numer = refs[len(slots) : len(slots) + 9]
    out_gain, w_out, source, out = refs[len(slots) + 9 : len(slots) + 13]
    new_peak, new_total, new_numer, headed, w_out_here, source_here, arrived, key, value = refs[len(slots) + 13 :]
    copies = [
        pltpu.make_async_copy(w_out, w_out_here, arrived.at[0]),
        pltpu.make_async_copy(source, source_here, arrived.at[1]),
    ]
    for copy in copies:
        copy.start()
    attend(
        join_normed(blocks, in_gain), listed(owners, slots, covis_list, covis_count),
        w_key, w_value_t, query, key, value,
        (peak, total, numer), (new_peak, new_total, new_numer),
    )
    for copy in copies:
        copy.wait()
    out[...] = finish(new_total, new_numer, out_gain, w_out_here, source_here[...], headed)


VMEM = pl.BlockSpec(memory_space=pltpu.VMEM)
SMEM = pl.BlockSpec(memory_space=pltpu.SMEM)
HBM = pl.BlockSpec(memory_space=pltpu.HBM)


def scratch_for(blocks, rows, width):
    return [pltpu.VMEM((blocks * rows, width), BF16), pltpu.VMEM((width, blocks * rows), BF16)]


def in_hbm(array):
    return pltpu.with_memory_space_constraint(array, pltpu.HBM)


def tie(block, *done):
    return lax.optimization_barrier((block, *done))[0]


def routes(axis, view_count):
    def swap(mask):
        return lambda block: lax.ppermute(block, axis, [(i, i ^ mask) for i in range(view_count)])

    def shift(step):
        return lambda block: lax.ppermute(
            block, axis, [(i, (i + step) % view_count) for i in range(view_count)]
        )

    masks = (1, 2, 4, 10, 3, 5, 6, 11, 7, 12, 14, 13, 15)
    reached = all(
        v == (v + d) % view_count or any(v ^ mask == (v + d) % view_count for mask in masks)
        for v in range(view_count)
        for d in range(-REACH, REACH + 1)
    )
    if reached and max(masks) < view_count:

        def first(own):
            return {mask: swap(mask)(own) for mask in (10, 4, 2, 1)}

        def second(got, after):
            got[12] = swap(6)(after(got[10]))
            got[14] = swap(4)(after(got[10]))
            got[6] = swap(2)(after(got[4]))
            for mask in (2, 4):
                got[mask ^ 1] = swap(1)(after(got[mask]))

        def third(got, after):
            for mask in (6, 10):
                got[mask ^ 1] = swap(1)(after(got[mask]))

        def fourth(got, after):
            for mask in (12, 14):
                got[mask ^ 1] = swap(1)(after(got[mask]))

        return first, second, third, fourth, masks, lambda me: {mask: me ^ mask for mask in masks}

    hops = (REACH + 1) // 2
    names = ["partner"] + [(way, hop, side) for hop in range(1, hops + 1) for side in (0, 1) for way in (2, -2)]

    def first(own):
        got = {"partner": swap(1)(own)}
        for way in (2, -2):
            got[way, 1, 0] = shift(way)(own)
        return got

    def second(got, after):
        for way in (2, -2):
            for hop in range(2, hops + 1):
                got[way, hop, 0] = shift(way)(after(got[way, hop - 1, 0]))
            got[way, 1, 1] = swap(1)(after(got[way, 1, 0]))

    def third(got, after):
        for way in (2, -2):
            got[way, 2, 1] = swap(1)(after(got[way, 2, 0]))

    def fourth(got, after):
        for way in (2, -2):
            for hop in range(3, hops + 1):
                got[way, hop, 1] = swap(1)(after(got[way, hop, 0]))

    def owners(me):
        ids = {"partner": me ^ 1}
        for way in (2, -2):
            for hop in range(1, hops + 1):
                far = lax.rem(me - way * hop + view_count, view_count)
                ids[way, hop, 0] = far
                ids[way, hop, 1] = far ^ 1
        return ids

    return first, second, third, fourth, names, owners


def cost_of(blocks, rows, width):
    keys = blocks * rows
    return pl.CostEstimate(
        flops=3 * (4 * keys * width * width + 8 * keys * rows * width),
        bytes_accessed=2 * keys * width,
        transcendentals=keys * rows * HEADS,
    )


def on_device(view_count, tokens, in_gain, w_query, w_key, w_value, w_out, out_gain, covis_list, covis_count):
    source = tokens[0]
    rows, width = source.shape
    first, second, third, fourth, names, owners = routes("views", view_count)
    gain_row = in_gain.reshape(1, width)
    gain_col = out_gain.reshape(width, 1)
    pair_rows = 2 * rows
    state_shapes = [
        pltpu.VMEM((PAIRS, pair_rows), F32),
        pltpu.VMEM((PAIRS, pair_rows), F32),
        pltpu.VMEM((width, rows), F32),
    ]
    params = pltpu.CompilerParams(vmem_limit_bytes=24 * MIB)

    def call_later(got, slots, state, tail=None):
        count = len(slots)
        held = [
            pltpu.with_memory_space_constraint(x, pltpu.VMEM) for x in (w_key_here, w_value_t, query, *state)
        ]
        parts = [got[s] for s in slots] + [covis_list, covis_count, gain_row] + held
        specs = [VMEM] * count + [SMEM] * 2 + [VMEM] * 7
        scratch = scratch_for(count, rows, width)
        if tail is None:
            return pl.pallas_call(
                functools.partial(later_kernel, slots, owners),
                out_shape=state_shapes,
                in_specs=specs,
                out_specs=[VMEM] * 3,
                scratch_shapes=scratch,
                compiler_params=params,
                cost_estimate=cost_of(count, rows, width),
            )(*parts)
        return pl.pallas_call(
            functools.partial(last_kernel, slots, owners),
            out_shape=jax.ShapeDtypeStruct((rows, width), BF16),
            in_specs=specs + [VMEM, HBM, HBM],
            out_specs=VMEM,
            scratch_shapes=state_shapes
            + [pltpu.VMEM((width, rows), BF16), pltpu.VMEM(w_out.shape, BF16)]
            + [pltpu.VMEM(source.shape, BF16), pltpu.SemaphoreType.DMA((2,))]
            + scratch,
            compiler_params=params,
            cost_estimate=cost_of(count, rows, width),
        )(*parts, *tail)

    got = first(source)
    query, *state, w_key_here, w_value_t = pl.pallas_call(
        functools.partial(first_kernel, owners, names[:1]),
        out_shape=[pltpu.VMEM((PAIRS, pair_rows, 2 * HEAD_DIM), BF16)]
        + state_shapes
        + [pltpu.VMEM(w_key.shape, BF16), pltpu.VMEM(w_value.shape, BF16)],
        in_specs=[HBM, VMEM, SMEM, SMEM, HBM, HBM, HBM, HBM],
        out_specs=[VMEM] * 6,
        scratch_shapes=[
            pltpu.VMEM(source.shape, BF16),
            pltpu.VMEM(gain_row.shape, F32),
            pltpu.VMEM(w_query.shape, BF16),
            pltpu.VMEM(w_value.shape, BF16),
        ]
        + scratch_for(2, rows, width)
        + [pltpu.SemaphoreType.DMA((5,))],
        compiler_params=params,
        cost_estimate=cost_of(2, rows, width),
    )(
        in_hbm(source), got[names[0]], covis_list, covis_count,
        *map(in_hbm, (gain_row, w_query, w_key, w_value)),
    )
    mark = state[0]
    second(got, lambda block: tie(block, mark))
    state = call_later(got, names[1:4], state)
    third(got, lambda block: tie(block, state[0]))
    state = call_later(got, names[4:7], state)
    fourth(got, lambda block: tie(block, state[0]))
    state = call_later(got, names[7:11], state)
    return call_later(got, names[11:], state, (gain_col, in_hbm(w_out), in_hbm(source)))[None]


def solution(mesh):
    in_specs = (
        P(("groups", "views"), None, None),
        P(),
        P(),
        P(),
        P(),
        P(),
        P(),
        P(("groups", "views"), None),
        P(("groups", "views")),
    )
    out_specs = P(("groups", "views"), None, None)
    return jax.shard_map(
        functools.partial(on_device, mesh.shape["views"]),
        mesh=mesh, in_specs=in_specs, out_specs=out_specs, check_vma=False,
    )
```

time: 61.1 us -> 47.1 us (0.77)
  waiting for transfers between devices: 9.84 us -> 4.24 us
  local copies, waits for them, and re-layouts: 6.42 us -> 1.56 us
  Pallas kernels: 26.4 us -> 24.3 us
  other arithmetic: 0.85 us -> 0 us
    ppermute x13, waiting for transfers between devices: 9.84 us -> 4.24 us  [swap(): lax.ppermute(block, axis, [(i, i ^ mask) for i in range(view_count)])]
    unnamed x15 -> x4, local copies, waits for them, and re-layouts: 6.11 us -> 0.65 us
    pallas_call x4 -> x5, Pallas kernels: 26.4 us -> 24.3 us  [the longest x3 12.3 us: call_later(): pl.pallas_call(functools.partial(later_kernel, slots, owners), out_shape=...]
    reduce_or x1 -> x0, other arithmetic: 0.84 us -> none  [on_device(): jnp.any((covis_list[0][None, :] == ids[:, None]) & valid[None, :], axis=1)]
    reshape x1, local copies, waits for them, and re-layouts: 0.22 us -> 0.9 us  [on_device(): gain_col = out_gain.reshape(width, 1)]
  transfers between devices with their start and end apart: 13 -> 13, of which waited for: 2 -> 2; matrix products, arithmetic and copies ran while one was open for 7% -> 2% of each run, Pallas kernels for 30% -> 39%
where the time goes in v2:
time: 47.1 us; the launch traced here: 46.6 us
  Pallas kernels  24.3 us (52%)
  starting transfers between devices  15.6 us (33%)
  waiting for transfers between devices  4.24 us (9%)
  local copies, waits for them, and re-layouts  1.56 us (3%)
  between operations  0.9 us (2%)
    ppermute x13, starting transfers between devices, swap(): lax.ppermute(block, axis, [(i, i ^ mask) for i in range(view_count)])  15.6 us
    pallas_call x3, Pallas kernels, call_later(): pl.pallas_call(functools.partial(later_kernel, slots, owners), out_shape=...  12.3 us
    pallas_call x1, Pallas kernels, call_later(): pl.pallas_call(functools.partial(last_kernel, slots, owners), out_shape=j...  6.1 us
    pallas_call x1, Pallas kernels, on_device(): pl.pallas_call(functools.partial(first_kernel, owners, names[:1]), out_sh...  5.84 us
    ppermute x13, waiting for transfers between devices, swap(): lax.ppermute(block, axis, [(i, i ^ mask) for i in range(view_count)])  4.24 us
  transfers between devices with their start and end apart: 13, of which 2 were waited for; matrix products, arithmetic and copies ran while one was open for 2% of the time, Pallas kernels for 39%

profile of v2, /device:TPU:1, one launch (start us, length us, event | category | flops | bytes accessed | tf_op | source)
XLA Modules:
  0.0 46.6 jit_solution(4820147996985185932)
XLA Ops:
  0.0 0.1 collective-permute-start.1
  0.1 4.7 %collective-permute-start = (bf16[128,1024]{1,0:T(8,128)(2,1)}, bf16[128,1024]{1,0:T(8,128)(2,1)S(1)}, u32[]{:S(2)}, u32[]{:S(2)}) collective-permute-start(bf16[128,1024]{1,0:T(8,128)(2,1)} %bitcast.11), channel_id=1, source_target_pairs={{0,10},{1,11},{2,8},{3,9},{4,14},{5,15},{6,12},{7,13},{8,2},{9,3},... | collective-permute-start | bytes 786440 | tf_op jit(solution)/shard_map/ppermute | solution.py:209
  4.8 0.2 collective-permute-start.3
  5.0 1.3 %collective-permute-start.5 = (bf16[128,1024]{1,0:T(8,128)(2,1)}, bf16[128,1024]{1,0:T(8,128)(2,1)S(1)}, u32[]{:S(2)}, u32[]{:S(2)}) collective-permute-start(bf16[128,1024]{1,0:T(8,128)(2,1)} %bitcast.13), channel_id=1, source_target_pairs={{0,4},{1,5},{2,6},{3,7},{4,0},{5,1},{6,2},{7,3},{8,12},{9,13},{10,... | collective-permute-start | bytes 786440 | tf_op jit(solution)/shard_map/ppermute | solution.py:209
  6.9 0.9 %copy.10.refs_11_ = f32[1024,1]{1,0:T(8,128)S(1)} copy(f32[1024,1]{0,1:T(1,128)} %bitcast.9) | data formatting | bytes 8192 | tf_op jit(solution)/shard_map/reshape | solution.py:294
  7.9 0.0 collective-permute-done.1.other
  7.9 0.0 copy-start.1
  7.9 0.6 %copy-done.1 = s32[1,12]{1,0:T(1,128)S(1)} copy-done((s32[1,12]{1,0:T(1,128)S(1)}, s32[1,12]{1,0:T(1,128)}, u32[]{:S(2)}) %copy-start.1) | copy-done | bytes 72
  8.5 0.0 copy-start
  8.5 5.8 %shard_map.91 = (bf16[8,256,128]{2,1,0:T(8,128)(2,1)S(1)}, f32[8,256]{1,0:T(8,128)S(1)}, f32[8,256]{1,0:T(8,128)S(1)}, f32[1024,128]{1,0:T(8,128)S(1)}, bf16[102...) custom-call(bf16[128,1024]{1,0:T(8,128)(2,1)} %bitcast.14, bf16[128,1024]{1,0:T(8,128)(2,1)S(1)} %collective-permute-done.1.other, ...), custom_call_target="tpu_custom_call" | custom-call | flops 4026531840 | bytes 524288 | tf_op jit(solution)/shard_map/pallas_call | solution.py:335
  14.4 2.1 %collective-permute-done.5.refs_1_ = bf16[128,1024]{1,0:T(8,128)(2,1)S(1)} collective-permute-done((bf16[128,1024]{1,0:T(8,128)(2,1)}, bf16[128,1024]{1,0:T(8,128)(2,1)S(1)}, u32[]{:S(2)}, u32[]{:S(2)}) %collective-permute-start.5) | collective-permute-done | bytes 262176 | tf_op jit(solution)/shard_map/ppermute | solution.py:209
  16.5 1.8 %collective-permute-start.7 = (bf16[128,1024]{1,0:T(8,128)(2,1)S(1)}, bf16[128,1024]{1,0:T(8,128)(2,1)S(1)}, u32[]{:S(2)}, u32[]{:S(2)}) collective-permute-start(bf16[128,1024]{1,0:T(8,128)(2,1)S(1)} %collective-permute-done.5.refs_1_), channel_id=1, source_target_pairs={{0,2},{1,3},{2,0},{3,1},{4,6},{5,7},{6,4},{7,5},{8,10},{9,11},{10,... | collective-permute-start | bytes 786440 | tf_op jit(solution)/shard_map/ppermute | solution.py:209
  18.3 1.7 %collective-permute-start.6 = (bf16[128,1024]{1,0:T(8,128)(2,1)S(1)}, bf16[128,1024]{1,0:T(8,128)(2,1)S(1)}, u32[]{:S(2)}, u32[]{:S(2)}) collective-permute-start(bf16[128,1024]{1,0:T(8,128)(2,1)S(1)} %collective-permute-done.5.refs_1_), channel_id=1, source_target_pairs={{0,1},{1,0},{2,3},{3,2},{4,5},{5,4},{6,7},{7,6},{8,9},{9,8},{10,11... | collective-permute-start | bytes 786440 | tf_op jit(solution)/shard_map/ppermute | solution.py:209
  20.0 0.0 collective-permute-done.refs_2_
  20.0 0.9 %collective-permute-start.2 = (bf16[128,1024]{1,0:T(8,128)(2,1)S(1)}, bf16[128,1024]{1,0:T(8,128)(2,1)S(1)}, u32[]{:S(2)}, u32[]{:S(2)}) collective-permute-start(bf16[128,1024]{1,0:T(8,128)(2,1)S(1)} %collective-permute-done.refs_2_), channel_id=1, source_target_pairs={{0,6},{1,7},{2,4},{3,5},{4,2},{5,3},{6,0},{7,1},{8,14},{9,15},{10,... | collective-permute-start | bytes 786440 | tf_op jit(solution)/shard_map/ppermute | solution.py:209
  20.8 0.5 %collective-permute-start.9 = (bf16[128,1024]{1,0:T(8,128)(2,1)S(1)}, bf16[128,1024]{1,0:T(8,128)(2,1)S(1)}, u32[]{:S(2)}, u32[]{:S(2)}) collective-permute-start(bf16[128,1024]{1,0:T(8,128)(2,1)S(1)} %collective-permute-done.refs_2_), channel_id=1, source_target_pairs={{0,4},{1,5},{2,6},{3,7},{4,0},{5,1},{6,2},{7,3},{8,12},{9,13},{10,... | collective-permute-start | bytes 786440 | tf_op jit(solution)/shard_map/ppermute | solution.py:209
  21.4 0.0 collective-permute-done.3.refs_0_
  21.4 0.6 %collective-permute-start.4 = (bf16[128,1024]{1,0:T(8,128)(2,1)S(1)}, bf16[128,1024]{1,0:T(8,128)(2,1)S(1)}, u32[]{:S(2)}, u32[]{:S(2)}) collective-permute-start(bf16[128,1024]{1,0:T(8,128)(2,1)S(1)} %collective-permute-done.3.refs_0_), channel_id=1, source_target_pairs={{0,1},{1,0},{2,3},{3,2},{4,5},{5,4},{6,7},{7,6},{8,9},{9,8},{10,11... | collective-permute-start | bytes 786440 | tf_op jit(solution)/shard_map/ppermute | solution.py:209
  21.9 0.0 copy-done
  21.9 3.9 %shard_map.92 = (f32[8,256]{1,0:T(8,128)S(1)}, f32[8,256]{1,0:T(8,128)S(1)}, f32[1024,128]{1,0:T(8,128)S(1)}) custom-call(bf16[128,1024]{1,0:T(8,128)(2,1)S(1)} %collective-permute-done.3.refs_0_, bf16[128,1024]{1,0:T(8,128)(2,1)S(1)} %collective-permute-done.5.refs_1_, bf16[128,1024]{1,0:T(8,128)(2,1)S(1)} %collective-permute-done.refs_2_, ...), custom_call_target="tpu_custom_call" | custom-call | flops 6039797760 | bytes 786432 | tf_op jit(solution)/shard_map/pallas_call | solution.py:312
  25.8 2.1 %collective-permute-done.7.refs_2_ = bf16[128,1024]{1,0:T(8,128)(2,1)S(1)} collective-permute-done((bf16[128,1024]{1,0:T(8,128)(2,1)S(1)}, bf16[128,1024]{1,0:T(8,128)(2,1)S(1)}, u32[]{:S(2)}, u32[]{:S(2)}) %collective-permute-start.7) | collective-permute-done | bytes 262176 | tf_op jit(solution)/shard_map/ppermute | solution.py:209
  27.9 3.2 %collective-permute-start.11 = (bf16[128,1024]{1,0:T(8,128)(2,1)S(1)}, bf16[128,1024]{1,0:T(8,128)(2,1)S(1)}, u32[]{:S(2)}, u32[]{:S(2)}) collective-permute-start(bf16[128,1024]{1,0:T(8,128)(2,1)S(1)} %collective-permute-done.refs_2_), channel_id=1, source_target_pairs={{0,1},{1,0},{2,3},{3,2},{4,5},{5,4},{6,7},{7,6},{8,9},{9,8},{10,11... | collective-permute-start | bytes 786440 | tf_op jit(solution)/shard_map/ppermute | solution.py:209
  31.1 0.0 collective-permute-done.6.refs_1_
  31.1 0.0 collective-permute-start.12
  31.1 0.0 collective-permute-done.4.refs_0_
  31.1 3.9 %shard_map.93 = (f32[8,256]{1,0:T(8,128)S(1)}, f32[8,256]{1,0:T(8,128)S(1)}, f32[1024,128]{1,0:T(8,128)S(1)}) custom-call(bf16[128,1024]{1,0:T(8,128)(2,1)S(1)} %collective-permute-done.4.refs_0_, bf16[128,1024]{1,0:T(8,128)(2,1)S(1)} %collective-permute-done.6.refs_1_, bf16[128,1024]{1,0:T(8,128)(2,1)S(1)} %collective-permute-done.7.refs_2_, ...), custom_call_target="tpu_custom_call" | custom-call | flops 6039797760 | bytes 786432 | tf_op jit(solution)/shard_map/pallas_call | solution.py:312
  35.0 0.0 collective-permute-done.9.refs_3_
  35.0 0.6 %collective-permute-start.10 = (bf16[128,1024]{1,0:T(8,128)(2,1)S(1)}, bf16[128,1024]{1,0:T(8,128)(2,1)S(1)}, u32[]{:S(2)}, u32[]{:S(2)}) collective-permute-start(bf16[128,1024]{1,0:T(8,128)(2,1)S(1)} %collective-permute-done.9.refs_3_), channel_id=1, source_target_pairs={{0,1},{1,0},{2,3},{3,2},{4,5},{5,4},{6,7},{7,6},{8,9},{9,8},{10,11... | collective-permute-start | bytes 786440 | tf_op jit(solution)/shard_map/ppermute | solution.py:209
  35.6 0.0 collective-permute-done.2.refs_2_
  35.6 0.1 collective-permute-start.8
  35.7 0.0 collective-permute-done.11.refs_0_
  35.7 0.0 collective-permute-done.12.refs_1_
  35.7 4.6 %shard_map.94 = (f32[8,256]{1,0:T(8,128)S(1)}, f32[8,256]{1,0:T(8,128)S(1)}, f32[1024,128]{1,0:T(8,128)S(1)}) custom-call(bf16[128,1024]{1,0:T(8,128)(2,1)S(1)} %collective-permute-done.11.refs_0_, bf16[128,1024]{1,0:T(8,128)(2,1)S(1)} %collective-permute-done.12.refs_1_, bf16[128,1024]{1,0:T(8,128)(2,1)S(1)} %collective-permute-done.2.refs_2_, ...), custom_call_target="tpu_custom_call" | custom-call | flops 8053063680 | bytes 1048576 | tf_op jit(solution)/shard_map/pallas_call | solution.py:312
  40.3 0.0 collective-permute-done.10.refs_1_
  40.3 0.0 collective-permute-done.8.refs_0_
  40.3 6.1 %shard_map.95 = bf16[128,1024]{1,0:T(8,128)(2,1)} custom-call(bf16[128,1024]{1,0:T(8,128)(2,1)S(1)} %collective-permute-done.8.refs_0_, bf16[128,1024]{1,0:T(8,128)(2,1)S(1)} %collective-permute-done.10.refs_1_, s32[1,12]{1,0:T(1,128)S(1)} %copy-done.1, s32[1]{0:T(128)S(6)} %copy.11.covis_count.refs_4_.refs_5_.refs_3_, f32[1,1024]{1,0:T(1,128)S(1)} %bitcast.8, ...), custom_call_target="tpu_custom_call" | custom-call | flops 4026531840 | bytes 524288 | tf_op jit(solution)/shard_map/pallas_call | solution.py:321
Async XLA Ops:
  0.0 7.9 %collective-permute-start.1 = (bf16[128,1024]{1,0:T(8,128)(2,1)}, bf16[128,1024]{1,0:T(8,128)(2,1)S(1)}, u32[]{:S(2)}, u32[]{:S(2)}) collective-permute-start(bf16[128,1024]{1,0:T(8,128)(2,1)} %bitcast.10), channel_id=1, source_target_pairs={{0,1},{1,0},{2,3},{3,2},{4,5},{5,4},{6,7},{7,6},{8,9},{9,8},{10,11... | collective-permute-start | bytes 786440 | tf_op jit(solution)/shard_map/ppermute | solution.py:209
  0.1 19.9 %collective-permute-start = (bf16[128,1024]{1,0:T(8,128)(2,1)}, bf16[128,1024]{1,0:T(8,128)(2,1)S(1)}, u32[]{:S(2)}, u32[]{:S(2)}) collective-permute-start(bf16[128,1024]{1,0:T(8,128)(2,1)} %bitcast.11), channel_id=1, source_target_pairs={{0,10},{1,11},{2,8},{3,9},{4,14},{5,15},{6,12},{7,13},{8,2},{9,3},... | collective-permute-start | bytes 786440 | tf_op jit(solution)/shard_map/ppermute | solution.py:209
  4.8 16.6 %collective-permute-start.3 = (bf16[128,1024]{1,0:T(8,128)(2,1)}, bf16[128,1024]{1,0:T(8,128)(2,1)S(1)}, u32[]{:S(2)}, u32[]{:S(2)}) collective-permute-start(bf16[128,1024]{1,0:T(8,128)(2,1)} %bitcast.12), channel_id=1, source_target_pairs={{0,2},{1,3},{2,0},{3,1},{4,6},{5,7},{6,4},{7,5},{8,10},{9,11},{10,... | collective-permute-start | bytes 786440 | tf_op jit(solution)/shard_map/ppermute | solution.py:209
  5.0 11.5 %collective-permute-start.5 = (bf16[128,1024]{1,0:T(8,128)(2,1)}, bf16[128,1024]{1,0:T(8,128)(2,1)S(1)}, u32[]{:S(2)}, u32[]{:S(2)}) collective-permute-start(bf16[128,1024]{1,0:T(8,128)(2,1)} %bitcast.13), channel_id=1, source_target_pairs={{0,4},{1,5},{2,6},{3,7},{4,0},{5,1},{6,2},{7,3},{8,12},{9,13},{10,... | collective-permute-start | bytes 786440 | tf_op jit(solution)/shard_map/ppermute | solution.py:209
  7.9 0.7 %copy-start.1 = (s32[1,12]{1,0:T(1,128)S(1)}, s32[1,12]{1,0:T(1,128)}, u32[]{:S(2)}) copy-start(s32[1,12]{1,0:T(1,128)} %refs_2_.1) | copy-start | bytes 148
  8.5 13.4 %copy-start = (f32[1024]{0:T(1024)S(1)}, f32[1024]{0:T(1024)}, u32[]{:S(2)}) copy-start(f32[1024]{0:T(1024)} %param.10) | copy-start | bytes 12292
  16.5 11.4 %collective-permute-start.7 = (bf16[128,1024]{1,0:T(8,128)(2,1)S(1)}, bf16[128,1024]{1,0:T(8,128)(2,1)S(1)}, u32[]{:S(2)}, u32[]{:S(2)}) collective-permute-start(bf16[128,1024]{1,0:T(8,128)(2,1)S(1)} %collective-permute-done.5.refs_1_), channel_id=1, source_target_pairs={{0,2},{1,3},{2,0},{3,1},{4,6},{5,7},{6,4},{7,5},{8,10},{9,11},{10,... | collective-permute-start | bytes 786440 | tf_op jit(solution)/shard_map/ppermute | solution.py:209
  18.3 12.9 %collective-permute-start.6 = (bf16[128,1024]{1,0:T(8,128)(2,1)S(1)}, bf16[128,1024]{1,0:T(8,128)(2,1)S(1)}, u32[]{:S(2)}, u32[]{:S(2)}) collective-permute-start(bf16[128,1024]{1,0:T(8,128)(2,1)S(1)} %collective-permute-done.5.refs_1_), channel_id=1, source_target_pairs={{0,1},{1,0},{2,3},{3,2},{4,5},{5,4},{6,7},{7,6},{8,9},{9,8},{10,11... | collective-permute-start | bytes 786440 | tf_op jit(solution)/shard_map/ppermute | solution.py:209
  20.0 15.6 %collective-permute-start.2 = (bf16[128,1024]{1,0:T(8,128)(2,1)S(1)}, bf16[128,1024]{1,0:T(8,128)(2,1)S(1)}, u32[]{:S(2)}, u32[]{:S(2)}) collective-permute-start(bf16[128,1024]{1,0:T(8,128)(2,1)S(1)} %collective-permute-done.refs_2_), channel_id=1, source_target_pairs={{0,6},{1,7},{2,4},{3,5},{4,2},{5,3},{6,0},{7,1},{8,14},{9,15},{10,... | collective-permute-start | bytes 786440 | tf_op jit(solution)/shard_map/ppermute | solution.py:209
  20.8 14.2 %collective-permute-start.9 = (bf16[128,1024]{1,0:T(8,128)(2,1)S(1)}, bf16[128,1024]{1,0:T(8,128)(2,1)S(1)}, u32[]{:S(2)}, u32[]{:S(2)}) collective-permute-start(bf16[128,1024]{1,0:T(8,128)(2,1)S(1)} %collective-permute-done.refs_2_), channel_id=1, source_target_pairs={{0,4},{1,5},{2,6},{3,7},{4,0},{5,1},{6,2},{7,3},{8,12},{9,13},{10,... | collective-permute-start | bytes 786440 | tf_op jit(solution)/shard_map/ppermute | solution.py:209
  21.4 9.8 %collective-permute-start.4 = (bf16[128,1024]{1,0:T(8,128)(2,1)S(1)}, bf16[128,1024]{1,0:T(8,128)(2,1)S(1)}, u32[]{:S(2)}, u32[]{:S(2)}) collective-permute-start(bf16[128,1024]{1,0:T(8,128)(2,1)S(1)} %collective-permute-done.3.refs_0_), channel_id=1, source_target_pairs={{0,1},{1,0},{2,3},{3,2},{4,5},{5,4},{6,7},{7,6},{8,9},{9,8},{10,11... | collective-permute-start | bytes 786440 | tf_op jit(solution)/shard_map/ppermute | solution.py:209
  27.9 7.8 %collective-permute-start.11 = (bf16[128,1024]{1,0:T(8,128)(2,1)S(1)}, bf16[128,1024]{1,0:T(8,128)(2,1)S(1)}, u32[]{:S(2)}, u32[]{:S(2)}) collective-permute-start(bf16[128,1024]{1,0:T(8,128)(2,1)S(1)} %collective-permute-done.refs_2_), channel_id=1, source_target_pairs={{0,1},{1,0},{2,3},{3,2},{4,5},{5,4},{6,7},{7,6},{8,9},{9,8},{10,11... | collective-permute-start | bytes 786440 | tf_op jit(solution)/shard_map/ppermute | solution.py:209
  31.1 4.6 %collective-permute-start.12 = (bf16[128,1024]{1,0:T(8,128)(2,1)S(1)}, bf16[128,1024]{1,0:T(8,128)(2,1)S(1)}, u32[]{:S(2)}, u32[]{:S(2)}) collective-permute-start(bf16[128,1024]{1,0:T(8,128)(2,1)S(1)} %collective-permute-done.7.refs_2_), channel_id=1, source_target_pairs={{0,1},{1,0},{2,3},{3,2},{4,5},{5,4},{6,7},{7,6},{8,9},{9,8},{10,11... | collective-permute-start | bytes 786440 | tf_op jit(solution)/shard_map/ppermute | solution.py:209
  35.0 5.3 %collective-permute-start.10 = (bf16[128,1024]{1,0:T(8,128)(2,1)S(1)}, bf16[128,1024]{1,0:T(8,128)(2,1)S(1)}, u32[]{:S(2)}, u32[]{:S(2)}) collective-permute-start(bf16[128,1024]{1,0:T(8,128)(2,1)S(1)} %collective-permute-done.9.refs_3_), channel_id=1, source_target_pairs={{0,1},{1,0},{2,3},{3,2},{4,5},{5,4},{6,7},{7,6},{8,9},{9,8},{10,11... | collective-permute-start | bytes 786440 | tf_op jit(solution)/shard_map/ppermute | solution.py:209
  35.6 4.7 %collective-permute-start.8 = (bf16[128,1024]{1,0:T(8,128)(2,1)S(1)}, bf16[128,1024]{1,0:T(8,128)(2,1)S(1)}, u32[]{:S(2)}, u32[]{:S(2)}) collective-permute-start(bf16[128,1024]{1,0:T(8,128)(2,1)S(1)} %collective-permute-done.2.refs_2_), channel_id=1, source_target_pairs={{0,1},{1,0},{2,3},{3,2},{4,5},{5,4},{6,7},{7,6},{8,9},{9,8},{10,11... | collective-permute-start | bytes 786440 | tf_op jit(solution)/shard_map/ppermute | solution.py:209

commit v3 on v2

--- a/solution.py
+++ b/solution.py
@@ -11,6 +11,8 @@
 HEAD_DIM = 64
 REACH = 6
 PAIRS = HEADS // 2
+GROUP = 2
+WEIGHT = (3, 3, 3, 3, 3, 3)
 F32 = jnp.float32
 BF16 = jnp.bfloat16
 BY_ROWS = (((1,), (1,)), ((), ()))
@@ -85,13 +87,19 @@
                 part = old[2][head, :] * keep[:, lanes] + part
             numer_ref[head, :] = part
 
-    key_ref[...] = jnp.dot(normed, w_key[...], preferred_element_type=F32).astype(BF16)
+    def project(group):
+        span = slice(2 * HEAD_DIM * GROUP * group, 2 * HEAD_DIM * GROUP * (group + 1))
+        key_ref[:, span] = jnp.dot(normed, w_key[:, span], preferred_element_type=F32).astype(BF16)
+        value_ref[span, :] = lax.dot_general(
+            w_value_t[span, :], normed, BY_ROWS, preferred_element_type=F32
+        ).astype(BF16)
+
+    project(0)
     scores = scores_of(0)
-    value_ref[...] = lax.dot_general(
-        w_value_t[...], normed, BY_ROWS, preferred_element_type=F32
-    ).astype(BF16)
     held = None
     for pair in range(PAIRS):
+        if pair % GROUP == 0 and pair + GROUP < PAIRS:
+            project(pair // GROUP + 1)
         ahead = scores_of(pair + 1) if pair + 1 < PAIRS else None
         if held is not None:
             gather_values(pair - 1, *held)
@@ -105,7 +113,7 @@
     for pair in range(PAIRS):
         for j in range(2):
             head = slice((2 * pair + j) * HEAD_DIM, (2 * pair + j + 1) * HEAD_DIM)
-            attended = numer_ref[head, :] / total_ref[pair : pair + 1, rows * j : rows * (j + 1)]
+            attended = numer_ref[head, :] * (1.0 / total_ref[pair : pair + 1, rows * j : rows * (j + 1)])
             mean_sq = jnp.mean(attended * attended, axis=0, keepdims=True)
             headed_ref[head, :] = (attended * lax.rsqrt(mean_sq + 1e-06) * gain_col[head, :]).astype(BF16)
     update = lax.dot_general(headed_ref[...], w_out[...], BY_COLUMNS, preferred_element_type=F32)
@@ -222,21 +230,21 @@
     if reached and max(masks) < view_count:
 
         def first(own):
-            return {mask: swap(mask)(own) for mask in (10, 4, 2, 1)}
+            return {0: own} | {mask: swap(mask)(own) for mask in (10, 4, 2, 1)}
 
         def second(got, after):
             got[12] = swap(6)(after(got[10]))
             got[14] = swap(4)(after(got[10]))
             got[6] = swap(2)(after(got[4]))
-            for mask in (2, 4):
+            for mask in (4, 2):
                 got[mask ^ 1] = swap(1)(after(got[mask]))
 
         def third(got, after):
-            for mask in (6, 10):
+            for mask in (10, 6):
                 got[mask ^ 1] = swap(1)(after(got[mask]))
 
         def fourth(got, after):
-            for mask in (12, 14):
+            for mask in (14, 12):
                 got[mask ^ 1] = swap(1)(after(got[mask]))
 
         return first, second, third, fourth, masks, lambda me: {mask: me ^ mask for mask in masks}
@@ -277,12 +285,12 @@
     return first, second, third, fourth, names, owners
 
 
-def cost_of(blocks, rows, width):
-    keys = blocks * rows
+def cost_of(blocks, rows, width, weight):
+    keys = int(blocks * rows * weight)
     return pl.CostEstimate(
-        flops=3 * (4 * keys * width * width + 8 * keys * rows * width),
-        bytes_accessed=2 * keys * width,
-        transcendentals=keys * rows * HEADS,
+        flops=4 * keys * width * width + 8 * keys * rows * width,
+        bytes_accessed=2 * blocks * rows * width,
+        transcendentals=0,
     )
 
 
@@ -300,7 +308,10 @@
     ]
     params = pltpu.CompilerParams(vmem_limit_bytes=24 * MIB)
 
+    slots_done = []
+
     def call_later(got, slots, state, tail=None):
+        slots_done.append(slots)
         count = len(slots)
         held = [
             pltpu.with_memory_space_constraint(x, pltpu.VMEM) for x in (w_key_here, w_value_t, query, *state)
@@ -316,7 +327,7 @@
                 out_specs=[VMEM] * 3,
                 scratch_shapes=scratch,
                 compiler_params=params,
-                cost_estimate=cost_of(count, rows, width),
+                cost_estimate=cost_of(count, rows, width, WEIGHT[len(slots_done)]),
             )(*parts)
         return pl.pallas_call(
             functools.partial(last_kernel, slots, owners),
@@ -328,7 +339,7 @@
             + [pltpu.VMEM(source.shape, BF16), pltpu.SemaphoreType.DMA((2,))]
             + scratch,
             compiler_params=params,
-            cost_estimate=cost_of(count, rows, width),
+            cost_estimate=cost_of(count, rows, width, WEIGHT[len(slots_done)]),
         )(*parts, *tail)
 
     got = first(source)
@@ -348,18 +359,21 @@
         + scratch_for(2, rows, width)
         + [pltpu.SemaphoreType.DMA((5,))],
         compiler_params=params,
-        cost_estimate=cost_of(2, rows, width),
+        cost_estimate=cost_of(2, rows, width, WEIGHT[0]),
     )(
         in_hbm(source), got[names[0]], covis_list, covis_count,
         *map(in_hbm, (gain_row, w_query, w_key, w_value)),
     )
-    mark = state[0]
-    second(got, lambda block: tie(block, mark))
-    state = call_later(got, names[1:4], state)
-    third(got, lambda block: tie(block, state[0]))
-    state = call_later(got, names[4:7], state)
-    fourth(got, lambda block: tie(block, state[0]))
-    state = call_later(got, names[7:11], state)
+    for wave, slots in (
+        (second, names[1:4]),
+        (third, names[4:7]),
+        (None, names[7:9]),
+        (fourth, names[9:11]),
+    ):
+        if wave is not None:
+            mark = state[0]
+            wave(got, lambda block: tie(block, mark))
+        state = call_later(got, slots, state)
     return call_later(got, names[11:], state, (gain_col, in_hbm(w_out), in_hbm(source)))[None]
 
 

time: 47.1 us -> 42.2 us (0.90)
  starting transfers between devices: 15.6 us -> 13.2 us
  waiting for transfers between devices: 4.24 us -> 2.83 us
  Pallas kernels: 24.3 us -> 23.5 us
    ppermute x13, starting transfers between devices: 15.6 us -> 13.2 us  [swap(): lax.ppermute(block, axis, [(i, i ^ mask) for i in range(view_count)])]
    ppermute x13, waiting for transfers between devices: 4.24 us -> 2.83 us  [swap(): lax.ppermute(block, axis, [(i, i ^ mask) for i in range(view_count)])]
    pallas_call x1, Pallas kernels: 6.1 us -> 4.74 us  [call_later(): pl.pallas_call(functools.partial(last_kernel, slots, owners), out_shape=j...]
    pallas_call x3 -> x4, Pallas kernels: 12.3 us -> 13.2 us  [call_later(): pl.pallas_call(functools.partial(later_kernel, slots, owners), out_shape=...]
  transfers between devices with their start and end apart: 13 -> 13, of which waited for: 2 -> 2; matrix products, arithmetic and copies ran while one was open for 2% -> 2% of each run, Pallas kernels for 39% -> 45%
where the time goes in v3:
time: 42.2 us; the launch traced here: 42.1 us
  Pallas kernels  23.5 us (56%)
  starting transfers between devices  13.2 us (31%)
  waiting for transfers between devices  2.83 us (7%)
  local copies, waits for them, and re-layouts  1.56 us (4%)
  between operations  0.94 us (2%)
    ppermute x13, starting transfers between devices, swap(): lax.ppermute(block, axis, [(i, i ^ mask) for i in range(view_count)])  13.2 us
    pallas_call x4, Pallas kernels, call_later(): pl.pallas_call(functools.partial(later_kernel, slots, owners), out_shape=...  13.2 us
    pallas_call x1, Pallas kernels, on_device(): pl.pallas_call(functools.partial(first_kernel, owners, names[:1]), out_sh...  5.58 us
    pallas_call x1, Pallas kernels, call_later(): pl.pallas_call(functools.partial(last_kernel, slots, owners), out_shape=j...  4.74 us
    ppermute x13, waiting for transfers between devices, swap(): lax.ppermute(block, axis, [(i, i ^ mask) for i in range(view_count)])  2.83 us
    reshape x1, local copies, waits for them, and re-layouts, on_device(): gain_col = out_gain.reshape(width, 1)  0.9 us
  transfers between devices with their start and end apart: 13, of which 2 were waited for; matrix products, arithmetic and copies ran while one was open for 2% of the time, Pallas kernels for 45%

profile of v3, /device:TPU:1, one launch (start us, length us, event | category | flops | bytes accessed | tf_op | source)
XLA Modules:
  0.0 42.1 jit_solution(15145611064982840216)
XLA Ops:
  0.0 0.1 collective-permute-start.1
  0.1 4.7 %collective-permute-start = (bf16[128,1024]{1,0:T(8,128)(2,1)}, bf16[128,1024]{1,0:T(8,128)(2,1)S(1)}, u32[]{:S(2)}, u32[]{:S(2)}) collective-permute-start(bf16[128,1024]{1,0:T(8,128)(2,1)} %bitcast.12), channel_id=1, source_target_pairs={{0,10},{1,11},{2,8},{3,9},{4,14},{5,15},{6,12},{7,13},{8,2},{9,3},... | collective-permute-start | bytes 786440 | tf_op jit(solution)/shard_map/ppermute | solution.py:217
  4.8 0.2 collective-permute-start.3
  5.0 1.3 %collective-permute-start.4 = (bf16[128,1024]{1,0:T(8,128)(2,1)}, bf16[128,1024]{1,0:T(8,128)(2,1)S(1)}, u32[]{:S(2)}, u32[]{:S(2)}) collective-permute-start(bf16[128,1024]{1,0:T(8,128)(2,1)} %bitcast.14), channel_id=1, source_target_pairs={{0,4},{1,5},{2,6},{3,7},{4,0},{5,1},{6,2},{7,3},{8,12},{9,13},{10,... | collective-permute-start | bytes 786440 | tf_op jit(solution)/shard_map/ppermute | solution.py:217
  6.9 0.9 %copy.10.refs_11_ = f32[1024,1]{1,0:T(8,128)S(1)} copy(f32[1024,1]{0,1:T(1,128)} %bitcast.10) | data formatting | bytes 8192 | tf_op jit(solution)/shard_map/reshape | solution.py:302
  7.9 0.0 collective-permute-done.1.other
  7.9 0.0 copy-start.1
  7.9 0.6 %copy-done.1 = s32[1,12]{1,0:T(1,128)S(1)} copy-done((s32[1,12]{1,0:T(1,128)S(1)}, s32[1,12]{1,0:T(1,128)}, u32[]{:S(2)}) %copy-start.1) | copy-done | bytes 72
  8.5 0.0 copy-start
  8.5 5.6 %shard_map.91 = (bf16[8,256,128]{2,1,0:T(8,128)(2,1)S(1)}, f32[8,256]{1,0:T(8,128)S(1)}, f32[8,256]{1,0:T(8,128)S(1)}, f32[1024,128]{1,0:T(8,128)S(1)}, bf16[102...) custom-call(bf16[128,1024]{1,0:T(8,128)(2,1)} %bitcast.15, bf16[128,1024]{1,0:T(8,128)(2,1)S(1)} %collective-permute-done.1.other, ...), custom_call_target="tpu_custom_call" | custom-call | flops 4026531840 | bytes 524288 | tf_op jit(solution)/shard_map/pallas_call | solution.py:346
  14.1 2.4 %collective-permute-done.4.refs_1_ = bf16[128,1024]{1,0:T(8,128)(2,1)S(1)} collective-permute-done((bf16[128,1024]{1,0:T(8,128)(2,1)}, bf16[128,1024]{1,0:T(8,128)(2,1)S(1)}, u32[]{:S(2)}, u32[]{:S(2)}) %collective-permute-start.4) | collective-permute-done | bytes 262176 | tf_op jit(solution)/shard_map/ppermute | solution.py:217
  16.5 1.8 %collective-permute-start.6 = (bf16[128,1024]{1,0:T(8,128)(2,1)S(1)}, bf16[128,1024]{1,0:T(8,128)(2,1)S(1)}, u32[]{:S(2)}, u32[]{:S(2)}) collective-permute-start(bf16[128,1024]{1,0:T(8,128)(2,1)S(1)} %collective-permute-done.4.refs_1_), channel_id=1, source_target_pairs={{0,2},{1,3},{2,0},{3,1},{4,6},{5,7},{6,4},{7,5},{8,10},{9,11},{10,... | collective-permute-start | bytes 786440 | tf_op jit(solution)/shard_map/ppermute | solution.py:217
  18.3 1.7 %collective-permute-start.9 = (bf16[128,1024]{1,0:T(8,128)(2,1)S(1)}, bf16[128,1024]{1,0:T(8,128)(2,1)S(1)}, u32[]{:S(2)}, u32[]{:S(2)}) collective-permute-start(bf16[128,1024]{1,0:T(8,128)(2,1)S(1)} %collective-permute-done.4.refs_1_), channel_id=1, source_target_pairs={{0,1},{1,0},{2,3},{3,2},{4,5},{5,4},{6,7},{7,6},{8,9},{9,8},{10,11... | collective-permute-start | bytes 786440 | tf_op jit(solution)/shard_map/ppermute | solution.py:217
  20.0 0.0 collective-permute-done.refs_2_
  20.0 0.0 collective-permute-start.11
  20.0 1.4 %collective-permute-start.2 = (bf16[128,1024]{1,0:T(8,128)(2,1)S(1)}, bf16[128,1024]{1,0:T(8,128)(2,1)S(1)}, u32[]{:S(2)}, u32[]{:S(2)}) collective-permute-start(bf16[128,1024]{1,0:T(8,128)(2,1)S(1)} %collective-permute-done.refs_2_), channel_id=1, source_target_pairs={{0,6},{1,7},{2,4},{3,5},{4,2},{5,3},{6,0},{7,1},{8,14},{9,15},{10,... | collective-permute-start | bytes 786440 | tf_op jit(solution)/shard_map/ppermute | solution.py:217
  21.4 0.0 collective-permute-done.3.refs_0_
  21.4 0.6 %collective-permute-start.8 = (bf16[128,1024]{1,0:T(8,128)(2,1)S(1)}, bf16[128,1024]{1,0:T(8,128)(2,1)S(1)}, u32[]{:S(2)}, u32[]{:S(2)}) collective-permute-start(bf16[128,1024]{1,0:T(8,128)(2,1)S(1)} %collective-permute-done.3.refs_0_), channel_id=1, source_target_pairs={{0,1},{1,0},{2,3},{3,2},{4,5},{5,4},{6,7},{7,6},{8,9},{9,8},{10,11... | collective-permute-start | bytes 786440 | tf_op jit(solution)/shard_map/ppermute | solution.py:217
  21.9 0.0 copy-done
  21.9 3.8 %shard_map.92 = (f32[8,256]{1,0:T(8,128)S(1)}, f32[8,256]{1,0:T(8,128)S(1)}, f32[1024,128]{1,0:T(8,128)S(1)}) custom-call(bf16[128,1024]{1,0:T(8,128)(2,1)S(1)} %collective-permute-done.3.refs_0_, bf16[128,1024]{1,0:T(8,128)(2,1)S(1)} %collective-permute-done.4.refs_1_, bf16[128,1024]{1,0:T(8,128)(2,1)S(1)} %collective-permute-done.refs_2_, ...), custom_call_target="tpu_custom_call" | custom-call | flops 6039797760 | bytes 786432 | tf_op jit(solution)/shard_map/pallas_call | solution.py:323
  25.7 0.0 collective-permute-done.6.refs_2_
  25.7 0.1 collective-permute-start.5
  25.8 0.0 collective-permute-done.9.refs_1_
  25.8 0.5 %collective-permute-start.7 = (bf16[128,1024]{1,0:T(8,128)(2,1)S(1)}, bf16[128,1024]{1,0:T(8,128)(2,1)S(1)}, u32[]{:S(2)}, u32[]{:S(2)}) collective-permute-start(bf16[128,1024]{1,0:T(8,128)(2,1)S(1)} %collective-permute-done.6.refs_2_), channel_id=1, source_target_pairs={{0,1},{1,0},{2,3},{3,2},{4,5},{5,4},{6,7},{7,6},{8,9},{9,8},{10,11... | collective-permute-start | bytes 786440 | tf_op jit(solution)/shard_map/ppermute | solution.py:217
  26.3 0.0 collective-permute-done.8.refs_0_
  26.3 3.8 %shard_map.93 = (f32[8,256]{1,0:T(8,128)S(1)}, f32[8,256]{1,0:T(8,128)S(1)}, f32[1024,128]{1,0:T(8,128)S(1)}) custom-call(bf16[128,1024]{1,0:T(8,128)(2,1)S(1)} %collective-permute-done.8.refs_0_, bf16[128,1024]{1,0:T(8,128)(2,1)S(1)} %collective-permute-done.9.refs_1_, bf16[128,1024]{1,0:T(8,128)(2,1)S(1)} %collective-permute-done.6.refs_2_, ...), custom_call_target="tpu_custom_call" | custom-call | flops 6039797760 | bytes 786432 | tf_op jit(solution)/shard_map/pallas_call | solution.py:323
  30.1 0.0 collective-permute-done.5.refs_0_
  30.1 0.0 collective-permute-done.7.refs_1_
  30.1 2.7 %shard_map.94 = (f32[8,256]{1,0:T(8,128)S(1)}, f32[8,256]{1,0:T(8,128)S(1)}, f32[1024,128]{1,0:T(8,128)S(1)}) custom-call(bf16[128,1024]{1,0:T(8,128)(2,1)S(1)} %collective-permute-done.5.refs_0_, bf16[128,1024]{1,0:T(8,128)(2,1)S(1)} %collective-permute-done.7.refs_1_, s32[1,12]{1,0:T(1,128)S(1)} %copy-done.1, s32[1]{0:T(128)S(6)} %copy.11.covis_count.refs_4_.refs_3_, ...), custom_call_target="tpu_custom_call" | custom-call | flops 4026531840 | bytes 524288 | tf_op jit(solution)/shard_map/pallas_call | solution.py:323
  32.9 0.0 collective-permute-done.11.refs_1_
  32.9 0.1 collective-permute-start.12
  33.0 0.4 %collective-permute-done.2.refs_0_ = bf16[128,1024]{1,0:T(8,128)(2,1)S(1)} collective-permute-done((bf16[128,1024]{1,0:T(8,128)(2,1)S(1)}, bf16[128,1024]{1,0:T(8,128)(2,1)S(1)}, u32[]{:S(2)}, u32[]{:S(2)}) %collective-permute-start.2) | collective-permute-done | bytes 262176 | tf_op jit(solution)/shard_map/ppermute | solution.py:217
  33.5 0.8 %collective-permute-start.10 = (bf16[128,1024]{1,0:T(8,128)(2,1)S(1)}, bf16[128,1024]{1,0:T(8,128)(2,1)S(1)}, u32[]{:S(2)}, u32[]{:S(2)}) collective-permute-start(bf16[128,1024]{1,0:T(8,128)(2,1)S(1)} %collective-permute-done.2.refs_0_), channel_id=1, source_target_pairs={{0,1},{1,0},{2,3},{3,2},{4,5},{5,4},{6,7},{7,6},{8,9},{9,8},{10,11... | collective-permute-start | bytes 786440 | tf_op jit(solution)/shard_map/ppermute | solution.py:217
  34.2 2.9 %shard_map.95 = (f32[8,256]{1,0:T(8,128)S(1)}, f32[8,256]{1,0:T(8,128)S(1)}, f32[1024,128]{1,0:T(8,128)S(1)}) custom-call(bf16[128,1024]{1,0:T(8,128)(2,1)S(1)} %collective-permute-done.2.refs_0_, bf16[128,1024]{1,0:T(8,128)(2,1)S(1)} %collective-permute-done.11.refs_1_, s32[1,12]{1,0:T(1,128)S(1)} %copy-done.1, s32[1]{0:T(128)S(6)} %copy.11.covis_count.refs_4_.refs_3_, ...), custom_call_target="tpu_custom_call" | custom-call | flops 4026531840 | bytes 524288 | tf_op jit(solution)/shard_map/pallas_call | solution.py:323
  37.1 0.0 collective-permute-done.12.refs_1_
  37.1 0.0 collective-permute-done.10.refs_0_
  37.2 4.7 %shard_map.96 = bf16[128,1024]{1,0:T(8,128)(2,1)} custom-call(bf16[128,1024]{1,0:T(8,128)(2,1)S(1)} %collective-permute-done.10.refs_0_, bf16[128,1024]{1,0:T(8,128)(2,1)S(1)} %collective-permute-done.12.refs_1_, s32[1,12]{1,0:T(1,128)S(1)} %copy-done.1, s32[1]{0:T(128)S(6)} %copy.11.covis_count.refs_4_.refs_3_, f32[1,1024]{1,0:T(1,128)S(1)} %bitcast.9, ...), custom_call_target="tpu_custom_call" | custom-call | flops 4026531840 | bytes 524288 | tf_op jit(solution)/shard_map/pallas_call | solution.py:332
Async XLA Ops:
  0.0 7.9 %collective-permute-start.1 = (bf16[128,1024]{1,0:T(8,128)(2,1)}, bf16[128,1024]{1,0:T(8,128)(2,1)S(1)}, u32[]{:S(2)}, u32[]{:S(2)}) collective-permute-start(bf16[128,1024]{1,0:T(8,128)(2,1)} %bitcast.11), channel_id=1, source_target_pairs={{0,1},{1,0},{2,3},{3,2},{4,5},{5,4},{6,7},{7,6},{8,9},{9,8},{10,11... | collective-permute-start | bytes 786440 | tf_op jit(solution)/shard_map/ppermute | solution.py:217
  0.1 19.9 %collective-permute-start = (bf16[128,1024]{1,0:T(8,128)(2,1)}, bf16[128,1024]{1,0:T(8,128)(2,1)S(1)}, u32[]{:S(2)}, u32[]{:S(2)}) collective-permute-start(bf16[128,1024]{1,0:T(8,128)(2,1)} %bitcast.12), channel_id=1, source_target_pairs={{0,10},{1,11},{2,8},{3,9},{4,14},{5,15},{6,12},{7,13},{8,2},{9,3},... | collective-permute-start | bytes 786440 | tf_op jit(solution)/shard_map/ppermute | solution.py:217
  4.8 16.6 %collective-permute-start.3 = (bf16[128,1024]{1,0:T(8,128)(2,1)}, bf16[128,1024]{1,0:T(8,128)(2,1)S(1)}, u32[]{:S(2)}, u32[]{:S(2)}) collective-permute-start(bf16[128,1024]{1,0:T(8,128)(2,1)} %bitcast.13), channel_id=1, source_target_pairs={{0,2},{1,3},{2,0},{3,1},{4,6},{5,7},{6,4},{7,5},{8,10},{9,11},{10,... | collective-permute-start | bytes 786440 | tf_op jit(solution)/shard_map/ppermute | solution.py:217
  5.0 11.5 %collective-permute-start.4 = (bf16[128,1024]{1,0:T(8,128)(2,1)}, bf16[128,1024]{1,0:T(8,128)(2,1)S(1)}, u32[]{:S(2)}, u32[]{:S(2)}) collective-permute-start(bf16[128,1024]{1,0:T(8,128)(2,1)} %bitcast.14), channel_id=1, source_target_pairs={{0,4},{1,5},{2,6},{3,7},{4,0},{5,1},{6,2},{7,3},{8,12},{9,13},{10,... | collective-permute-start | bytes 786440 | tf_op jit(solution)/shard_map/ppermute | solution.py:217
  7.9 0.7 %copy-start.1 = (s32[1,12]{1,0:T(1,128)S(1)}, s32[1,12]{1,0:T(1,128)}, u32[]{:S(2)}) copy-start(s32[1,12]{1,0:T(1,128)} %refs_2_.5) | copy-start | bytes 148
  8.5 13.4 %copy-start = (f32[1024]{0:T(1024)S(1)}, f32[1024]{0:T(1024)}, u32[]{:S(2)}) copy-start(f32[1024]{0:T(1024)} %param.10) | copy-start | bytes 12292
  16.5 9.3 %collective-permute-start.6 = (bf16[128,1024]{1,0:T(8,128)(2,1)S(1)}, bf16[128,1024]{1,0:T(8,128)(2,1)S(1)}, u32[]{:S(2)}, u32[]{:S(2)}) collective-permute-start(bf16[128,1024]{1,0:T(8,128)(2,1)S(1)} %collective-permute-done.4.refs_1_), channel_id=1, source_target_pairs={{0,2},{1,3},{2,0},{3,1},{4,6},{5,7},{6,4},{7,5},{8,10},{9,11},{10,... | collective-permute-start | bytes 786440 | tf_op jit(solution)/shard_map/ppermute | solution.py:217
  18.3 7.6 %collective-permute-start.9 = (bf16[128,1024]{1,0:T(8,128)(2,1)S(1)}, bf16[128,1024]{1,0:T(8,128)(2,1)S(1)}, u32[]{:S(2)}, u32[]{:S(2)}) collective-permute-start(bf16[128,1024]{1,0:T(8,128)(2,1)S(1)} %collective-permute-done.4.refs_1_), channel_id=1, source_target_pairs={{0,1},{1,0},{2,3},{3,2},{4,5},{5,4},{6,7},{7,6},{8,9},{9,8},{10,11... | collective-permute-start | bytes 786440 | tf_op jit(solution)/shard_map/ppermute | solution.py:217
  20.0 12.9 %collective-permute-start.11 = (bf16[128,1024]{1,0:T(8,128)(2,1)S(1)}, bf16[128,1024]{1,0:T(8,128)(2,1)S(1)}, u32[]{:S(2)}, u32[]{:S(2)}) collective-permute-start(bf16[128,1024]{1,0:T(8,128)(2,1)S(1)} %collective-permute-done.refs_2_), channel_id=1, source_target_pairs={{0,4},{1,5},{2,6},{3,7},{4,0},{5,1},{6,2},{7,3},{8,12},{9,13},{10,... | collective-permute-start | bytes 786440 | tf_op jit(solution)/shard_map/ppermute | solution.py:217
  20.0 13.5 %collective-permute-start.2 = (bf16[128,1024]{1,0:T(8,128)(2,1)S(1)}, bf16[128,1024]{1,0:T(8,128)(2,1)S(1)}, u32[]{:S(2)}, u32[]{:S(2)}) collective-permute-start(bf16[128,1024]{1,0:T(8,128)(2,1)S(1)} %collective-permute-done.refs_2_), channel_id=1, source_target_pairs={{0,6},{1,7},{2,4},{3,5},{4,2},{5,3},{6,0},{7,1},{8,14},{9,15},{10,... | collective-permute-start | bytes 786440 | tf_op jit(solution)/shard_map/ppermute | solution.py:217
  21.4 5.0 %collective-permute-start.8 = (bf16[128,1024]{1,0:T(8,128)(2,1)S(1)}, bf16[128,1024]{1,0:T(8,128)(2,1)S(1)}, u32[]{:S(2)}, u32[]{:S(2)}) collective-permute-start(bf16[128,1024]{1,0:T(8,128)(2,1)S(1)} %collective-permute-done.3.refs_0_), channel_id=1, source_target_pairs={{0,1},{1,0},{2,3},{3,2},{4,5},{5,4},{6,7},{7,6},{8,9},{9,8},{10,11... | collective-permute-start | bytes 786440 | tf_op jit(solution)/shard_map/ppermute | solution.py:217
  25.7 4.4 %collective-permute-start.5 = (bf16[128,1024]{1,0:T(8,128)(2,1)S(1)}, bf16[128,1024]{1,0:T(8,128)(2,1)S(1)}, u32[]{:S(2)}, u32[]{:S(2)}) collective-permute-start(bf16[128,1024]{1,0:T(8,128)(2,1)S(1)} %collective-permute-done.refs_2_), channel_id=1, source_target_pairs={{0,1},{1,0},{2,3},{3,2},{4,5},{5,4},{6,7},{7,6},{8,9},{9,8},{10,11... | collective-permute-start | bytes 786440 | tf_op jit(solution)/shard_map/ppermute | solution.py:217
  25.8 4.3 %collective-permute-start.7 = (bf16[128,1024]{1,0:T(8,128)(2,1)S(1)}, bf16[128,1024]{1,0:T(8,128)(2,1)S(1)}, u32[]{:S(2)}, u32[]{:S(2)}) collective-permute-start(bf16[128,1024]{1,0:T(8,128)(2,1)S(1)} %collective-permute-done.6.refs_2_), channel_id=1, source_target_pairs={{0,1},{1,0},{2,3},{3,2},{4,5},{5,4},{6,7},{7,6},{8,9},{9,8},{10,11... | collective-permute-start | bytes 786440 | tf_op jit(solution)/shard_map/ppermute | solution.py:217
  32.9 4.3 %collective-permute-start.12 = (bf16[128,1024]{1,0:T(8,128)(2,1)S(1)}, bf16[128,1024]{1,0:T(8,128)(2,1)S(1)}, u32[]{:S(2)}, u32[]{:S(2)}) collective-permute-start(bf16[128,1024]{1,0:T(8,128)(2,1)S(1)} %collective-permute-done.11.refs_1_), channel_id=1, source_target_pairs={{0,1},{1,0},{2,3},{3,2},{4,5},{5,4},{6,7},{7,6},{8,9},{9,8},{10,11... | collective-permute-start | bytes 786440 | tf_op jit(solution)/shard_map/ppermute | solution.py:217
  33.5 3.7 %collective-permute-start.10 = (bf16[128,1024]{1,0:T(8,128)(2,1)S(1)}, bf16[128,1024]{1,0:T(8,128)(2,1)S(1)}, u32[]{:S(2)}, u32[]{:S(2)}) collective-permute-start(bf16[128,1024]{1,0:T(8,128)(2,1)S(1)} %collective-permute-done.2.refs_0_), channel_id=1, source_target_pairs={{0,1},{1,0},{2,3},{3,2},{4,5},{5,4},{6,7},{7,6},{8,9},{9,8},{10,11... | collective-permute-start | bytes 786440 | tf_op jit(solution)/shard_map/ppermute | solution.py:217

commit v4 on v3

--- a/solution.py
+++ b/solution.py
@@ -11,7 +11,7 @@
 HEAD_DIM = 64
 REACH = 6
 PAIRS = HEADS // 2
-GROUP = 2
+GROUP = 4
 WEIGHT = (3, 3, 3, 3, 3, 3)
 F32 = jnp.float32
 BF16 = jnp.bfloat16
@@ -38,7 +38,7 @@
         query_ref[pair, rows:, :] = jnp.where(lane >= HEAD_DIM, both, zero)
 
 
-def attend(normed, flags, w_key, w_value_t, query_ref, key_ref, value_ref, old, new):
+def attend(normed, flags, w_key, w_value_t, query_ref, key_ref, value_ref, old, new, after_pair=None):
     blocks = len(flags)
     rows = normed.shape[0] // blocks
     peak_ref, total_ref, numer_ref = new
@@ -85,7 +85,10 @@
             part = numer[HEAD_DIM * j : HEAD_DIM * (j + 1), lanes]
             if keep is not None:
                 part = old[2][head, :] * keep[:, lanes] + part
-            numer_ref[head, :] = part
+            if after_pair is None:
+                numer_ref[head, :] = part
+            else:
+                after_pair(pair, head, lanes, part)
 
     def project(group):
         span = slice(2 * HEAD_DIM * GROUP * group, 2 * HEAD_DIM * GROUP * (group + 1))
@@ -108,14 +111,13 @@
     gather_values(PAIRS - 1, *held)
 
 
-def finish(total_ref, numer_ref, gain_col, w_out, source, headed_ref):
-    rows = source.shape[0]
-    for pair in range(PAIRS):
-        for j in range(2):
-            head = slice((2 * pair + j) * HEAD_DIM, (2 * pair + j + 1) * HEAD_DIM)
-            attended = numer_ref[head, :] * (1.0 / total_ref[pair : pair + 1, rows * j : rows * (j + 1)])
-            mean_sq = jnp.mean(attended * attended, axis=0, keepdims=True)
-            headed_ref[head, :] = (attended * lax.rsqrt(mean_sq + 1e-06) * gain_col[head, :]).astype(BF16)
+def finish_head(total_ref, gain_col, headed_ref, pair, head, lanes, numer):
+    attended = numer * (1.0 / total_ref[pair : pair + 1, lanes])
+    mean_sq = jnp.mean(attended * attended, axis=0, keepdims=True)
+    headed_ref[head, :] = (attended * lax.rsqrt(mean_sq + 1e-06) * gain_col[head, :]).astype(BF16)
+
+
+def mix(headed_ref, w_out, source):
     update = lax.dot_general(headed_ref[...], w_out[...], BY_COLUMNS, preferred_element_type=F32)
     return (source.astype(F32) + update).astype(BF16)
 
@@ -178,7 +180,7 @@
     blocks = refs[: len(slots)]
     covis_list, covis_count, in_gain, w_key, w_value_t, query, peak, total, numer = refs[len(slots) : len(slots) + 9]
     out_gain, w_out, source, out = refs[len(slots) + 9 : len(slots) + 13]
-    new_peak, new_total, new_numer, headed, w_out_here, source_here, arrived, key, value = refs[len(slots) + 13 :]
+    new_peak, new_total, headed, w_out_here, source_here, arrived, key, value = refs[len(slots) + 13 :]
     copies = [
         pltpu.make_async_copy(w_out, w_out_here, arrived.at[0]),
         pltpu.make_async_copy(source, source_here, arrived.at[1]),
@@ -188,11 +190,12 @@
     attend(
         join_normed(blocks, in_gain), listed(owners, slots, covis_list, covis_count),
         w_key, w_value_t, query, key, value,
-        (peak, total, numer), (new_peak, new_total, new_numer),
+        (peak, total, numer), (new_peak, new_total, None),
+        functools.partial(finish_head, new_total, out_gain, headed),
     )
     for copy in copies:
         copy.wait()
-    out[...] = finish(new_total, new_numer, out_gain, w_out_here, source_here[...], headed)
+    out[...] = mix(headed, w_out_here, source_here[...])
 
 
 VMEM = pl.BlockSpec(memory_space=pltpu.VMEM)
@@ -334,7 +337,7 @@
             out_shape=jax.ShapeDtypeStruct((rows, width), BF16),
             in_specs=specs + [VMEM, HBM, HBM],
             out_specs=VMEM,
-            scratch_shapes=state_shapes
+            scratch_shapes=state_shapes[:2]
             + [pltpu.VMEM((width, rows), BF16), pltpu.VMEM(w_out.shape, BF16)]
             + [pltpu.VMEM(source.shape, BF16), pltpu.SemaphoreType.DMA((2,))]
             + scratch,

time: 42.2 us -> 42 us (level)
  no operation moved by 1% of the time
where the time goes in v4:
time: 42 us; the launch traced here: 41.8 us
  Pallas kernels  23.4 us (56%)
  starting transfers between devices  13.2 us (31%)
  waiting for transfers between devices  2.66 us (6%)
  local copies, waits for them, and re-layouts  1.56 us (4%)
  between operations  0.95 us (2%)
    pallas_call x4, Pallas kernels, call_later(): pl.pallas_call(functools.partial(later_kernel, slots, owners), out_shape=...  13.3 us
    ppermute x13, starting transfers between devices, swap(): lax.ppermute(block, axis, [(i, i ^ mask) for i in range(view_count)])  13.2 us
    pallas_call x1, Pallas kernels, on_device(): pl.pallas_call(functools.partial(first_kernel, owners, names[:1]), out_sh...  5.59 us
    pallas_call x1, Pallas kernels, call_later(): pl.pallas_call(functools.partial(last_kernel, slots, owners), out_shape=j...  4.48 us
    ppermute x13, waiting for transfers between devices, swap(): lax.ppermute(block, axis, [(i, i ^ mask) for i in range(view_count)])  2.66 us
    reshape x1, local copies, waits for them, and re-layouts, on_device(): gain_col = out_gain.reshape(width, 1)  0.9 us
  transfers between devices with their start and end apart: 13, of which 2 were waited for; matrix products, arithmetic and copies ran while one was open for 2% of the time, Pallas kernels for 45%

profile of v4, /device:TPU:1, one launch (start us, length us, event | category | flops | bytes accessed | tf_op | source)
XLA Modules:
  0.0 41.8 jit_solution(10719901029375846627)
XLA Ops:
  0.0 0.1 collective-permute-start.1
  0.1 4.7 %collective-permute-start = (bf16[128,1024]{1,0:T(8,128)(2,1)}, bf16[128,1024]{1,0:T(8,128)(2,1)S(1)}, u32[]{:S(2)}, u32[]{:S(2)}) collective-permute-start(bf16[128,1024]{1,0:T(8,128)(2,1)} %bitcast.12), channel_id=1, source_target_pairs={{0,10},{1,11},{2,8},{3,9},{4,14},{5,15},{6,12},{7,13},{8,2},{9,3},... | collective-permute-start | bytes 786440 | tf_op jit(solution)/shard_map/ppermute | solution.py:220
  4.8 0.2 collective-permute-start.3
  5.0 1.3 %collective-permute-start.4 = (bf16[128,1024]{1,0:T(8,128)(2,1)}, bf16[128,1024]{1,0:T(8,128)(2,1)S(1)}, u32[]{:S(2)}, u32[]{:S(2)}) collective-permute-start(bf16[128,1024]{1,0:T(8,128)(2,1)} %bitcast.14), channel_id=1, source_target_pairs={{0,4},{1,5},{2,6},{3,7},{4,0},{5,1},{6,2},{7,3},{8,12},{9,13},{10,... | collective-permute-start | bytes 786440 | tf_op jit(solution)/shard_map/ppermute | solution.py:220
  6.9 0.9 %copy.10.refs_11_ = f32[1024,1]{1,0:T(8,128)S(1)} copy(f32[1024,1]{0,1:T(1,128)} %bitcast.10) | data formatting | bytes 8192 | tf_op jit(solution)/shard_map/reshape | solution.py:305
  7.9 0.0 collective-permute-done.1.other
  7.9 0.0 copy-start.1
  7.9 0.6 %copy-done.1 = s32[1,12]{1,0:T(1,128)S(1)} copy-done((s32[1,12]{1,0:T(1,128)S(1)}, s32[1,12]{1,0:T(1,128)}, u32[]{:S(2)}) %copy-start.1) | copy-done | bytes 72
  8.5 0.0 copy-start
  8.5 5.6 %shard_map.91 = (bf16[8,256,128]{2,1,0:T(8,128)(2,1)S(1)}, f32[8,256]{1,0:T(8,128)S(1)}, f32[8,256]{1,0:T(8,128)S(1)}, f32[1024,128]{1,0:T(8,128)S(1)}, bf16[102...) custom-call(bf16[128,1024]{1,0:T(8,128)(2,1)} %bitcast.15, bf16[128,1024]{1,0:T(8,128)(2,1)S(1)} %collective-permute-done.1.other, ...), custom_call_target="tpu_custom_call" | custom-call | flops 4026531840 | bytes 524288 | tf_op jit(solution)/shard_map/pallas_call | solution.py:349
  14.1 2.4 %collective-permute-done.4.refs_1_ = bf16[128,1024]{1,0:T(8,128)(2,1)S(1)} collective-permute-done((bf16[128,1024]{1,0:T(8,128)(2,1)}, bf16[128,1024]{1,0:T(8,128)(2,1)S(1)}, u32[]{:S(2)}, u32[]{:S(2)}) %collective-permute-start.4) | collective-permute-done | bytes 262176 | tf_op jit(solution)/shard_map/ppermute | solution.py:220
  16.5 1.8 %collective-permute-start.6 = (bf16[128,1024]{1,0:T(8,128)(2,1)S(1)}, bf16[128,1024]{1,0:T(8,128)(2,1)S(1)}, u32[]{:S(2)}, u32[]{:S(2)}) collective-permute-start(bf16[128,1024]{1,0:T(8,128)(2,1)S(1)} %collective-permute-done.4.refs_1_), channel_id=1, source_target_pairs={{0,2},{1,3},{2,0},{3,1},{4,6},{5,7},{6,4},{7,5},{8,10},{9,11},{10,... | collective-permute-start | bytes 786440 | tf_op jit(solution)/shard_map/ppermute | solution.py:220
  18.3 1.7 %collective-permute-start.9 = (bf16[128,1024]{1,0:T(8,128)(2,1)S(1)}, bf16[128,1024]{1,0:T(8,128)(2,1)S(1)}, u32[]{:S(2)}, u32[]{:S(2)}) collective-permute-start(bf16[128,1024]{1,0:T(8,128)(2,1)S(1)} %collective-permute-done.4.refs_1_), channel_id=1, source_target_pairs={{0,1},{1,0},{2,3},{3,2},{4,5},{5,4},{6,7},{7,6},{8,9},{9,8},{10,11... | collective-permute-start | bytes 786440 | tf_op jit(solution)/shard_map/ppermute | solution.py:220
  20.0 0.0 collective-permute-done.refs_2_
  20.0 0.0 collective-permute-start.11
  20.0 1.4 %collective-permute-start.2 = (bf16[128,1024]{1,0:T(8,128)(2,1)S(1)}, bf16[128,1024]{1,0:T(8,128)(2,1)S(1)}, u32[]{:S(2)}, u32[]{:S(2)}) collective-permute-start(bf16[128,1024]{1,0:T(8,128)(2,1)S(1)} %collective-permute-done.refs_2_), channel_id=1, source_target_pairs={{0,6},{1,7},{2,4},{3,5},{4,2},{5,3},{6,0},{7,1},{8,14},{9,15},{10,... | collective-permute-start | bytes 786440 | tf_op jit(solution)/shard_map/ppermute | solution.py:220
  21.4 0.0 collective-permute-done.3.refs_0_
  21.4 0.6 %collective-permute-start.8 = (bf16[128,1024]{1,0:T(8,128)(2,1)S(1)}, bf16[128,1024]{1,0:T(8,128)(2,1)S(1)}, u32[]{:S(2)}, u32[]{:S(2)}) collective-permute-start(bf16[128,1024]{1,0:T(8,128)(2,1)S(1)} %collective-permute-done.3.refs_0_), channel_id=1, source_target_pairs={{0,1},{1,0},{2,3},{3,2},{4,5},{5,4},{6,7},{7,6},{8,9},{9,8},{10,11... | collective-permute-start | bytes 786440 | tf_op jit(solution)/shard_map/ppermute | solution.py:220
  21.9 0.0 copy-done
  21.9 3.9 %shard_map.92 = (f32[8,256]{1,0:T(8,128)S(1)}, f32[8,256]{1,0:T(8,128)S(1)}, f32[1024,128]{1,0:T(8,128)S(1)}) custom-call(bf16[128,1024]{1,0:T(8,128)(2,1)S(1)} %collective-permute-done.3.refs_0_, bf16[128,1024]{1,0:T(8,128)(2,1)S(1)} %collective-permute-done.4.refs_1_, bf16[128,1024]{1,0:T(8,128)(2,1)S(1)} %collective-permute-done.refs_2_, ...), custom_call_target="tpu_custom_call" | custom-call | flops 6039797760 | bytes 786432 | tf_op jit(solution)/shard_map/pallas_call | solution.py:326
  25.8 0.0 collective-permute-done.6.refs_2_
  25.8 0.1 collective-permute-start.5
  25.9 0.0 collective-permute-done.9.refs_1_
  25.9 0.5 %collective-permute-start.7 = (bf16[128,1024]{1,0:T(8,128)(2,1)S(1)}, bf16[128,1024]{1,0:T(8,128)(2,1)S(1)}, u32[]{:S(2)}, u32[]{:S(2)}) collective-permute-start(bf16[128,1024]{1,0:T(8,128)(2,1)S(1)} %collective-permute-done.6.refs_2_), channel_id=1, source_target_pairs={{0,1},{1,0},{2,3},{3,2},{4,5},{5,4},{6,7},{7,6},{8,9},{9,8},{10,11... | collective-permute-start | bytes 786440 | tf_op jit(solution)/shard_map/ppermute | solution.py:220
  26.4 0.0 collective-permute-done.8.refs_0_
  26.4 3.9 %shard_map.93 = (f32[8,256]{1,0:T(8,128)S(1)}, f32[8,256]{1,0:T(8,128)S(1)}, f32[1024,128]{1,0:T(8,128)S(1)}) custom-call(bf16[128,1024]{1,0:T(8,128)(2,1)S(1)} %collective-permute-done.8.refs_0_, bf16[128,1024]{1,0:T(8,128)(2,1)S(1)} %collective-permute-done.9.refs_1_, bf16[128,1024]{1,0:T(8,128)(2,1)S(1)} %collective-permute-done.6.refs_2_, ...), custom_call_target="tpu_custom_call" | custom-call | flops 6039797760 | bytes 786432 | tf_op jit(solution)/shard_map/pallas_call | solution.py:326
  30.3 0.0 collective-permute-done.5.refs_0_
  30.3 0.0 collective-permute-done.7.refs_1_
  30.3 2.7 %shard_map.94 = (f32[8,256]{1,0:T(8,128)S(1)}, f32[8,256]{1,0:T(8,128)S(1)}, f32[1024,128]{1,0:T(8,128)S(1)}) custom-call(bf16[128,1024]{1,0:T(8,128)(2,1)S(1)} %collective-permute-done.5.refs_0_, bf16[128,1024]{1,0:T(8,128)(2,1)S(1)} %collective-permute-done.7.refs_1_, s32[1,12]{1,0:T(1,128)S(1)} %copy-done.1, s32[1]{0:T(128)S(6)} %copy.11.covis_count.refs_4_.refs_3_, ...), custom_call_target="tpu_custom_call" | custom-call | flops 4026531840 | bytes 524288 | tf_op jit(solution)/shard_map/pallas_call | solution.py:326
  33.0 0.0 collective-permute-done.11.refs_1_
  33.0 0.1 collective-permute-start.12
  33.2 0.3 collective-permute-done.2.refs_0_
  33.5 0.8 %collective-permute-start.10 = (bf16[128,1024]{1,0:T(8,128)(2,1)S(1)}, bf16[128,1024]{1,0:T(8,128)(2,1)S(1)}, u32[]{:S(2)}, u32[]{:S(2)}) collective-permute-start(bf16[128,1024]{1,0:T(8,128)(2,1)S(1)} %collective-permute-done.2.refs_0_), channel_id=1, source_target_pairs={{0,1},{1,0},{2,3},{3,2},{4,5},{5,4},{6,7},{7,6},{8,9},{9,8},{10,11... | collective-permute-start | bytes 786440 | tf_op jit(solution)/shard_map/ppermute | solution.py:220
  34.2 2.9 %shard_map.95 = (f32[8,256]{1,0:T(8,128)S(1)}, f32[8,256]{1,0:T(8,128)S(1)}, f32[1024,128]{1,0:T(8,128)S(1)}) custom-call(bf16[128,1024]{1,0:T(8,128)(2,1)S(1)} %collective-permute-done.2.refs_0_, bf16[128,1024]{1,0:T(8,128)(2,1)S(1)} %collective-permute-done.11.refs_1_, s32[1,12]{1,0:T(1,128)S(1)} %copy-done.1, s32[1]{0:T(128)S(6)} %copy.11.covis_count.refs_4_.refs_3_, ...), custom_call_target="tpu_custom_call" | custom-call | flops 4026531840 | bytes 524288 | tf_op jit(solution)/shard_map/pallas_call | solution.py:326
  37.1 0.0 collective-permute-done.12.refs_1_
  37.2 0.0 collective-permute-done.10.refs_0_
  37.2 4.5 %shard_map.96 = bf16[128,1024]{1,0:T(8,128)(2,1)} custom-call(bf16[128,1024]{1,0:T(8,128)(2,1)S(1)} %collective-permute-done.10.refs_0_, bf16[128,1024]{1,0:T(8,128)(2,1)S(1)} %collective-permute-done.12.refs_1_, s32[1,12]{1,0:T(1,128)S(1)} %copy-done.1, s32[1]{0:T(128)S(6)} %copy.11.covis_count.refs_4_.refs_3_, f32[1,1024]{1,0:T(1,128)S(1)} %bitcast.9, ...), custom_call_target="tpu_custom_call" | custom-call | flops 4026531840 | bytes 524288 | tf_op jit(solution)/shard_map/pallas_call | solution.py:335
Async XLA Ops:
  0.0 7.9 %collective-permute-start.1 = (bf16[128,1024]{1,0:T(8,128)(2,1)}, bf16[128,1024]{1,0:T(8,128)(2,1)S(1)}, u32[]{:S(2)}, u32[]{:S(2)}) collective-permute-start(bf16[128,1024]{1,0:T(8,128)(2,1)} %bitcast.11), channel_id=1, source_target_pairs={{0,1},{1,0},{2,3},{3,2},{4,5},{5,4},{6,7},{7,6},{8,9},{9,8},{10,11... | collective-permute-start | bytes 786440 | tf_op jit(solution)/shard_map/ppermute | solution.py:220
  0.1 19.9 %collective-permute-start = (bf16[128,1024]{1,0:T(8,128)(2,1)}, bf16[128,1024]{1,0:T(8,128)(2,1)S(1)}, u32[]{:S(2)}, u32[]{:S(2)}) collective-permute-start(bf16[128,1024]{1,0:T(8,128)(2,1)} %bitcast.12), channel_id=1, source_target_pairs={{0,10},{1,11},{2,8},{3,9},{4,14},{5,15},{6,12},{7,13},{8,2},{9,3},... | collective-permute-start | bytes 786440 | tf_op jit(solution)/shard_map/ppermute | solution.py:220
  4.8 16.6 %collective-permute-start.3 = (bf16[128,1024]{1,0:T(8,128)(2,1)}, bf16[128,1024]{1,0:T(8,128)(2,1)S(1)}, u32[]{:S(2)}, u32[]{:S(2)}) collective-permute-start(bf16[128,1024]{1,0:T(8,128)(2,1)} %bitcast.13), channel_id=1, source_target_pairs={{0,2},{1,3},{2,0},{3,1},{4,6},{5,7},{6,4},{7,5},{8,10},{9,11},{10,... | collective-permute-start | bytes 786440 | tf_op jit(solution)/shard_map/ppermute | solution.py:220
  5.0 11.5 %collective-permute-start.4 = (bf16[128,1024]{1,0:T(8,128)(2,1)}, bf16[128,1024]{1,0:T(8,128)(2,1)S(1)}, u32[]{:S(2)}, u32[]{:S(2)}) collective-permute-start(bf16[128,1024]{1,0:T(8,128)(2,1)} %bitcast.14), channel_id=1, source_target_pairs={{0,4},{1,5},{2,6},{3,7},{4,0},{5,1},{6,2},{7,3},{8,12},{9,13},{10,... | collective-permute-start | bytes 786440 | tf_op jit(solution)/shard_map/ppermute | solution.py:220
  7.9 0.7 %copy-start.1 = (s32[1,12]{1,0:T(1,128)S(1)}, s32[1,12]{1,0:T(1,128)}, u32[]{:S(2)}) copy-start(s32[1,12]{1,0:T(1,128)} %refs_2_.5) | copy-start | bytes 148
  8.5 13.4 %copy-start = (f32[1024]{0:T(1024)S(1)}, f32[1024]{0:T(1024)}, u32[]{:S(2)}) copy-start(f32[1024]{0:T(1024)} %param.10) | copy-start | bytes 12292
  16.5 9.3 %collective-permute-start.6 = (bf16[128,1024]{1,0:T(8,128)(2,1)S(1)}, bf16[128,1024]{1,0:T(8,128)(2,1)S(1)}, u32[]{:S(2)}, u32[]{:S(2)}) collective-permute-start(bf16[128,1024]{1,0:T(8,128)(2,1)S(1)} %collective-permute-done.4.refs_1_), channel_id=1, source_target_pairs={{0,2},{1,3},{2,0},{3,1},{4,6},{5,7},{6,4},{7,5},{8,10},{9,11},{10,... | collective-permute-start | bytes 786440 | tf_op jit(solution)/shard_map/ppermute | solution.py:220
  18.3 7.7 %collective-permute-start.9 = (bf16[128,1024]{1,0:T(8,128)(2,1)S(1)}, bf16[128,1024]{1,0:T(8,128)(2,1)S(1)}, u32[]{:S(2)}, u32[]{:S(2)}) collective-permute-start(bf16[128,1024]{1,0:T(8,128)(2,1)S(1)} %collective-permute-done.4.refs_1_), channel_id=1, source_target_pairs={{0,1},{1,0},{2,3},{3,2},{4,5},{5,4},{6,7},{7,6},{8,9},{9,8},{10,11... | collective-permute-start | bytes 786440 | tf_op jit(solution)/shard_map/ppermute | solution.py:220
  20.0 13.1 %collective-permute-start.11 = (bf16[128,1024]{1,0:T(8,128)(2,1)S(1)}, bf16[128,1024]{1,0:T(8,128)(2,1)S(1)}, u32[]{:S(2)}, u32[]{:S(2)}) collective-permute-start(bf16[128,1024]{1,0:T(8,128)(2,1)S(1)} %collective-permute-done.refs_2_), channel_id=1, source_target_pairs={{0,4},{1,5},{2,6},{3,7},{4,0},{5,1},{6,2},{7,3},{8,12},{9,13},{10,... | collective-permute-start | bytes 786440 | tf_op jit(solution)/shard_map/ppermute | solution.py:220
  20.0 13.5 %collective-permute-start.2 = (bf16[128,1024]{1,0:T(8,128)(2,1)S(1)}, bf16[128,1024]{1,0:T(8,128)(2,1)S(1)}, u32[]{:S(2)}, u32[]{:S(2)}) collective-permute-start(bf16[128,1024]{1,0:T(8,128)(2,1)S(1)} %collective-permute-done.refs_2_), channel_id=1, source_target_pairs={{0,6},{1,7},{2,4},{3,5},{4,2},{5,3},{6,0},{7,1},{8,14},{9,15},{10,... | collective-permute-start | bytes 786440 | tf_op jit(solution)/shard_map/ppermute | solution.py:220
  21.4 5.0 %collective-permute-start.8 = (bf16[128,1024]{1,0:T(8,128)(2,1)S(1)}, bf16[128,1024]{1,0:T(8,128)(2,1)S(1)}, u32[]{:S(2)}, u32[]{:S(2)}) collective-permute-start(bf16[128,1024]{1,0:T(8,128)(2,1)S(1)} %collective-permute-done.3.refs_0_), channel_id=1, source_target_pairs={{0,1},{1,0},{2,3},{3,2},{4,5},{5,4},{6,7},{7,6},{8,9},{9,8},{10,11... | collective-permute-start | bytes 786440 | tf_op jit(solution)/shard_map/ppermute | solution.py:220
  25.8 4.5 %collective-permute-start.5 = (bf16[128,1024]{1,0:T(8,128)(2,1)S(1)}, bf16[128,1024]{1,0:T(8,128)(2,1)S(1)}, u32[]{:S(2)}, u32[]{:S(2)}) collective-permute-start(bf16[128,1024]{1,0:T(8,128)(2,1)S(1)} %collective-permute-done.refs_2_), channel_id=1, source_target_pairs={{0,1},{1,0},{2,3},{3,2},{4,5},{5,4},{6,7},{7,6},{8,9},{9,8},{10,11... | collective-permute-start | bytes 786440 | tf_op jit(solution)/shard_map/ppermute | solution.py:220
  25.9 4.4 %collective-permute-start.7 = (bf16[128,1024]{1,0:T(8,128)(2,1)S(1)}, bf16[128,1024]{1,0:T(8,128)(2,1)S(1)}, u32[]{:S(2)}, u32[]{:S(2)}) collective-permute-start(bf16[128,1024]{1,0:T(8,128)(2,1)S(1)} %collective-permute-done.6.refs_2_), channel_id=1, source_target_pairs={{0,1},{1,0},{2,3},{3,2},{4,5},{5,4},{6,7},{7,6},{8,9},{9,8},{10,11... | collective-permute-start | bytes 786440 | tf_op jit(solution)/shard_map/ppermute | solution.py:220
  33.0 4.1 %collective-permute-start.12 = (bf16[128,1024]{1,0:T(8,128)(2,1)S(1)}, bf16[128,1024]{1,0:T(8,128)(2,1)S(1)}, u32[]{:S(2)}, u32[]{:S(2)}) collective-permute-start(bf16[128,1024]{1,0:T(8,128)(2,1)S(1)} %collective-permute-done.11.refs_1_), channel_id=1, source_target_pairs={{0,1},{1,0},{2,3},{3,2},{4,5},{5,4},{6,7},{7,6},{8,9},{9,8},{10,11... | collective-permute-start | bytes 786440 | tf_op jit(solution)/shard_map/ppermute | solution.py:220
  33.5 3.7 %collective-permute-start.10 = (bf16[128,1024]{1,0:T(8,128)(2,1)S(1)}, bf16[128,1024]{1,0:T(8,128)(2,1)S(1)}, u32[]{:S(2)}, u32[]{:S(2)}) collective-permute-start(bf16[128,1024]{1,0:T(8,128)(2,1)S(1)} %collective-permute-done.2.refs_0_), channel_id=1, source_target_pairs={{0,1},{1,0},{2,3},{3,2},{4,5},{5,4},{6,7},{7,6},{8,9},{9,8},{10,11... | collective-permute-start | bytes 786440 | tf_op jit(solution)/shard_map/ppermute | solution.py:220

commit v5 on v4

--- a/solution.py
+++ b/solution.py
@@ -239,8 +239,8 @@
             got[12] = swap(6)(after(got[10]))
             got[14] = swap(4)(after(got[10]))
             got[6] = swap(2)(after(got[4]))
-            for mask in (4, 2):
-                got[mask ^ 1] = swap(1)(after(got[mask]))
+            got[5] = swap(1)(after(got[4]))
+            got[3] = swap(1)(tie(after(got[2]), got[4]))
 
         def third(got, after):
             for mask in (10, 6):

time: 42 us -> 41.8 us (level)
  transfers between devices with their start and end apart: 13 -> 13, of which waited for: 2 -> 2; matrix products, arithmetic and copies ran while one was open for 2% -> 2% of each run, Pallas kernels for 45% -> 46%
where the time goes in v5:
time: 41.8 us; the launch traced here: 41.6 us
  Pallas kernels  23.4 us (56%)
  starting transfers between devices  13 us (31%)
  waiting for transfers between devices  2.66 us (6%)
  local copies, waits for them, and re-layouts  1.56 us (4%)
  between operations  0.95 us (2%)
    pallas_call x4, Pallas kernels, call_later(): pl.pallas_call(functools.partial(later_kernel, slots, owners), out_shape=...  13.3 us
    ppermute x13, starting transfers between devices, swap(): lax.ppermute(block, axis, [(i, i ^ mask) for i in range(view_count)])  13 us
    pallas_call x1, Pallas kernels, on_device(): pl.pallas_call(functools.partial(first_kernel, owners, names[:1]), out_sh...  5.59 us
    pallas_call x1, Pallas kernels, call_later(): pl.pallas_call(functools.partial(last_kernel, slots, owners), out_shape=j...  4.48 us
    ppermute x13, waiting for transfers between devices, swap(): lax.ppermute(block, axis, [(i, i ^ mask) for i in range(view_count)])  2.66 us
    reshape x1, local copies, waits for them, and re-layouts, on_device(): gain_col = out_gain.reshape(width, 1)  0.9 us
  transfers between devices with their start and end apart: 13, of which 2 were waited for; matrix products, arithmetic and copies ran while one was open for 2% of the time, Pallas kernels for 46%

profile of v5, /device:TPU:1, one launch (start us, length us, event | category | flops | bytes accessed | tf_op | source)
XLA Modules:
  0.0 41.6 jit_solution(15995091726693329773)
XLA Ops:
  0.0 0.1 collective-permute-start.1
  0.1 4.7 %collective-permute-start = (bf16[128,1024]{1,0:T(8,128)(2,1)}, bf16[128,1024]{1,0:T(8,128)(2,1)S(1)}, u32[]{:S(2)}, u32[]{:S(2)}) collective-permute-start(bf16[128,1024]{1,0:T(8,128)(2,1)} %bitcast.12), channel_id=1, source_target_pairs={{0,10},{1,11},{2,8},{3,9},{4,14},{5,15},{6,12},{7,13},{8,2},{9,3},... | collective-permute-start | bytes 786440 | tf_op jit(solution)/shard_map/ppermute | solution.py:220
  4.8 1.3 %collective-permute-start.4 = (bf16[128,1024]{1,0:T(8,128)(2,1)}, bf16[128,1024]{1,0:T(8,128)(2,1)S(1)}, u32[]{:S(2)}, u32[]{:S(2)}) collective-permute-start(bf16[128,1024]{1,0:T(8,128)(2,1)} %bitcast.13), channel_id=1, source_target_pairs={{0,4},{1,5},{2,6},{3,7},{4,0},{5,1},{6,2},{7,3},{8,12},{9,13},{10,... | collective-permute-start | bytes 786440 | tf_op jit(solution)/shard_map/ppermute | solution.py:220
  6.1 0.2 collective-permute-start.3
  6.9 0.9 %copy.10.refs_11_ = f32[1024,1]{1,0:T(8,128)S(1)} copy(f32[1024,1]{0,1:T(1,128)} %bitcast.10) | data formatting | bytes 8192 | tf_op jit(solution)/shard_map/reshape | solution.py:305
  7.9 0.0 collective-permute-done.1.other
  7.9 0.0 copy-start.1
  7.9 0.6 %copy-done.1 = s32[1,12]{1,0:T(1,128)S(1)} copy-done((s32[1,12]{1,0:T(1,128)S(1)}, s32[1,12]{1,0:T(1,128)}, u32[]{:S(2)}) %copy-start.1) | copy-done | bytes 72
  8.5 0.0 copy-start
  8.5 5.6 %shard_map.91 = (bf16[8,256,128]{2,1,0:T(8,128)(2,1)S(1)}, f32[8,256]{1,0:T(8,128)S(1)}, f32[8,256]{1,0:T(8,128)S(1)}, f32[1024,128]{1,0:T(8,128)S(1)}, bf16[102...) custom-call(bf16[128,1024]{1,0:T(8,128)(2,1)} %bitcast.15, bf16[128,1024]{1,0:T(8,128)(2,1)S(1)} %collective-permute-done.1.other, ...), custom_call_target="tpu_custom_call" | custom-call | flops 4026531840 | bytes 524288 | tf_op jit(solution)/shard_map/pallas_call | solution.py:349
  14.1 2.4 %collective-permute-done.4.refs_1_ = bf16[128,1024]{1,0:T(8,128)(2,1)S(1)} collective-permute-done((bf16[128,1024]{1,0:T(8,128)(2,1)}, bf16[128,1024]{1,0:T(8,128)(2,1)S(1)}, u32[]{:S(2)}, u32[]{:S(2)}) %collective-permute-start.4) | collective-permute-done | bytes 262176 | tf_op jit(solution)/shard_map/ppermute | solution.py:220
  16.5 0.2 collective-permute-start.6
  16.7 2.0 %collective-permute-start.9 = (bf16[128,1024]{1,0:T(8,128)(2,1)S(1)}, bf16[128,1024]{1,0:T(8,128)(2,1)S(1)}, u32[]{:S(2)}, u32[]{:S(2)}) collective-permute-start(bf16[128,1024]{1,0:T(8,128)(2,1)S(1)} %collective-permute-done.4.refs_1_), channel_id=1, source_target_pairs={{0,1},{1,0},{2,3},{3,2},{4,5},{5,4},{6,7},{7,6},{8,9},{9,8},{10,11... | collective-permute-start | bytes 786440 | tf_op jit(solution)/shard_map/ppermute | solution.py:220
  18.7 0.0 collective-permute-done.refs_2_
  18.7 1.2 %collective-permute-start.11 = (bf16[128,1024]{1,0:T(8,128)(2,1)S(1)}, bf16[128,1024]{1,0:T(8,128)(2,1)S(1)}, u32[]{:S(2)}, u32[]{:S(2)}) collective-permute-start(bf16[128,1024]{1,0:T(8,128)(2,1)S(1)} %collective-permute-done.refs_2_), channel_id=1, source_target_pairs={{0,4},{1,5},{2,6},{3,7},{4,0},{5,1},{6,2},{7,3},{8,12},{9,13},{10,... | collective-permute-start | bytes 786440 | tf_op jit(solution)/shard_map/ppermute | solution.py:220
  19.9 1.3 %collective-permute-start.2 = (bf16[128,1024]{1,0:T(8,128)(2,1)S(1)}, bf16[128,1024]{1,0:T(8,128)(2,1)S(1)}, u32[]{:S(2)}, u32[]{:S(2)}) collective-permute-start(bf16[128,1024]{1,0:T(8,128)(2,1)S(1)} %collective-permute-done.refs_2_), channel_id=1, source_target_pairs={{0,6},{1,7},{2,4},{3,5},{4,2},{5,3},{6,0},{7,1},{8,14},{9,15},{10,... | collective-permute-start | bytes 786440 | tf_op jit(solution)/shard_map/ppermute | solution.py:220
  21.1 0.0 collective-permute-done.3.refs_0_
  21.1 0.6 %collective-permute-start.8 = (bf16[128,1024]{1,0:T(8,128)(2,1)S(1)}, bf16[128,1024]{1,0:T(8,128)(2,1)S(1)}, u32[]{:S(2)}, u32[]{:S(2)}) collective-permute-start(bf16[128,1024]{1,0:T(8,128)(2,1)S(1)} %collective-permute-done.3.refs_0_), channel_id=1, source_target_pairs={{0,1},{1,0},{2,3},{3,2},{4,5},{5,4},{6,7},{7,6},{8,9},{9,8},{10,11... | collective-permute-start | bytes 786440 | tf_op jit(solution)/shard_map/ppermute | solution.py:220
  21.7 0.0 copy-done
  21.7 3.9 %shard_map.92 = (f32[8,256]{1,0:T(8,128)S(1)}, f32[8,256]{1,0:T(8,128)S(1)}, f32[1024,128]{1,0:T(8,128)S(1)}) custom-call(bf16[128,1024]{1,0:T(8,128)(2,1)S(1)} %collective-permute-done.3.refs_0_, bf16[128,1024]{1,0:T(8,128)(2,1)S(1)} %collective-permute-done.4.refs_1_, bf16[128,1024]{1,0:T(8,128)(2,1)S(1)} %collective-permute-done.refs_2_, ...), custom_call_target="tpu_custom_call" | custom-call | flops 6039797760 | bytes 786432 | tf_op jit(solution)/shard_map/pallas_call | solution.py:326
  25.6 0.0 collective-permute-done.6.refs_2_
  25.6 0.1 collective-permute-start.5
  25.7 0.0 collective-permute-done.8.refs_0_
  25.7 0.5 %collective-permute-start.7 = (bf16[128,1024]{1,0:T(8,128)(2,1)S(1)}, bf16[128,1024]{1,0:T(8,128)(2,1)S(1)}, u32[]{:S(2)}, u32[]{:S(2)}) collective-permute-start(bf16[128,1024]{1,0:T(8,128)(2,1)S(1)} %collective-permute-done.6.refs_2_), channel_id=1, source_target_pairs={{0,1},{1,0},{2,3},{3,2},{4,5},{5,4},{6,7},{7,6},{8,9},{9,8},{10,11... | collective-permute-start | bytes 786440 | tf_op jit(solution)/shard_map/ppermute | solution.py:220
  26.2 0.0 collective-permute-done.9.refs_1_
  26.2 3.9 %shard_map.93 = (f32[8,256]{1,0:T(8,128)S(1)}, f32[8,256]{1,0:T(8,128)S(1)}, f32[1024,128]{1,0:T(8,128)S(1)}) custom-call(bf16[128,1024]{1,0:T(8,128)(2,1)S(1)} %collective-permute-done.8.refs_0_, bf16[128,1024]{1,0:T(8,128)(2,1)S(1)} %collective-permute-done.9.refs_1_, bf16[128,1024]{1,0:T(8,128)(2,1)S(1)} %collective-permute-done.6.refs_2_, ...), custom_call_target="tpu_custom_call" | custom-call | flops 6039797760 | bytes 786432 | tf_op jit(solution)/shard_map/pallas_call | solution.py:326
  30.1 0.0 collective-permute-done.5.refs_0_
  30.1 0.0 collective-permute-done.7.refs_1_
  30.1 2.7 %shard_map.94 = (f32[8,256]{1,0:T(8,128)S(1)}, f32[8,256]{1,0:T(8,128)S(1)}, f32[1024,128]{1,0:T(8,128)S(1)}) custom-call(bf16[128,1024]{1,0:T(8,128)(2,1)S(1)} %collective-permute-done.5.refs_0_, bf16[128,1024]{1,0:T(8,128)(2,1)S(1)} %collective-permute-done.7.refs_1_, s32[1,12]{1,0:T(1,128)S(1)} %copy-done.1, s32[1]{0:T(128)S(6)} %copy.11.covis_count.refs_4_.refs_3_, ...), custom_call_target="tpu_custom_call" | custom-call | flops 4026531840 | bytes 524288 | tf_op jit(solution)/shard_map/pallas_call | solution.py:326
  32.8 0.0 collective-permute-done.11.refs_1_
  32.8 0.1 collective-permute-start.12
  33.0 0.3 collective-permute-done.2.refs_0_
  33.2 0.8 %collective-permute-start.10 = (bf16[128,1024]{1,0:T(8,128)(2,1)S(1)}, bf16[128,1024]{1,0:T(8,128)(2,1)S(1)}, u32[]{:S(2)}, u32[]{:S(2)}) collective-permute-start(bf16[128,1024]{1,0:T(8,128)(2,1)S(1)} %collective-permute-done.2.refs_0_), channel_id=1, source_target_pairs={{0,1},{1,0},{2,3},{3,2},{4,5},{5,4},{6,7},{7,6},{8,9},{9,8},{10,11... | collective-permute-start | bytes 786440 | tf_op jit(solution)/shard_map/ppermute | solution.py:220
  34.0 2.9 %shard_map.95 = (f32[8,256]{1,0:T(8,128)S(1)}, f32[8,256]{1,0:T(8,128)S(1)}, f32[1024,128]{1,0:T(8,128)S(1)}) custom-call(bf16[128,1024]{1,0:T(8,128)(2,1)S(1)} %collective-permute-done.2.refs_0_, bf16[128,1024]{1,0:T(8,128)(2,1)S(1)} %collective-permute-done.11.refs_1_, s32[1,12]{1,0:T(1,128)S(1)} %copy-done.1, s32[1]{0:T(128)S(6)} %copy.11.covis_count.refs_4_.refs_3_, ...), custom_call_target="tpu_custom_call" | custom-call | flops 4026531840 | bytes 524288 | tf_op jit(solution)/shard_map/pallas_call | solution.py:326
  36.9 0.0 collective-permute-done.12.refs_1_
  36.9 0.0 collective-permute-done.10.refs_0_
  36.9 4.5 %shard_map.96 = bf16[128,1024]{1,0:T(8,128)(2,1)} custom-call(bf16[128,1024]{1,0:T(8,128)(2,1)S(1)} %collective-permute-done.10.refs_0_, bf16[128,1024]{1,0:T(8,128)(2,1)S(1)} %collective-permute-done.12.refs_1_, s32[1,12]{1,0:T(1,128)S(1)} %copy-done.1, s32[1]{0:T(128)S(6)} %copy.11.covis_count.refs_4_.refs_3_, f32[1,1024]{1,0:T(1,128)S(1)} %bitcast.9, ...), custom_call_target="tpu_custom_call" | custom-call | flops 4026531840 | bytes 524288 | tf_op jit(solution)/shard_map/pallas_call | solution.py:335
Async XLA Ops:
  0.0 7.9 %collective-permute-start.1 = (bf16[128,1024]{1,0:T(8,128)(2,1)}, bf16[128,1024]{1,0:T(8,128)(2,1)S(1)}, u32[]{:S(2)}, u32[]{:S(2)}) collective-permute-start(bf16[128,1024]{1,0:T(8,128)(2,1)} %bitcast.11), channel_id=1, source_target_pairs={{0,1},{1,0},{2,3},{3,2},{4,5},{5,4},{6,7},{7,6},{8,9},{9,8},{10,11... | collective-permute-start | bytes 786440 | tf_op jit(solution)/shard_map/ppermute | solution.py:220
  0.1 18.7 %collective-permute-start = (bf16[128,1024]{1,0:T(8,128)(2,1)}, bf16[128,1024]{1,0:T(8,128)(2,1)S(1)}, u32[]{:S(2)}, u32[]{:S(2)}) collective-permute-start(bf16[128,1024]{1,0:T(8,128)(2,1)} %bitcast.12), channel_id=1, source_target_pairs={{0,10},{1,11},{2,8},{3,9},{4,14},{5,15},{6,12},{7,13},{8,2},{9,3},... | collective-permute-start | bytes 786440 | tf_op jit(solution)/shard_map/ppermute | solution.py:220
  4.8 11.7 %collective-permute-start.4 = (bf16[128,1024]{1,0:T(8,128)(2,1)}, bf16[128,1024]{1,0:T(8,128)(2,1)S(1)}, u32[]{:S(2)}, u32[]{:S(2)}) collective-permute-start(bf16[128,1024]{1,0:T(8,128)(2,1)} %bitcast.13), channel_id=1, source_target_pairs={{0,4},{1,5},{2,6},{3,7},{4,0},{5,1},{6,2},{7,3},{8,12},{9,13},{10,... | collective-permute-start | bytes 786440 | tf_op jit(solution)/shard_map/ppermute | solution.py:220
  6.1 15.1 %collective-permute-start.3 = (bf16[128,1024]{1,0:T(8,128)(2,1)}, bf16[128,1024]{1,0:T(8,128)(2,1)S(1)}, u32[]{:S(2)}, u32[]{:S(2)}) collective-permute-start(bf16[128,1024]{1,0:T(8,128)(2,1)} %bitcast.14), channel_id=1, source_target_pairs={{0,2},{1,3},{2,0},{3,1},{4,6},{5,7},{6,4},{7,5},{8,10},{9,11},{10,... | collective-permute-start | bytes 786440 | tf_op jit(solution)/shard_map/ppermute | solution.py:220
  7.9 0.7 %copy-start.1 = (s32[1,12]{1,0:T(1,128)S(1)}, s32[1,12]{1,0:T(1,128)}, u32[]{:S(2)}) copy-start(s32[1,12]{1,0:T(1,128)} %refs_2_.5) | copy-start | bytes 148
  8.5 13.2 %copy-start = (f32[1024]{0:T(1024)S(1)}, f32[1024]{0:T(1024)}, u32[]{:S(2)}) copy-start(f32[1024]{0:T(1024)} %param.10) | copy-start | bytes 12292
  16.5 9.1 %collective-permute-start.6 = (bf16[128,1024]{1,0:T(8,128)(2,1)S(1)}, bf16[128,1024]{1,0:T(8,128)(2,1)S(1)}, u32[]{:S(2)}, u32[]{:S(2)}) collective-permute-start(bf16[128,1024]{1,0:T(8,128)(2,1)S(1)} %collective-permute-done.4.refs_1_), channel_id=1, source_target_pairs={{0,2},{1,3},{2,0},{3,1},{4,6},{5,7},{6,4},{7,5},{8,10},{9,11},{10,... | collective-permute-start | bytes 786440 | tf_op jit(solution)/shard_map/ppermute | solution.py:220
  16.7 9.5 %collective-permute-start.9 = (bf16[128,1024]{1,0:T(8,128)(2,1)S(1)}, bf16[128,1024]{1,0:T(8,128)(2,1)S(1)}, u32[]{:S(2)}, u32[]{:S(2)}) collective-permute-start(bf16[128,1024]{1,0:T(8,128)(2,1)S(1)} %collective-permute-done.4.refs_1_), channel_id=1, source_target_pairs={{0,1},{1,0},{2,3},{3,2},{4,5},{5,4},{6,7},{7,6},{8,9},{9,8},{10,11... | collective-permute-start | bytes 786440 | tf_op jit(solution)/shard_map/ppermute | solution.py:220
  18.7 14.1 %collective-permute-start.11 = (bf16[128,1024]{1,0:T(8,128)(2,1)S(1)}, bf16[128,1024]{1,0:T(8,128)(2,1)S(1)}, u32[]{:S(2)}, u32[]{:S(2)}) collective-permute-start(bf16[128,1024]{1,0:T(8,128)(2,1)S(1)} %collective-permute-done.refs_2_), channel_id=1, source_target_pairs={{0,4},{1,5},{2,6},{3,7},{4,0},{5,1},{6,2},{7,3},{8,12},{9,13},{10,... | collective-permute-start | bytes 786440 | tf_op jit(solution)/shard_map/ppermute | solution.py:220
  19.9 13.4 %collective-permute-start.2 = (bf16[128,1024]{1,0:T(8,128)(2,1)S(1)}, bf16[128,1024]{1,0:T(8,128)(2,1)S(1)}, u32[]{:S(2)}, u32[]{:S(2)}) collective-permute-start(bf16[128,1024]{1,0:T(8,128)(2,1)S(1)} %collective-permute-done.refs_2_), channel_id=1, source_target_pairs={{0,6},{1,7},{2,4},{3,5},{4,2},{5,3},{6,0},{7,1},{8,14},{9,15},{10,... | collective-permute-start | bytes 786440 | tf_op jit(solution)/shard_map/ppermute | solution.py:220
  21.1 4.5 %collective-permute-start.8 = (bf16[128,1024]{1,0:T(8,128)(2,1)S(1)}, bf16[128,1024]{1,0:T(8,128)(2,1)S(1)}, u32[]{:S(2)}, u32[]{:S(2)}) collective-permute-start(bf16[128,1024]{1,0:T(8,128)(2,1)S(1)} %collective-permute-done.3.refs_0_), channel_id=1, source_target_pairs={{0,1},{1,0},{2,3},{3,2},{4,5},{5,4},{6,7},{7,6},{8,9},{9,8},{10,11... | collective-permute-start | bytes 786440 | tf_op jit(solution)/shard_map/ppermute | solution.py:220
  25.6 4.5 %collective-permute-start.5 = (bf16[128,1024]{1,0:T(8,128)(2,1)S(1)}, bf16[128,1024]{1,0:T(8,128)(2,1)S(1)}, u32[]{:S(2)}, u32[]{:S(2)}) collective-permute-start(bf16[128,1024]{1,0:T(8,128)(2,1)S(1)} %collective-permute-done.refs_2_), channel_id=1, source_target_pairs={{0,1},{1,0},{2,3},{3,2},{4,5},{5,4},{6,7},{7,6},{8,9},{9,8},{10,11... | collective-permute-start | bytes 786440 | tf_op jit(solution)/shard_map/ppermute | solution.py:220
  25.7 4.4 %collective-permute-start.7 = (bf16[128,1024]{1,0:T(8,128)(2,1)S(1)}, bf16[128,1024]{1,0:T(8,128)(2,1)S(1)}, u32[]{:S(2)}, u32[]{:S(2)}) collective-permute-start(bf16[128,1024]{1,0:T(8,128)(2,1)S(1)} %collective-permute-done.6.refs_2_), channel_id=1, source_target_pairs={{0,1},{1,0},{2,3},{3,2},{4,5},{5,4},{6,7},{7,6},{8,9},{9,8},{10,11... | collective-permute-start | bytes 786440 | tf_op jit(solution)/shard_map/ppermute | solution.py:220
  32.8 4.1 %collective-permute-start.12 = (bf16[128,1024]{1,0:T(8,128)(2,1)S(1)}, bf16[128,1024]{1,0:T(8,128)(2,1)S(1)}, u32[]{:S(2)}, u32[]{:S(2)}) collective-permute-start(bf16[128,1024]{1,0:T(8,128)(2,1)S(1)} %collective-permute-done.11.refs_1_), channel_id=1, source_target_pairs={{0,1},{1,0},{2,3},{3,2},{4,5},{5,4},{6,7},{7,6},{8,9},{9,8},{10,11... | collective-permute-start | bytes 786440 | tf_op jit(solution)/shard_map/ppermute | solution.py:220
  33.2 3.7 %collective-permute-start.10 = (bf16[128,1024]{1,0:T(8,128)(2,1)S(1)}, bf16[128,1024]{1,0:T(8,128)(2,1)S(1)}, u32[]{:S(2)}, u32[]{:S(2)}) collective-permute-start(bf16[128,1024]{1,0:T(8,128)(2,1)S(1)} %collective-permute-done.2.refs_0_), channel_id=1, source_target_pairs={{0,1},{1,0},{2,3},{3,2},{4,5},{5,4},{6,7},{7,6},{8,9},{9,8},{10,11... | collective-permute-start | bytes 786440 | tf_op jit(solution)/shard_map/ppermute | solution.py:220
